TPU v7x, 256 devices: a whole 4x4x8 slice. The times are simulated.
256 devices in a mesh: field: 4 (over y_hi, core), tile: 64 (over y_lo, x, z).
Axes of the slice: x: 4, y: 4 (y_hi: 2, y_lo: 2; y = y_hi * 2 + y_lo), z: 8, core: 2. Of those that a mesh axis runs over, the one named last changes fastest.
Arguments:
- density: float32 [64, 4, 8, 128], P('tile'), may hold values from 0.8 to 1.2
- velocity: float32 [3, 64, 4, 8, 128], P(None, 'tile'), may hold values from -3 to 3
- energy: float32 [64, 4, 8, 128], P('tile'), may hold values from 0.8 to 1.2
- species: float32 [16, 16, 64, 4, 8, 128], P('field', None, 'tile'), may hold values from 0 to 1
- wiener: float32 [2, 16, 3, 64, 4, 8, 128], P(None, 'field', None, 'tile'), may hold values from -6 to 6
- substeps: int32 [64, 4, 8, 128], P('tile'), may hold values from 1 to 4
- mix_rate: float32 [64, 4, 8, 128], P('tile'), may hold values from 0.5 to 5
- reactants: float32 [96, 16], replicated, may hold values from -1.5 to 1.5
- stoich: float32 [16, 96], replicated, may hold values from -0.625 to 0.625
- kinetic_constants: float32 [96], replicated, may hold values from 0.2 to 2
- excitation_sensitivity: float32 [96], replicated, may hold values from 0.5 to 4
- heat: float32 [16], replicated, may hold values from -4 to 4
- molar: float32 [16], replicated, may hold values from 0.05 to 0.2
Outputs:
- flow_out: float32 [5, 64, 4, 8, 128], P(None, 'tile')
- species_out: float32 [16, 16, 64, 4, 8, 128], P('field', None, 'tile')
All inputs are finite; a program needn't handle non-finite values.
Results may differ from a plain program's by a relative error of at most 0.0003.
Values sent between devices are 32-bit elements; how exact they have to be, the bound alone decides.
No kernel may reach another device: no remote copies, remote signals or barrier semaphores. Data moves between devices by JAX's collectives and lax.ppermute only.
A program may use at most 64 MiB of HBM per device.

v0:
```python
import math

import jax
import jax.numpy as jnp
from jax import lax
from jax.sharding import PartitionSpec as P

SPECIES = 16
REALIZATIONS = 16
SUBS = 4
STEPS = 2


time_step = 0.1
viscosity = 0.4
diffusivity = 0.3
relaxation = 2.0
noise_scale = math.sqrt(2.0 * 0.3 * 0.1)


def from_behind(value, axis, steps):
    count = lax.axis_size(axis)
    initial, last = (max(0, -steps), min(count, count - steps))
    return lax.ppermute(value, axis, [(source, source + steps) for source in range(initial, last)])


def neighbours(padded):
    centre = padded[..., 1:-1, 1:-1, 1:-1]
    grad_z = (padded[..., 2:, 1:-1, 1:-1] - padded[..., :-2, 1:-1, 1:-1]) * 0.5
    grad_y = (padded[..., 1:-1, 2:, 1:-1] - padded[..., 1:-1, :-2, 1:-1]) * 0.5
    grad_x = (padded[..., 1:-1, 1:-1, 2:] - padded[..., 1:-1, 1:-1, :-2]) * 0.5
    laplacian = padded[..., 2:, 1:-1, 1:-1] + padded[..., :-2, 1:-1, 1:-1]
    laplacian = laplacian + padded[..., 1:-1, 2:, 1:-1] + padded[..., 1:-1, :-2, 1:-1]
    laplacian = (
        laplacian + padded[..., 1:-1, 1:-1, 2:] + padded[..., 1:-1, 1:-1, :-2] - 6.0 * centre
    )
    return (centre, (grad_z, grad_y, grad_x), laplacian)


def flow_update(padded):
    centre, gradients, laplacian = neighbours(padded)
    carried = centre[1] * gradients[0] + centre[2] * gradients[1] + centre[3] * gradients[2]
    return centre + time_step * (viscosity * laplacian - carried)


def march_forward(padded, speeds, noise_draw):
    centre, gradients, laplacian = neighbours(padded)
    carried = speeds[0] * gradients[0] + speeds[1] * gradients[1] + speeds[2] * gradients[2]
    noisy = (
        gradients[0] * noise_draw[:, 0][:, None]
        + gradients[1] * noise_draw[:, 1][:, None]
        + gradients[2] * noise_draw[:, 2][:, None]
    )
    return centre + time_step * (diffusivity * laplacian - carried) + noise_scale * noisy


def react_field(flattened, kinetic_multiplier, sub_counts, step_len, reactants, stoich):
    for fractional_increment in range(SUBS):
        driving = jnp.dot(reactants, flattened, precision=lax.Precision.HIGHEST)
        changes = jnp.dot(stoich, kinetic_multiplier * driving, precision=lax.Precision.HIGHEST)
        flattened = (
            flattened + jnp.where(sub_counts > fractional_increment, step_len, 0.0) * changes
        )
    return flattened


def attach_faces(values, below_y, above_y):
    leading = [(0, 0)] * (values.ndim - 3)
    widened_grid = jnp.concatenate([below_y, values, above_y], values.ndim - 2)
    return jnp.pad(widened_grid, leading + [(1, 1), (0, 0), (1, 1)])


def exchange_faces(fluid_state, scalars):
    below_y = from_behind((fluid_state[:, :, -1:], scalars[:, :, :, -1:]), "tile", 1)
    above_y = from_behind((fluid_state[:, :, :1], scalars[:, :, :, :1]), "tile", -1)
    padded_flow = attach_faces(fluid_state, below_y[0], above_y[0])
    padded_species = attach_faces(scalars, below_y[1], above_y[1])
    return (padded_flow, padded_species)


def on_device(
    density,
    velocity,
    energy,
    species,
    wiener,
    substeps,
    mix_rate,
    reactants,
    stoich,
    kinetic_constants,
    excitation_sensitivity,
    heat,
    molar,
):
    fluid_state = jnp.concatenate([density, velocity[:, 0], energy], 0)
    scalars = species[:, :, 0]
    noise_all = wiener[:, :, :, 0]
    rates = mix_rate[0]
    sub_counts = substeps.reshape(-1)
    step_len = time_step / sub_counts.astype(jnp.float32)
    number_of_cells = sub_counts.shape[0]
    local_fields = scalars.shape[0]
    for current_step_index in range(STEPS):
        padded_flow, padded_species = exchange_faces(fluid_state, scalars)
        fluid_state = flow_update(padded_flow)
        speeds = fluid_state[1:4]
        noise_draw = noise_all[current_step_index]
        carried = march_forward(padded_species, speeds, noise_draw)
        field_sum = lax.psum(jnp.sum(carried, 0), "field")
        field_mean = field_sum / REALIZATIONS
        mixed = carried - time_step * rates * (carried - field_mean)
        pointwise_thermal_level = fluid_state[4].reshape(-1)
        kinetic_multiplier = kinetic_constants[:, None] * jnp.exp(
            excitation_sensitivity[:, None] * (pointwise_thermal_level - 1.0)
        )
        flattened = mixed.reshape(local_fields, SPECIES, number_of_cells)
        reacted = lax.map(
            lambda one: react_field(
                one, kinetic_multiplier, sub_counts, step_len, reactants, stoich
            ),
            flattened,
        )
        heat_released = jnp.sum(heat[None, :, None] * (reacted - flattened), (0, 1))
        density_sum = jnp.sum(molar[None, :, None] * reacted, (0, 1))
        scalars = reacted.reshape(scalars.shape)
        partials = jnp.stack([density_sum, heat_released], 0).reshape((2,) + fluid_state.shape[1:])
        returned = lax.psum(partials, "field") / REALIZATIONS
        fluid_state = jnp.concatenate(
            [
                (fluid_state[0] + time_step * relaxation * (returned[0] - fluid_state[0]))[None],
                fluid_state[1:4],
                (fluid_state[4] + returned[1])[None],
            ],
            0,
        )
    return (fluid_state[:, None], scalars[:, :, None])


def solution(mesh):
    placed = (
        P("tile", None, None, None),
        P(None, "tile", None, None, None),
        P("tile", None, None, None),
        P("field", None, "tile", None, None, None),
        P(None, "field", None, "tile", None, None, None),
        P("tile", None, None, None),
        P("tile", None, None, None),
        P(),
        P(),
        P(),
        P(),
        P(),
        P(),
    )
    return jax.shard_map(
        on_device,
        mesh=mesh,
        in_specs=placed,
        out_specs=(P(None, "tile", None, None, None), P("field", None, "tile", None, None, None)),
        check_vma=False,
    )
```

profile of v0, /device:TPU:9, one launch (start us, length us, event | category | flops | bytes accessed | tf_op | source)
XLA Modules:
  0.0 301.9 jit_solution(2130360371512400181)
XLA Ops:
  8.1 3.7 %collective-permute-start = (f32[5,4,1,128]{3,2,1,0:T(1,128)S(1)}, f32[5,4,1,128]{3,2,1,0:T(1,128)S(1)}, u32[]{:S(2)}, u32[]{:S(2)}) collective-permute-start(f32[5,4,1,128]{3,2,1,0:T(1,128)S(1)} %get-tuple-element.218), channel_id=1, source_target_pairs={{0,1},{1,2},{2,3},{3,4},{4,5},{5,6},{6,7},{7,8},{8,9},{9,10},{10,1... | collective-permute-start | bytes 30728 | tf_op jit(solution)/shard_map/ppermute | solution.py:24
  11.8 7.9 %collective-permute-start.1 = (f32[5,4,1,128]{3,2,1,0:T(1,128)S(1)}, f32[5,4,1,128]{3,2,1,0:T(1,128)S(1)}, u32[]{:S(2)}, u32[]{:S(2)}) collective-permute-start(f32[5,4,1,128]{3,2,1,0:T(1,128)S(1)} %get-tuple-element.219), channel_id=1, source_target_pairs={{1,0},{2,1},{3,2},{4,3},{5,4},{6,5},{7,6},{8,7},{9,8},{10,9},{11,1... | collective-permute-start | bytes 30728 | tf_op jit(solution)/shard_map/ppermute | solution.py:24
  23.5 7.6 %collective-permute-start.3 = (f32[4,16,4,1,128]{4,3,2,1,0:T(1,128)S(1)}, f32[4,16,4,1,128]{4,3,2,1,0:T(1,128)S(1)}, u32[]{:S(2)}, u32[]{:S(2)}) collective-permute-start(f32[4,16,4,1,128]{4,3,2,1,0:T(1,128)S(1)} %get-tuple-element.197), channel_id=1, source_target_pairs={{1,0},{2,1},{3,2},{4,3},{5,4},{6,5},{7,6},{8,7},{9,8},{10,9},{11,1... | collective-permute-start | bytes 393224 | tf_op jit(solution)/shard_map/ppermute | solution.py:24
  34.8 2.8 select_maximum_fusion.2
  37.7 2.6 fusion.61
  40.6 44.6 %all-reduce.7.cloned.1.call-done = f32[16,4,8,128]{3,2,1,0:T(8,128)} async-done(((f32[16,4,8,128]{3,2,1,0:T(8,128)}), f32[16,4,8,128]{3,2,1,0:T(8,128)}) %all-reduce.7.cloned.1.call-update) | async-done | bytes 262160 | tf_op jit(solution)/shard_map/psum | solution.py:110
  87.2 51.6 %while.22 = (s32[]{:T(128)}, f32[4,16,4096]{2,1,0:T(8,128)S(1)}, f32[4,16,4096]{2,1,0:T(8,128)S(1)}, s32[4096]{0:T(1024)S(1)}, f32[4096]{0:T(1024)S(1)}, /*index...) while((s32[]{:T(128)}, f32[4,16,4096]{2,1,0:T(8,128)S(1)}, ...), condition=%wide.region_3.4_spmd.clone, body=%wide.region_2.3_spmd.clone.sunk | while | flops 609255424 | bytes 16014457 | solution.py:118
  90.4 2.3 fusion.162
  93.6 2.3 fusion.164
  100.1 2.3 fusion.160
  103.3 2.3 fusion.162
  113.0 2.3 fusion.160
  116.2 2.3 fusion.162
  125.9 2.3 fusion.160
  129.1 2.3 fusion.162
  139.8 13.2 %psum.29 = f32[2,4,8,128]{3,2,1,0:T(8,128)S(1)} all-reduce(f32[2,4,8,128]{3,2,1,0:T(8,128)S(1)} %pad_maximum_fusion.18), channel_id=1, replica_groups=mesh['field'=4,'tile'=64] {'field'}, use_global_device_ids=true, to_apply=%region_6.7 | all-reduce | flops 8192 | bytes 65536 | tf_op jit(solution)/shard_map/psum | solution.py:128
  153.1 3.2 %collective-permute-start.4 = (f32[5,4,1,128]{3,2,1,0:T(1,128)S(1)}, f32[5,4,1,128]{3,2,1,0:T(1,128)S(1)}, u32[]{:S(2)}, u32[]{:S(2)}) collective-permute-start(f32[5,4,1,128]{3,2,1,0:T(1,128)S(1)} %get-tuple-element.212), channel_id=1, source_target_pairs={{0,1},{1,2},{2,3},{3,4},{4,5},{5,6},{6,7},{7,8},{8,9},{9,10},{10,1... | collective-permute-start | bytes 30728 | tf_op jit(solution)/shard_map/ppermute | solution.py:24
  156.3 6.9 %collective-permute-start.5 = (f32[5,4,1,128]{3,2,1,0:T(1,128)S(1)}, f32[5,4,1,128]{3,2,1,0:T(1,128)S(1)}, u32[]{:S(2)}, u32[]{:S(2)}) collective-permute-start(f32[5,4,1,128]{3,2,1,0:T(1,128)S(1)} %get-tuple-element.213), channel_id=1, source_target_pairs={{1,0},{2,1},{3,2},{4,3},{5,4},{6,5},{7,6},{8,7},{9,8},{10,9},{11,1... | collective-permute-start | bytes 30728 | tf_op jit(solution)/shard_map/ppermute | solution.py:24
  165.3 7.8 %collective-permute-start.7 = (f32[4,16,4,1,128]{4,3,2,1,0:T(1,128)S(1)}, f32[4,16,4,1,128]{4,3,2,1,0:T(1,128)S(1)}, u32[]{:S(2)}, u32[]{:S(2)}) collective-permute-start(f32[4,16,4,1,128]{4,3,2,1,0:T(1,128)S(1)} %get-tuple-element.195), channel_id=1, source_target_pairs={{1,0},{2,1},{3,2},{4,3},{5,4},{6,5},{7,6},{8,7},{9,8},{10,9},{11,1... | collective-permute-start | bytes 393224 | tf_op jit(solution)/shard_map/ppermute | solution.py:24
  174.8 2.8 select_maximum_fusion
  177.6 2.7 fusion.60
  180.3 46.9 %all-reduce.9.cloned.1.call-done = f32[16,4,8,128]{3,2,1,0:T(8,128)} async-done(((f32[16,4,8,128]{3,2,1,0:T(8,128)}), f32[16,4,8,128]{3,2,1,0:T(8,128)}) %all-reduce.9.cloned.1.call-update) | async-done | bytes 262160 | tf_op jit(solution)/shard_map/psum | solution.py:110
  229.0 50.7 %while.23 = (s32[]{:T(128)}, f32[4,16,4096]{2,1,0:T(8,128)S(1)}, f32[4,16,4096]{2,1,0:T(8,128)S(1)}, s32[4096]{0:T(1024)S(1)}, f32[4096]{0:T(1024)S(1)}, /*index...) while((s32[]{:T(128)}, f32[4,16,4096]{2,1,0:T(8,128)S(1)}, ...), condition=%wide.region_10.11_spmd.clone, body=%wide.region_9.10_spmd.clone.sunk | while | flops 609255424 | bytes 16014457 | solution.py:118
  281.2 13.2 %psum.31 = f32[2,4,8,128]{3,2,1,0:T(8,128)S(1)} all-reduce(f32[2,4,8,128]{3,2,1,0:T(8,128)S(1)} %pad_maximum_fusion.19), channel_id=1, replica_groups=mesh['field'=4,'tile'=64] {'field'}, use_global_device_ids=true, to_apply=%region_13.14 | all-reduce | flops 8192 | bytes 65536 | tf_op jit(solution)/shard_map/psum | solution.py:128
  (148 shorter events, 102.6 us)
Async XLA Ops:
  7.2 26.6 %copy-start.3 = (f32[3,1,4,8,128]{4,3,2,1,0:T(8,128)S(1)}, f32[3,1,4,8,128]{4,3,2,1,0:T(8,128)}, u32[]{:S(2)}) copy-start(f32[3,1,4,8,128]{4,3,2,1,0:T(8,128)} %param.18) | copy-start | bytes 147460
  7.2 26.6 %copy-start.9 = (f32[1,4,8,128]{3,2,1,0:T(8,128)S(1)}, f32[1,4,8,128]{3,2,1,0:T(8,128)}, u32[]{:S(2)}) copy-start(f32[1,4,8,128]{3,2,1,0:T(8,128)} %param.17) | copy-start | bytes 49156
  7.2 26.6 %copy-start.8 = (f32[1,4,8,128]{3,2,1,0:T(8,128)S(1)}, f32[1,4,8,128]{3,2,1,0:T(8,128)}, u32[]{:S(2)}) copy-start(f32[1,4,8,128]{3,2,1,0:T(8,128)} %param.19) | copy-start | bytes 49156
  7.2 26.5 %copy-start.10 = (f32[1,4,8,128]{3,2,1,0:T(8,128)S(1)}, f32[1,4,8,128]{3,2,1,0:T(8,128)}, u32[]{:S(2)}) copy-start(f32[1,4,8,128]{3,2,1,0:T(8,128)} %param.23) | copy-start | bytes 49156
  7.2 78.1 %all-reduce.7.cloned.1.call-start = ((), (), s32[]{:S(2)}) async-start(), calls=%async_computation | async-start | bytes 524288 | tf_op jit(solution)/shard_map/psum | solution.py:110
  8.1 26.7 %copy-start.1 = (f32[4,16,1,4,8,128]{5,4,3,2,1,0:T(8,128)S(1)}, f32[4,16,1,4,8,128]{5,4,3,2,1,0:T(8,128)}, u32[]{:S(2)}) copy-start(f32[4,16,1,4,8,128]{5,4,3,2,1,0:T(8,128)} %param.20) | copy-start | bytes 3145732
  8.1 25.6 %collective-permute-start = (f32[5,4,1,128]{3,2,1,0:T(1,128)S(1)}, f32[5,4,1,128]{3,2,1,0:T(1,128)S(1)}, u32[]{:S(2)}, u32[]{:S(2)}) collective-permute-start(f32[5,4,1,128]{3,2,1,0:T(1,128)S(1)} %get-tuple-element.218), channel_id=1, source_target_pairs={{0,1},{1,2},{2,3},{3,4},{4,5},{5,6},{6,7},{7,8},{8,9},{9,10},{10,1... | collective-permute-start | bytes 30728 | tf_op jit(solution)/shard_map/ppermute | solution.py:24
  11.8 22.0 %collective-permute-start.1 = (f32[5,4,1,128]{3,2,1,0:T(1,128)S(1)}, f32[5,4,1,128]{3,2,1,0:T(1,128)S(1)}, u32[]{:S(2)}, u32[]{:S(2)}) collective-permute-start(f32[5,4,1,128]{3,2,1,0:T(1,128)S(1)} %get-tuple-element.219), channel_id=1, source_target_pairs={{1,0},{2,1},{3,2},{4,3},{5,4},{6,5},{7,6},{8,7},{9,8},{10,9},{11,1... | collective-permute-start | bytes 30728 | tf_op jit(solution)/shard_map/ppermute | solution.py:24
  21.5 13.3 %collective-permute-start.2 = (f32[4,16,4,1,128]{4,3,2,1,0:T(1,128)S(1)}, f32[4,16,4,1,128]{4,3,2,1,0:T(1,128)S(1)}, u32[]{:S(2)}, u32[]{:S(2)}) collective-permute-start(f32[4,16,4,1,128]{4,3,2,1,0:T(1,128)S(1)} %get-tuple-element.196), channel_id=1, source_target_pairs={{0,1},{1,2},{2,3},{3,4},{4,5},{5,6},{6,7},{7,8},{8,9},{9,10},{10,1... | collective-permute-start | bytes 393224 | tf_op jit(solution)/shard_map/ppermute | solution.py:24
  23.5 11.4 %collective-permute-start.3 = (f32[4,16,4,1,128]{4,3,2,1,0:T(1,128)S(1)}, f32[4,16,4,1,128]{4,3,2,1,0:T(1,128)S(1)}, u32[]{:S(2)}, u32[]{:S(2)}) collective-permute-start(f32[4,16,4,1,128]{4,3,2,1,0:T(1,128)S(1)} %get-tuple-element.197), channel_id=1, source_target_pairs={{1,0},{2,1},{3,2},{4,3},{5,4},{6,5},{7,6},{8,7},{9,8},{10,9},{11,1... | collective-permute-start | bytes 393224 | tf_op jit(solution)/shard_map/ppermute | solution.py:24
  34.8 2.9 copy-start.4
  34.8 2.9 copy-start.6
  37.7 2.9 copy-start.2
  40.3 186.8 %all-reduce.9.cloned.1.call-start = ((), (), s32[]{:S(2)}) async-start(), calls=%async_computation.1 | async-start | bytes 524288 | tf_op jit(solution)/shard_map/psum | solution.py:110
  86.5 0.7 copy-start
  86.5 0.7 copy-start.13
  138.8 0.7 copy-start.12
  139.8 33.6 %copy-start.5 = (f32[4,8,128]{2,1,0:T(8,128)S(1)}, f32[4,8,128]{2,1,0:T(8,128)}, u32[]{:S(2)}) copy-start(f32[4,8,128]{2,1,0:T(8,128)} %copy-done.4) | copy-start | bytes 49156
  139.8 33.6 %copy-start.7 = (f32[4,8,128]{2,1,0:T(8,128)S(1)}, f32[4,8,128]{2,1,0:T(8,128)}, u32[]{:S(2)}) copy-start(f32[4,8,128]{2,1,0:T(8,128)} %copy-done.6) | copy-start | bytes 49156
  153.1 20.0 %collective-permute-start.4 = (f32[5,4,1,128]{3,2,1,0:T(1,128)S(1)}, f32[5,4,1,128]{3,2,1,0:T(1,128)S(1)}, u32[]{:S(2)}, u32[]{:S(2)}) collective-permute-start(f32[5,4,1,128]{3,2,1,0:T(1,128)S(1)} %get-tuple-element.212), channel_id=1, source_target_pairs={{0,1},{1,2},{2,3},{3,4},{4,5},{5,6},{6,7},{7,8},{8,9},{9,10},{10,1... | collective-permute-start | bytes 30728 | tf_op jit(solution)/shard_map/ppermute | solution.py:24
  156.3 16.8 %collective-permute-start.5 = (f32[5,4,1,128]{3,2,1,0:T(1,128)S(1)}, f32[5,4,1,128]{3,2,1,0:T(1,128)S(1)}, u32[]{:S(2)}, u32[]{:S(2)}) collective-permute-start(f32[5,4,1,128]{3,2,1,0:T(1,128)S(1)} %get-tuple-element.213), channel_id=1, source_target_pairs={{1,0},{2,1},{3,2},{4,3},{5,4},{6,5},{7,6},{8,7},{9,8},{10,9},{11,1... | collective-permute-start | bytes 30728 | tf_op jit(solution)/shard_map/ppermute | solution.py:24
  163.4 10.2 %collective-permute-start.6 = (f32[4,16,4,1,128]{4,3,2,1,0:T(1,128)S(1)}, f32[4,16,4,1,128]{4,3,2,1,0:T(1,128)S(1)}, u32[]{:S(2)}, u32[]{:S(2)}) collective-permute-start(f32[4,16,4,1,128]{4,3,2,1,0:T(1,128)S(1)} %get-tuple-element.194), channel_id=1, source_target_pairs={{0,1},{1,2},{2,3},{3,4},{4,5},{5,6},{6,7},{7,8},{8,9},{9,10},{10,1... | collective-permute-start | bytes 393224 | tf_op jit(solution)/shard_map/ppermute | solution.py:24
  165.3 9.5 %collective-permute-start.7 = (f32[4,16,4,1,128]{4,3,2,1,0:T(1,128)S(1)}, f32[4,16,4,1,128]{4,3,2,1,0:T(1,128)S(1)}, u32[]{:S(2)}, u32[]{:S(2)}) collective-permute-start(f32[4,16,4,1,128]{4,3,2,1,0:T(1,128)S(1)} %get-tuple-element.195), channel_id=1, source_target_pairs={{1,0},{2,1},{3,2},{4,3},{5,4},{6,5},{7,6},{8,7},{9,8},{10,9},{11,1... | collective-permute-start | bytes 393224 | tf_op jit(solution)/shard_map/ppermute | solution.py:24
  228.3 0.7 copy-start.14
  (1 other events, 0.7 us)
Sparse Core Ops, SparseCore 0:
  40.5 44.7 all-reduce.6
  180.4 46.7 all-reduce.8
where the time goes:
time: 305 us; the launch traced here: 302 us
  matrix products  102 us (33%)
  waiting for transfers between devices  92.8 us (30%)
  starting transfers between devices  41.2 us (14%)
  blocking collectives  26.4 us (9%)
  other arithmetic  17.6 us (6%)
  between operations  14.6 us (5%)
  local copies, waits for them, and re-layouts  7.09 us (2%)
    psum x2, waiting for transfers between devices, on_device(): field_sum = lax.psum(jnp.sum(carried, 0), 'field')  91.5 us
    dot_general x32, matrix products, react_field(): driving = jnp.dot(reactants, flattened, precision=lax.Precision.HIGHEST)  71.9 us
    ppermute x8, starting transfers between devices, from_behind(): lax.ppermute(value, axis, [(source, source + steps) for source in range(i...  40.9 us
    dot_general x32, matrix products, react_field(): jnp.dot(stoich, kinetic_multiplier * driving, precision=lax.Precision.HIG...  29.8 us
    psum x2, blocking collectives, on_device(): returned = lax.psum(partials, 'field') / REALIZATIONS  26.4 us
    concatenate x4, other arithmetic, attach_faces(): widened_grid = jnp.concatenate([below_y, values, above_y], values.ndim - 2)  6.16 us
  transfers between devices with their start and end apart: 10, of which 3 were waited for; matrix products, arithmetic and copies ran while one was open for 2% of the time, Pallas kernels for 0%

commit v1 on v0

--- a/solution.py
+++ b/solution.py
@@ -22,6 +22,19 @@
     count = lax.axis_size(axis)
     initial, last = (max(0, -steps), min(count, count - steps))
     return lax.ppermute(value, axis, [(source, source + steps) for source in range(initial, last)])
+
+
+def field_total(value):
+    half = value.shape[0] // 2
+    core = lax.axis_index("field") % 2
+    core_pairs = [(i, i ^ 1) for i in range(4)]
+    chip_pairs = [(i, i ^ 2) for i in range(4)]
+    mine = jnp.where(core == 0, value[:half], value[half:])
+    other = jnp.where(core == 0, value[half:], value[:half])
+    mine = mine + lax.ppermute(other, "field", core_pairs)
+    mine = mine + lax.ppermute(mine, "field", chip_pairs)
+    other = lax.ppermute(mine, "field", core_pairs)
+    return jnp.concatenate([jnp.where(core == 0, mine, other), jnp.where(core == 0, other, mine)])
 
 
 def neighbours(padded):
@@ -107,7 +120,7 @@
         speeds = fluid_state[1:4]
         noise_draw = noise_all[current_step_index]
         carried = march_forward(padded_species, speeds, noise_draw)
-        field_sum = lax.psum(jnp.sum(carried, 0), "field")
+        field_sum = field_total(jnp.sum(carried, 0))
         field_mean = field_sum / REALIZATIONS
         mixed = carried - time_step * rates * (carried - field_mean)
         pointwise_thermal_level = fluid_state[4].reshape(-1)
@@ -125,7 +138,7 @@
         density_sum = jnp.sum(molar[None, :, None] * reacted, (0, 1))
         scalars = reacted.reshape(scalars.shape)
         partials = jnp.stack([density_sum, heat_released], 0).reshape((2,) + fluid_state.shape[1:])
-        returned = lax.psum(partials, "field") / REALIZATIONS
+        returned = field_total(partials) / REALIZATIONS
         fluid_state = jnp.concatenate(
             [
                 (fluid_state[0] + time_step * relaxation * (returned[0] - fluid_state[0]))[None],

time: 305 us -> 181 us (0.59)
  waiting for transfers between devices: 92.8 us -> 18.9 us
  blocking collectives: 26.4 us -> 0 us
  matrix products: 102 us -> 79.2 us
  starting transfers between devices: 41.2 us -> 60.7 us
  between operations: 14.6 us -> 1.19 us
  other arithmetic: 17.6 us -> 14.1 us
    psum x2 -> x0, waiting for transfers between devices: 91.5 us -> none  [on_device(): field_sum = lax.psum(jnp.sum(carried, 0), 'field')]
    psum x2 -> x0, blocking collectives: 26.4 us -> none  [on_device(): returned = lax.psum(partials, 'field') / REALIZATIONS]
    dot_general x32, matrix products: 71.9 us -> 49.4 us  [react_field(): driving = jnp.dot(reactants, flattened, precision=lax.Precision.HIGHEST)]
    ppermute x0 -> x12, starting transfers between devices: none -> 19.7 us  [the longest x4 9.39 us: field_total(): mine = mine + lax.ppermute(mine, 'field', chip_pairs)]
    ppermute x0 -> x12, waiting for transfers between devices: none -> 17.6 us  [the longest x4 11.4 us: field_total(): mine = mine + lax.ppermute(mine, 'field', chip_pairs)]
  transfers between devices with their start and end apart: 10 -> 20, of which waited for: 3 -> 13; matrix products, arithmetic and copies ran while one was open for 2% -> 3% of each run, Pallas kernels for 0% -> 0%
where the time goes in v1:
time: 181 us; the launch traced here: 180 us
  matrix products  79.2 us (44%)
  starting transfers between devices  60.7 us (34%)
  waiting for transfers between devices  18.9 us (10%)
  other arithmetic  14.1 us (8%)
  local copies, waits for them, and re-layouts  5.42 us (3%)
    dot_general x32, matrix products, react_field(): driving = jnp.dot(reactants, flattened, precision=lax.Precision.HIGHEST)  49.4 us
    ppermute x8, starting transfers between devices, from_behind(): lax.ppermute(value, axis, [(source, source + steps) for source in range(i...  40.9 us
    dot_general x32, matrix products, react_field(): jnp.dot(stoich, kinetic_multiplier * driving, precision=lax.Precision.HIG...  29.8 us
    ppermute x4, waiting for transfers between devices, field_total(): mine = mine + lax.ppermute(mine, 'field', chip_pairs)  11.4 us
    ppermute x4, starting transfers between devices, field_total(): mine = mine + lax.ppermute(mine, 'field', chip_pairs)  9.39 us
    concatenate x4, other arithmetic, attach_faces(): widened_grid = jnp.concatenate([below_y, values, above_y], values.ndim - 2)  6.17 us
    ppermute x4, starting transfers between devices, field_total(): other = lax.ppermute(mine, 'field', core_pairs)  5.72 us
    ppermute x4, starting transfers between devices, field_total(): mine = mine + lax.ppermute(other, 'field', core_pairs)  4.62 us
  transfers between devices with their start and end apart: 20, of which 13 were waited for; matrix products, arithmetic and copies ran while one was open for 3% of the time, Pallas kernels for 0%

profile of v1, /device:TPU:9, one launch (start us, length us, event | category | flops | bytes accessed | tf_op | source)
XLA Modules:
  0.0 180.0 jit_solution(4229770950956497184)
XLA Ops:
  1.6 3.5 %collective-permute-start = (f32[5,4,1,128]{3,2,1,0:T(1,128)S(1)}, f32[5,4,1,128]{3,2,1,0:T(1,128)S(1)}, u32[]{:S(2)}, u32[]{:S(2)}) collective-permute-start(f32[5,4,1,128]{3,2,1,0:T(1,128)S(1)} %get-tuple-element.222), channel_id=1, source_target_pairs={{0,1},{1,2},{2,3},{3,4},{4,5},{5,6},{6,7},{7,8},{8,9},{9,10},{10,1... | collective-permute-start | bytes 30728 | tf_op jit(solution)/shard_map/ppermute | solution.py:24
  5.2 7.9 %collective-permute-start.1 = (f32[5,4,1,128]{3,2,1,0:T(1,128)S(1)}, f32[5,4,1,128]{3,2,1,0:T(1,128)S(1)}, u32[]{:S(2)}, u32[]{:S(2)}) collective-permute-start(f32[5,4,1,128]{3,2,1,0:T(1,128)S(1)} %get-tuple-element.223), channel_id=1, source_target_pairs={{1,0},{2,1},{3,2},{4,3},{5,4},{6,5},{7,6},{8,7},{9,8},{10,9},{11,1... | collective-permute-start | bytes 30728 | tf_op jit(solution)/shard_map/ppermute | solution.py:24
  13.1 1.9 %fusion.63 = (f32[4,16,4,1,128]{4,3,2,1,0:T(1,128)S(1)}, f32[4,16,4,1,128]{4,3,2,1,0:T(1,128)S(1)}) fusion(f32[4,16,4,8,128]{4,3,2,1,0:T(8,128)} %bitcast.298), kind=kLoop, calls=%fused_computation.181 | loop fusion | bytes 524288 | tf_op jit(solution)/shard_map/slice | solution.py:87
  15.0 1.9 %collective-permute-start.2 = (f32[4,16,4,1,128]{4,3,2,1,0:T(1,128)S(1)}, f32[4,16,4,1,128]{4,3,2,1,0:T(1,128)S(1)}, u32[]{:S(2)}, u32[]{:S(2)}) collective-permute-start(f32[4,16,4,1,128]{4,3,2,1,0:T(1,128)S(1)} %get-tuple-element.196), channel_id=1, source_target_pairs={{0,1},{1,2},{2,3},{3,4},{4,5},{5,6},{6,7},{7,8},{8,9},{9,10},{10,1... | collective-permute-start | bytes 393224 | tf_op jit(solution)/shard_map/ppermute | solution.py:24
  17.0 7.6 %collective-permute-start.3 = (f32[4,16,4,1,128]{4,3,2,1,0:T(1,128)S(1)}, f32[4,16,4,1,128]{4,3,2,1,0:T(1,128)S(1)}, u32[]{:S(2)}, u32[]{:S(2)}) collective-permute-start(f32[4,16,4,1,128]{4,3,2,1,0:T(1,128)S(1)} %get-tuple-element.197), channel_id=1, source_target_pairs={{1,0},{2,1},{3,2},{4,3},{5,4},{6,5},{7,6},{8,7},{9,8},{10,9},{11,1... | collective-permute-start | bytes 393224 | tf_op jit(solution)/shard_map/ppermute | solution.py:24
  26.8 2.9 %select_maximum_fusion.2 = f32[4,16,6,10,130]{4,3,2,1,0:T(8,128)S(1)} fusion(f32[4,16,4,1,128]{4,3,2,1,0:T(1,128)S(1)} %collective-permute-done.3, f32[4,16,4,8,128]{4,3,2,1,0:T(8,128)S(1)} %bitcast.299, f32[4,16,4,1,128]{4,3,2,1,0:T(1,128)S(1)} %collective-permute-done.2), kind=kLoop, calls=%fused_computation.68 | loop fusion | flops 7488000 | bytes 3307520 | tf_op jit(solution)/shard_map/concatenate | solution.py:82
  29.7 2.0 %fusion.61 = (f32[16,4,8,128]{3,2,1,0:T(8,128)S(1)}, f32[4,16,4,8,128]{4,3,2,1,0:T(8,128)S(1)}) fusion(f32[4,4,8,128]{3,2,1,0:T(8,128)S(1)} %get-tuple-element.203, f32[4,4,8,128]{3,2,1,0:T(8,128)S(1)} %get-tuple-element.204, f32[4,4,8,128]{3,2,1,0:T(8,128)S(1)} %get-tuple-element.202, f32[4,16,4,8,128]{4,3,2,1,0:T(8,128)S(1)} %bitcast.300, ...), kind=kLoop, calls=%fused_computation.179 | loop fusion | flops 7536640 | bytes 7061504 | tf_op jit(solution)/shard_map/reduce_sum | solution.py:123
  31.7 1.9 %collective-permute-start.4 = (f32[8,4,8,128]{3,2,1,0:T(8,128)S(1)}, f32[8,4,8,128]{3,2,1,0:T(8,128)S(1)}, u32[]{:S(2)}, u32[]{:S(2)}) collective-permute-start(f32[8,4,8,128]{3,2,1,0:T(8,128)S(1)} %slice_select_fusion.1), channel_id=1, source_target_pairs={{0,64},{64,0},{128,192},{192,128},{1,65},{65,1},{129,193},{193,129... | collective-permute-start | bytes 393224 | tf_op jit(solution)/shard_map/ppermute | solution.py:34
  34.5 2.4 %collective-permute-start.5 = (f32[8,4,8,128]{3,2,1,0:T(8,128)S(1)}, f32[8,4,8,128]{3,2,1,0:T(8,128)S(1)}, u32[]{:S(2)}, u32[]{:S(2)}) collective-permute-start(f32[8,4,8,128]{3,2,1,0:T(8,128)S(1)} %select_add_fusion.1), channel_id=1, source_target_pairs={{0,128},{64,192},{128,0},{192,64},{1,129},{65,193},{129,1},{193,65... | collective-permute-start | bytes 393224 | tf_op jit(solution)/shard_map/ppermute | solution.py:35
  36.9 3.9 %collective-permute-done.5 = f32[8,4,8,128]{3,2,1,0:T(8,128)S(1)} collective-permute-done((f32[8,4,8,128]{3,2,1,0:T(8,128)S(1)}, f32[8,4,8,128]{3,2,1,0:T(8,128)S(1)}, u32[]{:S(2)}, u32[]{:S(2)}) %collective-permute-start.5) | collective-permute-done | bytes 131104 | tf_op jit(solution)/shard_map/ppermute | solution.py:35
  44.3 39.9 %while.22 = (s32[]{:T(128)}, f32[4,16,4096]{2,1,0:T(8,128)S(1)}, f32[4,16,4096]{2,1,0:T(8,128)S(1)}, s32[4096]{0:T(1024)S(1)}, f32[4096]{0:T(1024)S(1)}, /*index...) while((s32[]{:T(128)}, f32[4,16,4096]{2,1,0:T(8,128)S(1)}, ...), condition=%wide.region_2.3_spmd.clone, body=%wide.region_1.2_spmd.clone.sunk | while | flops 609255424 | bytes 16014713 | solution.py:131
  85.9 2.3 %collective-permute-start.8 = (f32[1,4,8,128]{3,2,1,0:T(8,128)S(1)}, f32[1,4,8,128]{3,2,1,0:T(8,128)S(1)}, u32[]{:S(2)}, u32[]{:S(2)}) collective-permute-start(f32[1,4,8,128]{3,2,1,0:T(8,128)S(1)} %bitcast_add_fusion.1), channel_id=1, source_target_pairs={{0,128},{64,192},{128,0},{192,64},{1,129},{65,193},{129,1},{193,65... | collective-permute-start | bytes 49160 | tf_op jit(solution)/shard_map/ppermute | solution.py:35
  92.4 1.9 %collective-permute-start.10 = (f32[5,4,1,128]{3,2,1,0:T(1,128)S(1)}, f32[5,4,1,128]{3,2,1,0:T(1,128)S(1)}, u32[]{:S(2)}, u32[]{:S(2)}) collective-permute-start(f32[5,4,1,128]{3,2,1,0:T(1,128)S(1)} %get-tuple-element.216), channel_id=1, source_target_pairs={{0,1},{1,2},{2,3},{3,4},{4,5},{5,6},{6,7},{7,8},{8,9},{9,10},{10,1... | collective-permute-start | bytes 30728 | tf_op jit(solution)/shard_map/ppermute | solution.py:24
  94.3 8.3 %collective-permute-start.11 = (f32[5,4,1,128]{3,2,1,0:T(1,128)S(1)}, f32[5,4,1,128]{3,2,1,0:T(1,128)S(1)}, u32[]{:S(2)}, u32[]{:S(2)}) collective-permute-start(f32[5,4,1,128]{3,2,1,0:T(1,128)S(1)} %get-tuple-element.217), channel_id=1, source_target_pairs={{1,0},{2,1},{3,2},{4,3},{5,4},{6,5},{7,6},{8,7},{9,8},{10,9},{11,1... | collective-permute-start | bytes 30728 | tf_op jit(solution)/shard_map/ppermute | solution.py:24
  102.8 1.9 %collective-permute-start.12 = (f32[4,16,4,1,128]{4,3,2,1,0:T(1,128)S(1)}, f32[4,16,4,1,128]{4,3,2,1,0:T(1,128)S(1)}, u32[]{:S(2)}, u32[]{:S(2)}) collective-permute-start(f32[4,16,4,1,128]{4,3,2,1,0:T(1,128)S(1)} %get-tuple-element.194), channel_id=1, source_target_pairs={{0,1},{1,2},{2,3},{3,4},{4,5},{5,6},{6,7},{7,8},{8,9},{9,10},{10,1... | collective-permute-start | bytes 393224 | tf_op jit(solution)/shard_map/ppermute | solution.py:24
  104.7 7.8 %collective-permute-start.13 = (f32[4,16,4,1,128]{4,3,2,1,0:T(1,128)S(1)}, f32[4,16,4,1,128]{4,3,2,1,0:T(1,128)S(1)}, u32[]{:S(2)}, u32[]{:S(2)}) collective-permute-start(f32[4,16,4,1,128]{4,3,2,1,0:T(1,128)S(1)} %get-tuple-element.195), channel_id=1, source_target_pairs={{1,0},{2,1},{3,2},{4,3},{5,4},{6,5},{7,6},{8,7},{9,8},{10,9},{11,1... | collective-permute-start | bytes 393224 | tf_op jit(solution)/shard_map/ppermute | solution.py:24
  114.2 2.8 %select_maximum_fusion = f32[4,16,6,10,130]{4,3,2,1,0:T(8,128)S(1)} fusion(f32[4,16,4,1,128]{4,3,2,1,0:T(1,128)S(1)} %collective-permute-done.13, f32[4,16,4,8,128]{4,3,2,1,0:T(8,128)S(1)} %bitcast.294, f32[4,16,4,1,128]{4,3,2,1,0:T(1,128)S(1)} %collective-permute-done.12), kind=kLoop, calls=%fused_computation.66 | loop fusion | flops 7488000 | bytes 3307520 | tf_op jit(solution)/shard_map/concatenate | solution.py:82
  117.1 2.0 %fusion.60 = (f32[16,4,8,128]{3,2,1,0:T(8,128)S(1)}, f32[4,16,4,8,128]{4,3,2,1,0:T(8,128)S(1)}) fusion(f32[4,4,8,128]{3,2,1,0:T(8,128)S(1)} %get-tuple-element.206, f32[4,4,8,128]{3,2,1,0:T(8,128)S(1)} %get-tuple-element.207, f32[4,4,8,128]{3,2,1,0:T(8,128)S(1)} %get-tuple-element.205, f32[4,16,4,8,128]{4,3,2,1,0:T(8,128)S(1)} %bitcast.295, ...), kind=kLoop, calls=%fused_computation.178 | loop fusion | flops 7536640 | bytes 7061504 | tf_op jit(solution)/shard_map/reduce_sum | solution.py:123
  119.1 1.8 %collective-permute-start.14 = (f32[8,4,8,128]{3,2,1,0:T(8,128)S(1)}, f32[8,4,8,128]{3,2,1,0:T(8,128)S(1)}, u32[]{:S(2)}, u32[]{:S(2)}) collective-permute-start(f32[8,4,8,128]{3,2,1,0:T(8,128)S(1)} %slice_select_fusion), channel_id=1, source_target_pairs={{0,64},{64,0},{128,192},{192,128},{1,65},{65,1},{129,193},{193,129... | collective-permute-start | bytes 393224 | tf_op jit(solution)/shard_map/ppermute | solution.py:34
  121.9 2.4 %collective-permute-start.15 = (f32[8,4,8,128]{3,2,1,0:T(8,128)S(1)}, f32[8,4,8,128]{3,2,1,0:T(8,128)S(1)}, u32[]{:S(2)}, u32[]{:S(2)}) collective-permute-start(f32[8,4,8,128]{3,2,1,0:T(8,128)S(1)} %select_add_fusion), channel_id=1, source_target_pairs={{0,128},{64,192},{128,0},{192,64},{1,129},{65,193},{129,1},{193,65... | collective-permute-start | bytes 393224 | tf_op jit(solution)/shard_map/ppermute | solution.py:35
  124.3 3.9 %collective-permute-done.15 = f32[8,4,8,128]{3,2,1,0:T(8,128)S(1)} collective-permute-done((f32[8,4,8,128]{3,2,1,0:T(8,128)S(1)}, f32[8,4,8,128]{3,2,1,0:T(8,128)S(1)}, u32[]{:S(2)}, u32[]{:S(2)}) %collective-permute-start.15) | collective-permute-done | bytes 131104 | tf_op jit(solution)/shard_map/ppermute | solution.py:35
  131.0 39.9 %while.23 = (s32[]{:T(128)}, f32[4,16,4096]{2,1,0:T(8,128)S(1)}, f32[4,16,4096]{2,1,0:T(8,128)S(1)}, s32[4096]{0:T(1024)S(1)}, f32[4096]{0:T(1024)S(1)}, /*index...) while((s32[]{:T(128)}, f32[4,16,4096]{2,1,0:T(8,128)S(1)}, ...), condition=%wide.region_7.8_spmd.clone, body=%wide.region_6.7_spmd.clone.sunk | while | flops 609255424 | bytes 16014713 | solution.py:131
  172.5 2.3 %collective-permute-start.18 = (f32[1,4,8,128]{3,2,1,0:T(8,128)S(1)}, f32[1,4,8,128]{3,2,1,0:T(8,128)S(1)}, u32[]{:S(2)}, u32[]{:S(2)}) collective-permute-start(f32[1,4,8,128]{3,2,1,0:T(8,128)S(1)} %bitcast_add_fusion), channel_id=1, source_target_pairs={{0,128},{64,192},{128,0},{192,64},{1,129},{65,193},{129,1},{193,65... | collective-permute-start | bytes 49160 | tf_op jit(solution)/shard_map/ppermute | solution.py:35
  174.8 1.8 collective-permute-done.18
  (174 shorter events, 103.0 us)
Async XLA Ops:
  0.6 25.7 %copy-start.3 = (f32[3,1,4,8,128]{4,3,2,1,0:T(8,128)S(1)}, f32[3,1,4,8,128]{4,3,2,1,0:T(8,128)}, u32[]{:S(2)}) copy-start(f32[3,1,4,8,128]{4,3,2,1,0:T(8,128)} %param.18) | copy-start | bytes 147460
  0.7 26.1 %copy-start.1 = (f32[4,16,1,4,8,128]{5,4,3,2,1,0:T(8,128)S(1)}, f32[4,16,1,4,8,128]{5,4,3,2,1,0:T(8,128)}, u32[]{:S(2)}) copy-start(f32[4,16,1,4,8,128]{5,4,3,2,1,0:T(8,128)} %param.20) | copy-start | bytes 3145732
  1.6 24.7 %collective-permute-start = (f32[5,4,1,128]{3,2,1,0:T(1,128)S(1)}, f32[5,4,1,128]{3,2,1,0:T(1,128)S(1)}, u32[]{:S(2)}, u32[]{:S(2)}) collective-permute-start(f32[5,4,1,128]{3,2,1,0:T(1,128)S(1)} %get-tuple-element.222), channel_id=1, source_target_pairs={{0,1},{1,2},{2,3},{3,4},{4,5},{5,6},{6,7},{7,8},{8,9},{9,10},{10,1... | collective-permute-start | bytes 30728 | tf_op jit(solution)/shard_map/ppermute | solution.py:24
  5.2 21.1 %collective-permute-start.1 = (f32[5,4,1,128]{3,2,1,0:T(1,128)S(1)}, f32[5,4,1,128]{3,2,1,0:T(1,128)S(1)}, u32[]{:S(2)}, u32[]{:S(2)}) collective-permute-start(f32[5,4,1,128]{3,2,1,0:T(1,128)S(1)} %get-tuple-element.223), channel_id=1, source_target_pairs={{1,0},{2,1},{3,2},{4,3},{5,4},{6,5},{7,6},{8,7},{9,8},{10,9},{11,1... | collective-permute-start | bytes 30728 | tf_op jit(solution)/shard_map/ppermute | solution.py:24
  15.0 11.7 %collective-permute-start.2 = (f32[4,16,4,1,128]{4,3,2,1,0:T(1,128)S(1)}, f32[4,16,4,1,128]{4,3,2,1,0:T(1,128)S(1)}, u32[]{:S(2)}, u32[]{:S(2)}) collective-permute-start(f32[4,16,4,1,128]{4,3,2,1,0:T(1,128)S(1)} %get-tuple-element.196), channel_id=1, source_target_pairs={{0,1},{1,2},{2,3},{3,4},{4,5},{5,6},{6,7},{7,8},{8,9},{9,10},{10,1... | collective-permute-start | bytes 393224 | tf_op jit(solution)/shard_map/ppermute | solution.py:24
  17.0 9.8 %collective-permute-start.3 = (f32[4,16,4,1,128]{4,3,2,1,0:T(1,128)S(1)}, f32[4,16,4,1,128]{4,3,2,1,0:T(1,128)S(1)}, u32[]{:S(2)}, u32[]{:S(2)}) collective-permute-start(f32[4,16,4,1,128]{4,3,2,1,0:T(1,128)S(1)} %get-tuple-element.197), channel_id=1, source_target_pairs={{1,0},{2,1},{3,2},{4,3},{5,4},{6,5},{7,6},{8,7},{9,8},{10,9},{11,1... | collective-permute-start | bytes 393224 | tf_op jit(solution)/shard_map/ppermute | solution.py:24
  31.7 2.9 %collective-permute-start.4 = (f32[8,4,8,128]{3,2,1,0:T(8,128)S(1)}, f32[8,4,8,128]{3,2,1,0:T(8,128)S(1)}, u32[]{:S(2)}, u32[]{:S(2)}) collective-permute-start(f32[8,4,8,128]{3,2,1,0:T(8,128)S(1)} %slice_select_fusion.1), channel_id=1, source_target_pairs={{0,64},{64,0},{128,192},{192,128},{1,65},{65,1},{129,193},{193,129... | collective-permute-start | bytes 393224 | tf_op jit(solution)/shard_map/ppermute | solution.py:34
  34.5 6.3 %collective-permute-start.5 = (f32[8,4,8,128]{3,2,1,0:T(8,128)S(1)}, f32[8,4,8,128]{3,2,1,0:T(8,128)S(1)}, u32[]{:S(2)}, u32[]{:S(2)}) collective-permute-start(f32[8,4,8,128]{3,2,1,0:T(8,128)S(1)} %select_add_fusion.1), channel_id=1, source_target_pairs={{0,128},{64,192},{128,0},{192,64},{1,129},{65,193},{129,1},{193,65... | collective-permute-start | bytes 393224 | tf_op jit(solution)/shard_map/ppermute | solution.py:35
  40.9 2.4 %collective-permute-start.6 = (f32[8,4,8,128]{3,2,1,0:T(8,128)S(1)}, f32[8,4,8,128]{3,2,1,0:T(8,128)S(1)}, u32[]{:S(2)}, u32[]{:S(2)}) collective-permute-start(f32[8,4,8,128]{3,2,1,0:T(8,128)S(1)} %add.232), channel_id=1, source_target_pairs={{0,64},{64,0},{128,192},{192,128},{1,65},{65,1},{129,193},{193,129... | collective-permute-start | bytes 393224 | tf_op jit(solution)/shard_map/ppermute | solution.py:36
  44.3 39.9 %copy-start.8 = (f32[16]{0:T(128)S(1)}, f32[16]{0:T(128)}, u32[]{:S(2)}) copy-start(f32[16]{0:T(128)} %param.29) | copy-start | bytes 196
  44.3 40.0 %copy-start.9 = (f32[16]{0:T(128)S(1)}, f32[16]{0:T(128)}, u32[]{:S(2)}) copy-start(f32[16]{0:T(128)} %param.28) | copy-start | bytes 196
  84.6 1.3 collective-permute-start.7
  85.9 4.1 %collective-permute-start.8 = (f32[1,4,8,128]{3,2,1,0:T(8,128)S(1)}, f32[1,4,8,128]{3,2,1,0:T(8,128)S(1)}, u32[]{:S(2)}, u32[]{:S(2)}) collective-permute-start(f32[1,4,8,128]{3,2,1,0:T(8,128)S(1)} %bitcast_add_fusion.1), channel_id=1, source_target_pairs={{0,128},{64,192},{128,0},{192,64},{1,129},{65,193},{129,1},{193,65... | collective-permute-start | bytes 49160 | tf_op jit(solution)/shard_map/ppermute | solution.py:35
  90.0 2.3 %collective-permute-start.9 = (f32[1,4,8,128]{3,2,1,0:T(8,128)S(1)}, f32[1,4,8,128]{3,2,1,0:T(8,128)S(1)}, u32[]{:S(2)}, u32[]{:S(2)}) collective-permute-start(f32[1,4,8,128]{3,2,1,0:T(8,128)S(1)} %fusion.97), channel_id=1, source_target_pairs={{0,64},{64,0},{128,192},{192,128},{1,65},{65,1},{129,193},{193,129... | collective-permute-start | bytes 49160 | tf_op jit(solution)/shard_map/ppermute | solution.py:36
  92.4 20.1 %collective-permute-start.10 = (f32[5,4,1,128]{3,2,1,0:T(1,128)S(1)}, f32[5,4,1,128]{3,2,1,0:T(1,128)S(1)}, u32[]{:S(2)}, u32[]{:S(2)}) collective-permute-start(f32[5,4,1,128]{3,2,1,0:T(1,128)S(1)} %get-tuple-element.216), channel_id=1, source_target_pairs={{0,1},{1,2},{2,3},{3,4},{4,5},{5,6},{6,7},{7,8},{8,9},{9,10},{10,1... | collective-permute-start | bytes 30728 | tf_op jit(solution)/shard_map/ppermute | solution.py:24
  94.3 18.2 %collective-permute-start.11 = (f32[5,4,1,128]{3,2,1,0:T(1,128)S(1)}, f32[5,4,1,128]{3,2,1,0:T(1,128)S(1)}, u32[]{:S(2)}, u32[]{:S(2)}) collective-permute-start(f32[5,4,1,128]{3,2,1,0:T(1,128)S(1)} %get-tuple-element.217), channel_id=1, source_target_pairs={{1,0},{2,1},{3,2},{4,3},{5,4},{6,5},{7,6},{8,7},{9,8},{10,9},{11,1... | collective-permute-start | bytes 30728 | tf_op jit(solution)/shard_map/ppermute | solution.py:24
  102.8 10.5 %collective-permute-start.12 = (f32[4,16,4,1,128]{4,3,2,1,0:T(1,128)S(1)}, f32[4,16,4,1,128]{4,3,2,1,0:T(1,128)S(1)}, u32[]{:S(2)}, u32[]{:S(2)}) collective-permute-start(f32[4,16,4,1,128]{4,3,2,1,0:T(1,128)S(1)} %get-tuple-element.194), channel_id=1, source_target_pairs={{0,1},{1,2},{2,3},{3,4},{4,5},{5,6},{6,7},{7,8},{8,9},{9,10},{10,1... | collective-permute-start | bytes 393224 | tf_op jit(solution)/shard_map/ppermute | solution.py:24
  104.7 9.5 %collective-permute-start.13 = (f32[4,16,4,1,128]{4,3,2,1,0:T(1,128)S(1)}, f32[4,16,4,1,128]{4,3,2,1,0:T(1,128)S(1)}, u32[]{:S(2)}, u32[]{:S(2)}) collective-permute-start(f32[4,16,4,1,128]{4,3,2,1,0:T(1,128)S(1)} %get-tuple-element.195), channel_id=1, source_target_pairs={{1,0},{2,1},{3,2},{4,3},{5,4},{6,5},{7,6},{8,7},{9,8},{10,9},{11,1... | collective-permute-start | bytes 393224 | tf_op jit(solution)/shard_map/ppermute | solution.py:24
  119.1 2.8 %collective-permute-start.14 = (f32[8,4,8,128]{3,2,1,0:T(8,128)S(1)}, f32[8,4,8,128]{3,2,1,0:T(8,128)S(1)}, u32[]{:S(2)}, u32[]{:S(2)}) collective-permute-start(f32[8,4,8,128]{3,2,1,0:T(8,128)S(1)} %slice_select_fusion), channel_id=1, source_target_pairs={{0,64},{64,0},{128,192},{192,128},{1,65},{65,1},{129,193},{193,129... | collective-permute-start | bytes 393224 | tf_op jit(solution)/shard_map/ppermute | solution.py:34
  121.9 6.3 %collective-permute-start.15 = (f32[8,4,8,128]{3,2,1,0:T(8,128)S(1)}, f32[8,4,8,128]{3,2,1,0:T(8,128)S(1)}, u32[]{:S(2)}, u32[]{:S(2)}) collective-permute-start(f32[8,4,8,128]{3,2,1,0:T(8,128)S(1)} %select_add_fusion), channel_id=1, source_target_pairs={{0,128},{64,192},{128,0},{192,64},{1,129},{65,193},{129,1},{193,65... | collective-permute-start | bytes 393224 | tf_op jit(solution)/shard_map/ppermute | solution.py:35
  128.3 2.3 %collective-permute-start.16 = (f32[8,4,8,128]{3,2,1,0:T(8,128)S(1)}, f32[8,4,8,128]{3,2,1,0:T(8,128)S(1)}, u32[]{:S(2)}, u32[]{:S(2)}) collective-permute-start(f32[8,4,8,128]{3,2,1,0:T(8,128)S(1)} %add.257), channel_id=1, source_target_pairs={{0,64},{64,0},{128,192},{192,128},{1,65},{65,1},{129,193},{193,129... | collective-permute-start | bytes 393224 | tf_op jit(solution)/shard_map/ppermute | solution.py:36
  171.2 1.3 collective-permute-start.17
  172.5 4.1 %collective-permute-start.18 = (f32[1,4,8,128]{3,2,1,0:T(8,128)S(1)}, f32[1,4,8,128]{3,2,1,0:T(8,128)S(1)}, u32[]{:S(2)}, u32[]{:S(2)}) collective-permute-start(f32[1,4,8,128]{3,2,1,0:T(8,128)S(1)} %bitcast_add_fusion), channel_id=1, source_target_pairs={{0,128},{64,192},{128,0},{192,64},{1,129},{65,193},{129,1},{193,65... | collective-permute-start | bytes 49160 | tf_op jit(solution)/shard_map/ppermute | solution.py:35
  176.6 2.7 %collective-permute-start.19 = (f32[1,4,8,128]{3,2,1,0:T(8,128)S(1)}, f32[1,4,8,128]{3,2,1,0:T(8,128)S(1)}, u32[]{:S(2)}, u32[]{:S(2)}) collective-permute-start(f32[1,4,8,128]{3,2,1,0:T(8,128)S(1)} %fusion.96), channel_id=1, source_target_pairs={{0,64},{64,0},{128,192},{192,128},{1,65},{65,1},{129,193},{193,129... | collective-permute-start | bytes 49160 | tf_op jit(solution)/shard_map/ppermute | solution.py:36
  (9 other events, 78.1 us)

commit v2 on v0

v2 whole, which is shorter than its diff:
```python
import math

import jax
import jax.numpy as jnp
from jax import lax
from jax.experimental import pallas as pl
from jax.experimental.pallas import tpu as pltpu
from jax.sharding import PartitionSpec as P

FIELDS = 4
SPECIES = 16
ALL_FIELDS = 16
REACT = 96
SUBS = 4
CZ, CY, NX = 4, 8, 128

time_step = 0.1
viscosity = 0.4
diffusivity = 0.3
relaxation = 2.0
noise_half = 0.5 * math.sqrt(2.0 * 0.3 * 0.1)
speed_half = 0.5 * time_step
spread = time_step * diffusivity
f32 = jnp.float32
bf16 = jnp.bfloat16

SPECIES_ROWS = 2 * FIELDS * CZ * SPECIES
FLOW_ROWS = 2 * CZ * 8
MESSAGE_ROWS = SPECIES_ROWS + FLOW_ROWS + CZ * 16


def lanes(shape):
    return lax.broadcasted_iota(jnp.int32, shape, 1)


def shift_x(value, lane):
    ahead = jnp.where(lane == NX - 1, 0.0, pltpu.roll(value, NX - 1, 1))
    behind = jnp.where(lane == 0, 0.0, pltpu.roll(value, 1, 1))
    return ahead, behind


def stencil(column, above, below, z, lane):
    zero = jnp.zeros_like(column[z])
    up = column[z + 1] if z + 1 < CZ else zero
    down = column[z - 1] if z > 0 else zero
    ahead, behind = shift_x(column[z], lane)
    total = (up + down) + (above[z] + below[z]) + (ahead + behind)
    return total, (up - down, above[z] - below[z], ahead - behind)


def pack(
    species, density, velocity, energy, wiener, mix, substeps,
    low, high, own, flow, noise_first, noise_second,
):
    for z in range(CZ):
        base = z * CY * 8
        rows = [density[0, z], velocity[0, 0, z], velocity[1, 0, z], velocity[2, 0, z], energy[0, z],
                time_step * mix[0, z], substeps[0, z].astype(f32), jnp.zeros((CY, NX), f32)]
        for v in range(8):
            for y in range(CY):
                flow[y, z, v : v + 1] = rows[v][y : y + 1]

    def layer(y, _):
        for z in range(CZ):
            for f in range(FIELDS):
                own[y, f, z] = species[pl.ds(f * 512 + z * 8 + y, SPECIES, stride=32), :]
            noise_first[y, z] = jnp.concatenate(
                [wiener[pl.ds(z * 8 + y, 12, stride=32), :], jnp.zeros((4, NX), f32)], 0
            )
            noise_second[y, z] = jnp.concatenate(
                [wiener[pl.ds(384 + z * 8 + y, 12, stride=32), :], jnp.zeros((4, NX), f32)], 0
            )
        return 0

    lax.fori_loop(0, CY, layer, 0)
    for out, first, edge in ((low, 0, 0), (high, CY - 2, CY - 1)):
        for y in range(2):
            for f in range(FIELDS):
                for z in range(CZ):
                    row = ((y * FIELDS + f) * CZ + z) * SPECIES
                    out[row : row + SPECIES] = own[first + y, f, z]
            for z in range(CZ):
                row = SPECIES_ROWS + (y * CZ + z) * 8
                out[row : row + 8] = flow[first + y, z]
        for z in range(CZ):
            row = SPECIES_ROWS + FLOW_ROWS + z * 16
            out[row : row + 16] = noise_first[edge, z]


def flow_step(source, y, lane, keep):
    column = [source[y, z] for z in range(CZ)]
    above = [source[y + 1, z] for z in range(CZ)]
    below = [source[y - 1, z] for z in range(CZ)]
    row = lax.broadcasted_iota(jnp.int32, (8, NX), 0)
    results = []
    for z in range(CZ):
        total, change = stencil(column, above, below, z, lane)
        centre = column[z]
        moved = (
            source[y, z, 1:2] * change[0] + source[y, z, 2:3] * change[1] + source[y, z, 3:4] * change[2]
        )
        new = centre + time_step * viscosity * (total - 6.0 * centre) - speed_half * moved
        if keep is not None:
            new = new * keep
        results.append(jnp.where(row < 5, new, centre))
    return results


def transport(get, y, noise, noise_y, speeds, speeds_y, lane, emit):
    slow = [[speed_half * speeds[speeds_y, z, 1 + d : 2 + d] for d in range(3)] for z in range(CZ)]
    for f in range(FIELDS):
        column = [get(y, f, z) for z in range(CZ)]
        above = [get(y + 1, f, z) for z in range(CZ)]
        below = [get(y - 1, f, z) for z in range(CZ)]
        for z in range(CZ):
            total, change = stencil(column, above, below, z, lane)
            value = (1.0 - 6.0 * spread) * column[z] + spread * total
            for d in range(3):
                weight = noise_half * noise[noise_y, z, 3 * f + d : 3 * f + d + 1] - slow[z][d]
                value = value + weight * change[d]
            emit(f, z, value)


def store_halves(total, mine, other):
    core = lax.rem(lax.axis_index("field"), 2)
    for i in range(CZ // 2):
        mine[i] = total[core * 2 + i]
        other[i] = total[(1 - core) * 2 + i]


def join_halves(mine, other, total):
    core = lax.rem(lax.axis_index("field"), 2)
    for i in range(CZ // 2):
        total[core * 2 + i] = mine[i]
        total[(1 - core) * 2 + i] = other[i]


def first_step(
    own, flow, noise_first, low_halo, high_halo,
    carried, flow_one, mine, other,
    wide, wide_flow, wide_noise, total,
):
    tile = lax.axis_index("tile")
    last = lax.axis_size("tile") - 1
    lane, lane_flow = lanes((SPECIES, NX)), lanes((8, NX))
    wide[2 : CY + 2] = own[...]
    wide_flow[2 : CY + 2] = flow[...]
    wide_noise[1 : CY + 1] = noise_first[...]
    for halo, at, edge in ((low_halo, 0, 0), (high_halo, CY + 2, CY + 1)):
        wide[at : at + 2] = halo[0:SPECIES_ROWS].reshape(2, FIELDS, CZ, SPECIES, NX)
        wide_flow[at : at + 2] = halo[SPECIES_ROWS : SPECIES_ROWS + FLOW_ROWS].reshape(2, CZ, 8, NX)
        wide_noise[edge] = halo[SPECIES_ROWS + FLOW_ROWS :].reshape(CZ, 16, NX)

    def layer(y, _):
        outside = ((y == 0) & (tile == 0)) | ((y == CY + 1) & (tile == last))
        keep = jnp.where(outside, 0.0, 1.0).astype(f32)
        for z, new in enumerate(flow_step(wide_flow, y + 1, lane_flow, keep)):
            flow_one[y, z] = new
        sums = [None] * CZ

        def emit(f, z, value):
            value = value * keep
            carried[y, f, z] = value
            sums[z] = value if sums[z] is None else sums[z] + value

        transport(lambda at, f, z: wide[at, f, z], y + 1, wide_noise, y, flow_one, y, lane, emit)
        for z in range(CZ):
            total[z, y] = sums[z]
        return 0

    lax.fori_loop(0, CY + 2, layer, 0)
    store_halves(total, mine, other)


def prepare(reactants, stoich, weights):
    for j in range(SPECIES):
        product = reactants[j : j + 1] * stoich[...]
        high = product.astype(bf16)
        low = (product - high.astype(f32)).astype(bf16)
        weights[SPECIES * j : SPECIES * (j + 1)] = jnp.concatenate([high, low, high], 1)


def form(consts, flow, y, weights, rates, out, out_y):
    for z in range(CZ):
        level = flow[y, z, 4:5] - 1.0
        length = time_step / jnp.maximum(flow[y, z, 6:7], 1.0)
        rate = consts[0:REACT] * jnp.exp(consts[REACT : 2 * REACT] * level) * length
        high = rate.astype(bf16)
        low = (rate - high.astype(f32)).astype(bf16)
        at = slice(NX * z, NX * (z + 1))
        rates[0:REACT, at] = high
        rates[REACT : 2 * REACT, at] = high
        rates[2 * REACT : 3 * REACT, at] = low
    out[out_y] = jnp.dot(weights[...], rates[...], preferred_element_type=f32)


def react(matrices, y, z, flow, flow_y, values, held):
    count = jnp.broadcast_to(flow[flow_y, z, 6:7], (SPECIES, NX))
    for k in range(SUBS):
        for n, value in enumerate(values):
            held[z, n] = value
        changes = [None] * len(values)
        for j in range(SPECIES):
            block = matrices[y, SPECIES * j : SPECIES * (j + 1), NX * z : NX * (z + 1)]
            for n in range(len(values)):
                part = block * held[z, n, j : j + 1]
                changes[n] = part if changes[n] is None else changes[n] + part
        values = [value + jnp.where(count > float(k), change, 0.0) for value, change in zip(values, changes)]
    return values


def react_first(
    carried, flow_one, noise_second, wiener, reactants, stoich, consts,
    matrices, partial, mine, other,
    weights, rates, held, reacted, flow_two, total,
):
    prepare(reactants, stoich, weights)
    lane, lane_flow = lanes((SPECIES, NX)), lanes((8, NX))

    def react_layer(y, _):
        form(consts, flow_one, y, weights, rates, matrices, y)
        for z in range(CZ):
            values = react(matrices, y, z, flow_one, y, [carried[y, f, z] for f in range(FIELDS)], held)
            own_share = 1.0 - flow_one[y, z, 5:6]
            for f in range(FIELDS):
                reacted[y, f, z] = own_share * values[f]
        return 0

    lax.fori_loop(0, CY + 2, react_layer, 0)

    def layer(y, _):
        for z, new in enumerate(flow_step(flow_one, y + 1, lane_flow, None)):
            flow_two[y, z] = new
        sums = [None] * CZ

        def emit(f, z, value):
            partial[y, f, z] = value
            sums[z] = value if sums[z] is None else sums[z] + value

        transport(lambda at, f, z: reacted[at, f, z], y + 1, noise_second, y, flow_two, y, lane, emit)
        for z in range(CZ):
            total[z, pl.ds(y * SPECIES, SPECIES)] = sums[z]
        return 0

    lax.fori_loop(0, CY, layer, 0)
    for z in range(CZ):
        for d in range(3):
            rows = [384 + (f * 3 + d) * 32 + z * 8 for f in range(FIELDS)]
            total[z, 128 + 8 * d : 136 + 8 * d] = (
                (wiener[rows[0] : rows[0] + 8] + wiener[rows[1] : rows[1] + 8])
                + (wiener[rows[2] : rows[2] + 8] + wiener[rows[3] : rows[3] + 8])
            )
    store_halves(total, mine, other)


def add_sources(flow_tile, total, after, heat, molar):
    density = jnp.sum(molar * after, 0, keepdims=True) / ALL_FIELDS
    released = jnp.sum(heat * (after - total), 0, keepdims=True) / ALL_FIELDS
    row = lax.broadcasted_iota(jnp.int32, (8, NX), 0)
    with_density = flow_tile + time_step * relaxation * (density - flow_tile)
    return jnp.where(row == 0, with_density, jnp.where(row == 4, flow_tile + released, flow_tile))


def second_step(
    sum_mine, sum_other, flow_one, matrices, partial, noise_second, reactants, stoich, consts,
    matrices_two, own_part, shared, flow_two,
    total, flow_mid, weights, rates, held,
):
    prepare(reactants, stoich, weights)
    join_halves(sum_mine, sum_other, total)
    lane, lane_flow = lanes((SPECIES, NX)), lanes((8, NX))

    def mean_layer(y, _):
        for z in range(CZ):
            before = total[z, y]
            (after,) = react(matrices, y, z, flow_one, y, [before], held)
            shared[y, z] = (flow_one[y, z, 5:6] / ALL_FIELDS) * after
            flow_mid[y, z] = add_sources(
                flow_one[y, z], before, after, consts[192:208], consts[208:224]
            )
        return 0

    lax.fori_loop(0, CY + 2, mean_layer, 0)

    def layer(y, _):
        for z, new in enumerate(flow_step(flow_mid, y + 1, lane_flow, None)):
            flow_two[y, z] = new
        form(consts, flow_two, y, weights, rates, matrices_two, y)
        column = [shared[y + 1, z] for z in range(CZ)]
        above = [shared[y + 2, z] for z in range(CZ)]
        below = [shared[y, z] for z in range(CZ)]
        for z in range(CZ):
            neighbour_sum, change = stencil(column, above, below, z, lane)
            base = (1.0 - 6.0 * spread) * column[z] + spread * neighbour_sum
            slow = [speed_half * flow_two[y, z, 1 + d : 2 + d] for d in range(3)]
            values = []
            for f in range(FIELDS):
                value = partial[y, f, z] + base
                for d in range(3):
                    weight = noise_half * noise_second[y, z, 3 * f + d : 3 * f + d + 1] - slow[d]
                    value = value + weight * change[d]
                values.append(value)
            values = react(matrices_two, y, z, flow_two, y, values, held)
            own_share = 1.0 - flow_two[y, z, 5:6]
            for f in range(FIELDS):
                own_part[y, f, z] = own_share * values[f]
        return 0

    lax.fori_loop(0, CY, layer, 0)


def finish(
    sum_mine, sum_other, shared, flow_two, matrices_two, own_part, consts,
    flow_out, species_out,
    total, held,
):
    join_halves(sum_mine, sum_other, total)
    lane = lanes((SPECIES, NX))

    def layer(y, _):
        column = [shared[y + 1, z] for z in range(CZ)]
        above = [shared[y + 2, z] for z in range(CZ)]
        below = [shared[y, z] for z in range(CZ)]
        for z in range(CZ):
            neighbour_sum, change = stencil(column, above, below, z, lane)
            before = total[z, pl.ds(y * SPECIES, SPECIES)] + ALL_FIELDS * (
                (1.0 - 6.0 * spread) * column[z] + spread * neighbour_sum
            )
            for d in range(3):
                weight = (
                    noise_half * total[z, pl.ds(128 + 8 * d + y, 1)]
                    - ALL_FIELDS * speed_half * flow_two[y, z, 1 + d : 2 + d]
                )
                before = before + weight * change[d]
            (after,) = react(matrices_two, y, z, flow_two, y, [before], held)
            tile = add_sources(flow_two[y, z], before, after, consts[192:208], consts[208:224])
            for v in range(5):
                flow_out[v, z, pl.ds(y, 1)] = tile[v : v + 1]
            mean = (flow_two[y, z, 5:6] / ALL_FIELDS) * after
            for f in range(FIELDS):
                species_out[pl.ds(f * 512 + z * 8 + y, SPECIES, stride=32), :] = own_part[y, f, z] + mean
        return 0

    lax.fori_loop(0, CY, layer, 0)


def call(kernel, name, outs, scratch, flops, *operands):
    shapes = tuple(jax.ShapeDtypeStruct(shape, f32) for shape in outs)
    moved = sum(4 * math.prod(shape) for shape in outs) + sum(x.size * 4 for x in operands)
    return pl.pallas_call(
        kernel,
        out_shape=shapes,
        scratch_shapes=[pltpu.VMEM(*entry) for entry in scratch],
        cost_estimate=pl.CostEstimate(flops=flops, bytes_accessed=moved, transcendentals=0),
        compiler_params=pltpu.CompilerParams(vmem_limit_bytes=24 << 20),
        name=name,
    )(*operands)


def move(value, axis, pairs):
    return lax.ppermute(value, axis, pairs)


def field_total(mine, other):
    core_pairs = [(i, i ^ 1) for i in range(4)]
    chip_pairs = [(i, i ^ 2) for i in range(4)]
    mine = mine + move(other, "field", core_pairs)
    mine = mine + move(mine, "field", chip_pairs)
    return mine, move(mine, "field", core_pairs)


def on_device(
    density, velocity, energy, species, wiener, substeps, mix_rate,
    reactants, stoich, kinetic_constants, excitation_sensitivity, heat, molar,
):
    tiles = lax.axis_size("tile")
    wide = CY + 2
    noise_rows = wiener.reshape(-1, NX)
    consts = jnp.broadcast_to(
        jnp.concatenate([kinetic_constants, excitation_sensitivity, heat, molar])[:, None], (2 * REACT + 32, NX)
    )
    by_species = reactants.T
    grid = (FIELDS, CZ, SPECIES, NX)
    low, high, own, flow, noise_first, noise_second = call(
        pack, "pack",
        [(MESSAGE_ROWS, NX)] * 2 + [(CY,) + grid, (CY, CZ, 8, NX), (CY, CZ, 16, NX), (CY, CZ, 16, NX)],
        [], 10**6,
        species.reshape(-1, NX), density, velocity, energy, noise_rows, mix_rate, substeps,
    )
    low_halo = move(high, "tile", [(i, i + 1) for i in range(tiles - 1)])
    high_halo = move(low, "tile", [(i + 1, i) for i in range(tiles - 1)])
    carried, flow_one, mine, other = call(
        first_step, "first_step",
        [(wide,) + grid, (wide, CZ, 8, NX)] + [(2, wide, SPECIES, NX)] * 2,
        [((CY + 4,) + grid, f32), ((CY + 4, CZ, 8, NX), f32), ((wide, CZ, 16, NX), f32), ((CZ, wide, SPECIES, NX), f32)],
        10**7, own, flow, noise_first, low_halo, high_halo,
    )
    first_sum = field_total(mine, other)
    working = [((256, 3 * REACT), bf16), ((3 * REACT, CZ * NX), bf16)]
    held = ((CZ, FIELDS, SPECIES, NX), f32)
    matrices, partial, mine, other = call(
        react_first, "react_first",
        [(wide, 256, CZ * NX), (CY,) + grid] + [(2, 152, NX)] * 2,
        working + [held, ((wide,) + grid, f32), ((CY, CZ, 8, NX), f32), ((CZ, 152, NX), f32)],
        10**9, carried, flow_one, noise_second, noise_rows, by_species, stoich, consts,
    )
    second_sum = field_total(mine, other)
    matrices_two, own_part, shared, flow_two = call(
        second_step, "second_step",
        [(CY, 256, CZ * NX), (CY,) + grid, (wide, CZ, SPECIES, NX), (CY, CZ, 8, NX)],
        [((CZ, wide, SPECIES, NX), f32), ((wide, CZ, 8, NX), f32)] + working + [held],
        10**9, *first_sum, flow_one, matrices, partial, noise_second, by_species, stoich, consts,
    )
    flow_out, species_out = call(
        finish, "finish",
        [(5, CZ, CY, NX), (FIELDS * SPECIES * CZ * CY, NX)],
        [((CZ, 152, NX), f32), held],
        10**8, *second_sum, shared, flow_two, matrices_two, own_part, consts,
    )
    return flow_out[:, None], species_out.reshape(species.shape)


def solution(mesh):
    placed = (
        P("tile", None, None, None),
        P(None, "tile", None, None, None),
        P("tile", None, None, None),
        P("field", None, "tile", None, None, None),
        P(None, "field", None, "tile", None, None, None),
        P("tile", None, None, None),
        P("tile", None, None, None),
        P(),
        P(),
        P(),
        P(),
        P(),
        P(),
    )
    return jax.shard_map(
        on_device,
        mesh=mesh,
        in_specs=placed,
        out_specs=(P(None, "tile", None, None, None), P("field", None, "tile", None, None, None)),
        check_vma=False,
    )
```

time: 305 us -> 71.4 us (0.23)
  matrix products: 102 us -> 0 us
  waiting for transfers between devices: 92.8 us -> 10.4 us
  Pallas kernels: 0 us -> 29.4 us
  blocking collectives: 26.4 us -> 0 us
  starting transfers between devices: 41.2 us -> 20.7 us
  other arithmetic: 17.6 us -> 0.86 us
  between operations: 14.6 us -> 0.74 us
    dot_general x64 -> x0, matrix products: 102 us -> none  [the longest x32 71.9 us: react_field(): driving = jnp.dot(reactants, flattened, precision=lax.Precision.HIGHEST)]
    psum x2 -> x0, waiting for transfers between devices: 91.5 us -> none  [on_device(): field_sum = lax.psum(jnp.sum(carried, 0), 'field')]
    pallas_call x0 -> x5, Pallas kernels: none -> 29.4 us  [call(): pl.pallas_call(kernel, out_shape=shapes, scratch_shapes=[pltpu.VMEM(*entr...]
    psum x2 -> x0, blocking collectives: 26.4 us -> none  [on_device(): returned = lax.psum(partials, 'field') / REALIZATIONS]
    ppermute x8, starting transfers between devices: 40.9 us -> 20.7 us  [move(): return lax.ppermute(value, axis, pairs)]
    ppermute x8, waiting for transfers between devices: 1.25 us -> 10.4 us  [move(): return lax.ppermute(value, axis, pairs)]
    concatenate x6 -> x1, other arithmetic: 6.99 us -> 0.78 us  [on_device(): jnp.concatenate([kinetic_constants, excitation_sensitivity, heat, molar])]
    reduce_sum x4 -> x0, other arithmetic: 5.87 us -> none  [the longest x2 5.26 us: on_device(): field_sum = lax.psum(jnp.sum(carried, 0), 'field')]
  transfers between devices with their start and end apart: 10 -> 8, of which waited for: 3 -> 4; matrix products, arithmetic and copies ran while one was open for 2% -> 1% of each run, Pallas kernels for 0% -> 30%
where the time goes in v2:
time: 71.4 us; the launch traced here: 70.5 us
  Pallas kernels  29.4 us (41%)
  starting transfers between devices  20.7 us (29%)
  waiting for transfers between devices  10.4 us (15%)
  local copies, waits for them, and re-layouts  8.35 us (12%)
  other arithmetic  0.86 us (1%)
  between operations  0.74 us (1%)
    pallas_call x5, Pallas kernels, call(): pl.pallas_call(kernel, out_shape=shapes, scratch_shapes=[pltpu.VMEM(*entr...  29.4 us
    ppermute x8, starting transfers between devices, move(): return lax.ppermute(value, axis, pairs)  20.7 us
    ppermute x8, waiting for transfers between devices, move(): return lax.ppermute(value, axis, pairs)  10.4 us
    unnamed x20, local copies, waits for them, and re-layouts  8.27 us
  transfers between devices with their start and end apart: 8, of which 4 were waited for; matrix products, arithmetic and copies ran while one was open for 1% of the time, Pallas kernels for 30%

profile of v2, /device:TPU:9, one launch (start us, length us, event | category | flops | bytes accessed | tf_op | source)
XLA Modules:
  0.0 70.5 jit_solution(1542835032431518835)
XLA Ops:
  0.6 1.2 %copy-done = f32[4,16,1,4,8,128]{5,4,3,2,1,0:T(8,128)S(1)} copy-done((f32[4,16,1,4,8,128]{5,4,3,2,1,0:T(8,128)S(1)}, f32[4,16,1,4,8,128]{5,4,3,2,1,0:T(8,128)}, u32[]{:S(2)}) %copy-start) | copy-done | bytes 1048600
  1.9 1.0 %copy-done.1 = f32[2,4,3,1,4,8,128]{6,5,4,3,2,1,0:T(8,128)S(1)} copy-done((f32[2,4,3,1,4,8,128]{6,5,4,3,2,1,0:T(8,128)S(1)}, f32[2,4,3,1,4,8,128]{6,5,4,3,2,1,0:T(8,128)}, u32[]{:S(2)}) %copy-start.1) | copy-done | bytes 393240
  2.9 0.8 %copy-done.3 = f32[3,1,4,8,128]{4,3,2,1,0:T(8,128)S(1)} copy-done((f32[3,1,4,8,128]{4,3,2,1,0:T(8,128)S(1)}, f32[3,1,4,8,128]{4,3,2,1,0:T(8,128)}, u32[]{:S(2)}) %copy-start.3) | copy-done | bytes 49176
  3.7 0.7 %copy-done.4 = f32[1,4,8,128]{3,2,1,0:T(8,128)S(1)} copy-done((f32[1,4,8,128]{3,2,1,0:T(8,128)S(1)}, f32[1,4,8,128]{3,2,1,0:T(8,128)}, u32[]{:S(2)}) %copy-start.4) | copy-done | bytes 16408
  4.4 0.7 %copy-done.5 = f32[1,4,8,128]{3,2,1,0:T(8,128)S(1)} copy-done((f32[1,4,8,128]{3,2,1,0:T(8,128)S(1)}, f32[1,4,8,128]{3,2,1,0:T(8,128)}, u32[]{:S(2)}) %copy-start.5) | copy-done | bytes 16408
  5.1 0.7 %copy-done.6 = f32[1,4,8,128]{3,2,1,0:T(8,128)S(1)} copy-done((f32[1,4,8,128]{3,2,1,0:T(8,128)S(1)}, f32[1,4,8,128]{3,2,1,0:T(8,128)}, u32[]{:S(2)}) %copy-start.6) | copy-done | bytes 16408
  6.5 1.2 %pack.1 = (f32[640,128]{1,0:T(8,128)S(1)}, f32[640,128]{1,0:T(8,128)S(1)}, f32[8,4,4,16,128]{4,3,2,1,0:T(8,128)S(1)}, f32[8,4,8,128]{3,2,1,0:T(8,128)S(1)}, f32[...) custom-call(f32[2048,128]{1,0:T(8,128)S(1)} %bitcast.9, f32[1,4,8,128]{3,2,1,0:T(8,128)S(1)} %copy-done.4, ...), custom_call_target="tpu_custom_call" | custom-call | flops 1000000 | bytes 3915776 | tf_op jit(solution)/shard_map/pack/pallas_call | solution.py:350
  7.8 3.5 %collective-permute-start = (f32[640,128]{1,0:T(8,128)S(1)}, f32[640,128]{1,0:T(8,128)S(1)}, u32[]{:S(2)}, u32[]{:S(2)}) collective-permute-start(f32[640,128]{1,0:T(8,128)S(1)} %get-tuple-element.25), channel_id=1, source_target_pairs={{0,1},{1,2},{2,3},{3,4},{4,5},{5,6},{6,7},{7,8},{8,9},{9,10},{10,1... | collective-permute-start | bytes 983048 | tf_op jit(solution)/shard_map/ppermute | solution.py:361
  11.3 7.9 %collective-permute-start.1 = (f32[640,128]{1,0:T(8,128)S(1)}, f32[640,128]{1,0:T(8,128)S(1)}, u32[]{:S(2)}, u32[]{:S(2)}) collective-permute-start(f32[640,128]{1,0:T(8,128)S(1)} %get-tuple-element.26), channel_id=1, source_target_pairs={{1,0},{2,1},{3,2},{4,3},{5,4},{6,5},{7,6},{8,7},{9,8},{10,9},{11,1... | collective-permute-start | bytes 983048 | tf_op jit(solution)/shard_map/ppermute | solution.py:361
  19.3 5.5 %collective-permute-done.low_halo = f32[640,128]{1,0:T(8,128)S(1)} collective-permute-done((f32[640,128]{1,0:T(8,128)S(1)}, f32[640,128]{1,0:T(8,128)S(1)}, u32[]{:S(2)}, u32[]{:S(2)}) %collective-permute-start) | collective-permute-done | bytes 327712 | tf_op jit(solution)/shard_map/ppermute | solution.py:361
  24.8 0.9 %collective-permute-done.1.high_halo = f32[640,128]{1,0:T(8,128)S(1)} collective-permute-done((f32[640,128]{1,0:T(8,128)S(1)}, f32[640,128]{1,0:T(8,128)S(1)}, u32[]{:S(2)}, u32[]{:S(2)}) %collective-permute-start.1) | collective-permute-done | bytes 327712 | tf_op jit(solution)/shard_map/ppermute | solution.py:361
  25.6 2.0 %first_step.1 = (f32[10,4,4,16,128]{4,3,2,1,0:T(8,128)S(1)}, f32[10,4,8,128]{3,2,1,0:T(8,128)S(1)}, f32[2,10,16,128]{3,2,1,0:T(8,128)S(1)}, f32[2,10,16,128]{3,2,1,0:T(8,128)S(1)}) custom-call(f32[8,4,4,16,128]{4,3,2,1,0:T(8,128)S(1)} %get-tuple-element.22.own, f32[8,4,8,128]{3,2,1,0:T(8,128)S(1)} %get-tuple-element.23.flow, ...), custom_call_target="tpu_custom_call" | custom-call | flops 10000000 | bytes 3899392 | tf_op jit(solution)/shard_map/first_step/pallas_call | solution.py:350
  27.6 1.6 %collective-permute-start.5 = (f32[2,10,16,128]{3,2,1,0:T(8,128)S(1)}, f32[2,10,16,128]{3,2,1,0:T(8,128)S(1)}, u32[]{:S(2)}, u32[]{:S(2)}) collective-permute-start(f32[2,10,16,128]{3,2,1,0:T(8,128)S(1)} %get-tuple-element.33), channel_id=1, source_target_pairs={{0,64},{64,0},{128,192},{192,128},{1,65},{65,1},{129,193},{193,129... | collective-permute-start | bytes 491528 | tf_op jit(solution)/shard_map/ppermute | solution.py:361
  29.3 0.8 %pad_maximum_fusion = f32[224]{0:T(256)S(1)} fusion(f32[16]{0:T(128)} %param.25, f32[16]{0:T(128)} %param.24, f32[96]{0:T(128)} %param.23, f32[96]{0:T(128)} %param.22), kind=kLoop, calls=%fused_computation | loop fusion | flops 672 | bytes 1792 | tf_op jit(solution)/shard_map/concatenate | solution.py:380
  30.2 1.0 %copy-done.2 = f32[2,4,3,1,4,8,128]{6,5,4,3,2,1,0:T(8,128)S(1)} copy-done((f32[2,4,3,1,4,8,128]{6,5,4,3,2,1,0:T(8,128)S(1)}, f32[2,4,3,1,4,8,128]{6,5,4,3,2,1,0:T(8,128)}, u32[]{:S(2)}) %copy-start.2) | copy-done | bytes 393240
  32.5 10.5 %react_first.1 = (f32[10,256,512]{2,1,0:T(8,128)S(1)}, f32[8,4,4,16,128]{4,3,2,1,0:T(8,128)S(1)}, f32[2,152,128]{2,1,0:T(8,128)S(1)}, f32[2,152,128]{2,1,0:T(8,128)S(1)}) custom-call(f32[10,4,4,16,128]{4,3,2,1,0:T(8,128)S(1)} %get-tuple-element.27.carried, f32[10,4,8,128]{3,2,1,0:T(8,128)S(1)} %get-tuple-element.28.flow_one, ...), custom_call_target="tpu_custom_call" | custom-call | flops 1000000000 | bytes 8859648 | tf_op jit(solution)/shard_map/react_first/pallas_call | solution.py:350
  43.2 2.4 %collective-permute-start.6 = (f32[2,10,16,128]{3,2,1,0:T(8,128)S(1)}, f32[2,10,16,128]{3,2,1,0:T(8,128)S(1)}, u32[]{:S(2)}, u32[]{:S(2)}) collective-permute-start(f32[2,10,16,128]{3,2,1,0:T(8,128)S(1)} %add.14), channel_id=1, source_target_pairs={{0,128},{64,192},{128,0},{192,64},{1,129},{65,193},{129,1},{193,65... | collective-permute-start | bytes 491528 | tf_op jit(solution)/shard_map/ppermute | solution.py:361
  45.6 1.3 %collective-permute-start.3 = (f32[2,152,128]{2,1,0:T(8,128)S(1)}, f32[2,152,128]{2,1,0:T(8,128)S(1)}, u32[]{:S(2)}, u32[]{:S(2)}) collective-permute-start(f32[2,152,128]{2,1,0:T(8,128)S(1)} %add.12), channel_id=1, source_target_pairs={{0,128},{64,192},{128,0},{192,64},{1,129},{65,193},{129,1},{193,65... | collective-permute-start | bytes 466952 | tf_op jit(solution)/shard_map/ppermute | solution.py:361
  47.0 3.1 %collective-permute-done.6 = f32[2,10,16,128]{3,2,1,0:T(8,128)S(1)} collective-permute-done((f32[2,10,16,128]{3,2,1,0:T(8,128)S(1)}, f32[2,10,16,128]{3,2,1,0:T(8,128)S(1)}, u32[]{:S(2)}, u32[]{:S(2)}) %collective-permute-start.6) | collective-permute-done | bytes 163872 | tf_op jit(solution)/shard_map/ppermute | solution.py:361
  50.1 2.4 %collective-permute-start.7 = (f32[2,10,16,128]{3,2,1,0:T(8,128)S(1)}, f32[2,10,16,128]{3,2,1,0:T(8,128)S(1)}, u32[]{:S(2)}, u32[]{:S(2)}) collective-permute-start(f32[2,10,16,128]{3,2,1,0:T(8,128)S(1)} %add.15.sum_mine), channel_id=1, source_target_pairs={{0,64},{64,0},{128,192},{192,128},{1,65},{65,1},{129,193},{193,129... | collective-permute-start | bytes 491528 | tf_op jit(solution)/shard_map/ppermute | solution.py:361
  52.5 1.0 %collective-permute-done.3 = f32[2,152,128]{2,1,0:T(8,128)S(1)} collective-permute-done((f32[2,152,128]{2,1,0:T(8,128)S(1)}, f32[2,152,128]{2,1,0:T(8,128)S(1)}, u32[]{:S(2)}, u32[]{:S(2)}) %collective-permute-start.3) | collective-permute-done | bytes 155680 | tf_op jit(solution)/shard_map/ppermute | solution.py:361
  53.5 1.4 %collective-permute-start.4 = (f32[2,152,128]{2,1,0:T(8,128)S(1)}, f32[2,152,128]{2,1,0:T(8,128)S(1)}, u32[]{:S(2)}, u32[]{:S(2)}) collective-permute-start(f32[2,152,128]{2,1,0:T(8,128)S(1)} %add.13.sum_mine), channel_id=1, source_target_pairs={{0,64},{64,0},{128,192},{192,128},{1,65},{65,1},{129,193},{193,129... | collective-permute-start | bytes 466952 | tf_op jit(solution)/shard_map/ppermute | solution.py:361
  54.9 11.0 %second_step.1 = (f32[8,256,512]{2,1,0:T(8,128)S(1)}, f32[8,4,4,16,128]{4,3,2,1,0:T(8,128)S(1)}, f32[10,4,16,128]{3,2,1,0:T(8,128)S(1)}, f32[8,4,8,128]{3,2,1,0:T(8,128)S(1)}) custom-call(f32[2,10,16,128]{3,2,1,0:T(8,128)S(1)} %add.15.sum_mine, f32[2,10,16,128]{3,2,1,0:T(8,128)S(1)} %collective-permute-done.7.sum_other, ...), custom_call_target="tpu_custom_call" | custom-call | flops 1000000000 | bytes 12873728 | tf_op jit(solution)/shard_map/second_step/pallas_call | solution.py:350
  65.9 4.6 %finish.1 = (f32[5,4,8,128]{3,2,1,0:T(8,128)}, f32[2048,128]{1,0:T(8,128)}) custom-call(f32[2,152,128]{2,1,0:T(8,128)S(1)} %add.13.sum_mine, f32[2,152,128]{2,1,0:T(8,128)S(1)} %collective-permute-done.4.sum_other, f32[10,4,16,128]{3,2,1,0:T(8,128)S(1)} %get-tuple-element.36.shared, f32[8,4,8,128]{3,2,1,0:T(8,128)S(1)} %get-tuple-element.37.flow_two, ...), custom_call_target="tpu_custom_call" | custom-call | flops 100000000 | bytes 7258112 | tf_op jit(solution)/shard_map/finish/pallas_call | solution.py:350
  (23 shorter events, 2.4 us)
Async XLA Ops:
  0.6 1.2 %copy-start = (f32[4,16,1,4,8,128]{5,4,3,2,1,0:T(8,128)S(1)}, f32[4,16,1,4,8,128]{5,4,3,2,1,0:T(8,128)}, u32[]{:S(2)}) copy-start(f32[4,16,1,4,8,128]{5,4,3,2,1,0:T(8,128)} %param.16) | copy-start | bytes 3145732
  1.9 1.0 %copy-start.1 = (f32[2,4,3,1,4,8,128]{6,5,4,3,2,1,0:T(8,128)S(1)}, f32[2,4,3,1,4,8,128]{6,5,4,3,2,1,0:T(8,128)}, u32[]{:S(2)}) copy-start(f32[2,4,3,1,4,8,128]{6,5,4,3,2,1,0:T(8,128)} %param.17) | copy-start | bytes 1179652
  2.9 0.8 %copy-start.3 = (f32[3,1,4,8,128]{4,3,2,1,0:T(8,128)S(1)}, f32[3,1,4,8,128]{4,3,2,1,0:T(8,128)}, u32[]{:S(2)}) copy-start(f32[3,1,4,8,128]{4,3,2,1,0:T(8,128)} %velocity.1) | copy-start | bytes 147460
  3.7 0.7 %copy-start.4 = (f32[1,4,8,128]{3,2,1,0:T(8,128)S(1)}, f32[1,4,8,128]{3,2,1,0:T(8,128)}, u32[]{:S(2)}) copy-start(f32[1,4,8,128]{3,2,1,0:T(8,128)} %density.1) | copy-start | bytes 49156
  4.4 0.7 %copy-start.5 = (f32[1,4,8,128]{3,2,1,0:T(8,128)S(1)}, f32[1,4,8,128]{3,2,1,0:T(8,128)}, u32[]{:S(2)}) copy-start(f32[1,4,8,128]{3,2,1,0:T(8,128)} %energy.1) | copy-start | bytes 49156
  5.1 0.7 %copy-start.6 = (f32[1,4,8,128]{3,2,1,0:T(8,128)S(1)}, f32[1,4,8,128]{3,2,1,0:T(8,128)}, u32[]{:S(2)}) copy-start(f32[1,4,8,128]{3,2,1,0:T(8,128)} %mix.1) | copy-start | bytes 49156
  5.8 0.7 %copy-start.7 = (s32[1,4,8,128]{3,2,1,0:T(8,128)S(1)}, s32[1,4,8,128]{3,2,1,0:T(8,128)}, u32[]{:S(2)}) copy-start(s32[1,4,8,128]{3,2,1,0:T(8,128)} %substeps.1) | copy-start | bytes 49156
  7.8 17.0 %collective-permute-start = (f32[640,128]{1,0:T(8,128)S(1)}, f32[640,128]{1,0:T(8,128)S(1)}, u32[]{:S(2)}, u32[]{:S(2)}) collective-permute-start(f32[640,128]{1,0:T(8,128)S(1)} %get-tuple-element.25), channel_id=1, source_target_pairs={{0,1},{1,2},{2,3},{3,4},{4,5},{5,6},{6,7},{7,8},{8,9},{9,10},{10,1... | collective-permute-start | bytes 983048 | tf_op jit(solution)/shard_map/ppermute | solution.py:361
  11.3 14.3 %collective-permute-start.1 = (f32[640,128]{1,0:T(8,128)S(1)}, f32[640,128]{1,0:T(8,128)S(1)}, u32[]{:S(2)}, u32[]{:S(2)}) collective-permute-start(f32[640,128]{1,0:T(8,128)S(1)} %get-tuple-element.26), channel_id=1, source_target_pairs={{1,0},{2,1},{3,2},{4,3},{5,4},{6,5},{7,6},{8,7},{9,8},{10,9},{11,1... | collective-permute-start | bytes 983048 | tf_op jit(solution)/shard_map/ppermute | solution.py:361
  27.6 15.5 %collective-permute-start.5 = (f32[2,10,16,128]{3,2,1,0:T(8,128)S(1)}, f32[2,10,16,128]{3,2,1,0:T(8,128)S(1)}, u32[]{:S(2)}, u32[]{:S(2)}) collective-permute-start(f32[2,10,16,128]{3,2,1,0:T(8,128)S(1)} %get-tuple-element.33), channel_id=1, source_target_pairs={{0,64},{64,0},{128,192},{192,128},{1,65},{65,1},{129,193},{193,129... | collective-permute-start | bytes 491528 | tf_op jit(solution)/shard_map/ppermute | solution.py:361
  30.1 1.0 %copy-start.2 = (f32[2,4,3,1,4,8,128]{6,5,4,3,2,1,0:T(8,128)S(1)}, f32[2,4,3,1,4,8,128]{6,5,4,3,2,1,0:T(8,128)}, u32[]{:S(2)}) copy-start(f32[2,4,3,1,4,8,128]{6,5,4,3,2,1,0:T(8,128)} %param.17) | copy-start | bytes 1179652
  31.2 0.7 copy-start.8
  31.8 0.7 copy-start.9
  43.1 2.5 %collective-permute-start.2 = (f32[2,152,128]{2,1,0:T(8,128)S(1)}, f32[2,152,128]{2,1,0:T(8,128)S(1)}, u32[]{:S(2)}, u32[]{:S(2)}) collective-permute-start(f32[2,152,128]{2,1,0:T(8,128)S(1)} %get-tuple-element.31), channel_id=1, source_target_pairs={{0,64},{64,0},{128,192},{192,128},{1,65},{65,1},{129,193},{193,129... | collective-permute-start | bytes 466952 | tf_op jit(solution)/shard_map/ppermute | solution.py:361
  43.2 6.9 %collective-permute-start.6 = (f32[2,10,16,128]{3,2,1,0:T(8,128)S(1)}, f32[2,10,16,128]{3,2,1,0:T(8,128)S(1)}, u32[]{:S(2)}, u32[]{:S(2)}) collective-permute-start(f32[2,10,16,128]{3,2,1,0:T(8,128)S(1)} %add.14), channel_id=1, source_target_pairs={{0,128},{64,192},{128,0},{192,64},{1,129},{65,193},{129,1},{193,65... | collective-permute-start | bytes 491528 | tf_op jit(solution)/shard_map/ppermute | solution.py:361
  45.6 7.8 %collective-permute-start.3 = (f32[2,152,128]{2,1,0:T(8,128)S(1)}, f32[2,152,128]{2,1,0:T(8,128)S(1)}, u32[]{:S(2)}, u32[]{:S(2)}) collective-permute-start(f32[2,152,128]{2,1,0:T(8,128)S(1)} %add.12), channel_id=1, source_target_pairs={{0,128},{64,192},{128,0},{192,64},{1,129},{65,193},{129,1},{193,65... | collective-permute-start | bytes 466952 | tf_op jit(solution)/shard_map/ppermute | solution.py:361
  50.1 4.8 %collective-permute-start.7 = (f32[2,10,16,128]{3,2,1,0:T(8,128)S(1)}, f32[2,10,16,128]{3,2,1,0:T(8,128)S(1)}, u32[]{:S(2)}, u32[]{:S(2)}) collective-permute-start(f32[2,10,16,128]{3,2,1,0:T(8,128)S(1)} %add.15.sum_mine), channel_id=1, source_target_pairs={{0,64},{64,0},{128,192},{192,128},{1,65},{65,1},{129,193},{193,129... | collective-permute-start | bytes 491528 | tf_op jit(solution)/shard_map/ppermute | solution.py:361
  53.5 12.4 %collective-permute-start.4 = (f32[2,152,128]{2,1,0:T(8,128)S(1)}, f32[2,152,128]{2,1,0:T(8,128)S(1)}, u32[]{:S(2)}, u32[]{:S(2)}) collective-permute-start(f32[2,152,128]{2,1,0:T(8,128)S(1)} %add.13.sum_mine), channel_id=1, source_target_pairs={{0,64},{64,0},{128,192},{192,128},{1,65},{65,1},{129,193},{193,129... | collective-permute-start | bytes 466952 | tf_op jit(solution)/shard_map/ppermute | solution.py:361

commit v3 on v2

v3 whole, which is shorter than its diff:
```python
import math

import jax
import jax.numpy as jnp
from jax import lax
from jax.experimental import pallas as pl
from jax.experimental.pallas import tpu as pltpu
from jax.sharding import PartitionSpec as P

FIELDS = 4
SPECIES = 16
ALL_FIELDS = 16
REACT = 96
SUBS = 4
CZ, CY, NX = 4, 8, 128

time_step = 0.1
viscosity = 0.4
diffusivity = 0.3
relaxation = 2.0
noise_half = 0.5 * math.sqrt(2.0 * 0.3 * 0.1)
speed_half = 0.5 * time_step
spread = time_step * diffusivity
f32 = jnp.float32
bf16 = jnp.bfloat16

INNER, EDGES = CY - 2, 4
BUNDLE_ROWS = 2048 + 768 + 256
WEIGHTS = (256, 3 * REACT)
SPECIES_ROWS = 2 * FIELDS * CZ * SPECIES
FLOW_ROWS = 2 * CZ * 8
MESSAGE_ROWS = SPECIES_ROWS + FLOW_ROWS + CZ * 16


def lanes(shape):
    return lax.broadcasted_iota(jnp.int32, shape, 1)


def shift_x(value, lane):
    ahead = jnp.where(lane == NX - 1, 0.0, pltpu.roll(value, NX - 1, 1))
    behind = jnp.where(lane == 0, 0.0, pltpu.roll(value, 1, 1))
    return ahead, behind


def stencil(column, above, below, z, lane):
    zero = jnp.zeros_like(column[z])
    up = column[z + 1] if z + 1 < CZ else zero
    down = column[z - 1] if z > 0 else zero
    ahead, behind = shift_x(column[z], lane)
    total = (up + down) + (above[z] + below[z]) + (ahead + behind)
    return total, (up - down, above[z] - below[z], ahead - behind)


def start(copies, sems, first):
    started = [pltpu.make_async_copy(source, target, sems.at[first + n]) for n, (source, target) in enumerate(copies)]
    for one in started:
        one.start()
    return started


def flow_tiles(parts, flow):
    for z in range(CZ):
        rows = [part[z] for part in parts] + [jnp.zeros((CY, NX), f32)]
        rows[5] = time_step * rows[5]
        for v in range(8):
            flow[pl.ds(z * 8 + v, CY, stride=8 * CZ), :] = rows[v]


def noise_tile(wiener, first, step, y, z):
    rows = wiener[pl.ds(first + 384 * step + z * 8 + y, 12, stride=32), :]
    return jnp.concatenate([rows, jnp.zeros((4, NX), f32)], 0)


def pack(
    species_far, density_far, velocity_far, energy_far, wiener_far, mix_far, substeps_far,
    low, high, bundle,
    species, density, velocity, energy, wiener, mix, substeps, flow, sems,
):
    inputs = start([(species_far, species), (density_far, density), (velocity_far, velocity), (energy_far, energy),
                    (wiener_far, wiener), (mix_far, mix), (substeps_far, substeps)], sems, 0)
    for one in inputs:
        one.wait()
    passed = start([(species, bundle.at[0:2048]), (wiener, bundle.at[2048:2816])], sems, 7)
    parts = [density[0], velocity[0, 0], velocity[1, 0], velocity[2, 0], energy[0], mix[0], substeps[0].astype(f32)]
    flow_tiles(parts, flow)
    passed += start([(flow, bundle.at[2816:BUNDLE_ROWS])], sems, 9)
    for out, first, edge in ((low, 0, 0), (high, CY - 2, CY - 1)):
        for n in range(2):
            y = first + n
            for f in range(FIELDS):
                for z in range(CZ):
                    row = ((n * FIELDS + f) * CZ + z) * SPECIES
                    out[row : row + SPECIES] = species[pl.ds(f * 512 + z * 8 + y, SPECIES, stride=32), :]
            for z in range(CZ):
                row = SPECIES_ROWS + (n * CZ + z) * 8
                out[row : row + 8] = flow[(y * CZ + z) * 8 : (y * CZ + z + 1) * 8]
        for z in range(CZ):
            row = SPECIES_ROWS + FLOW_ROWS + z * 16
            out[row : row + 16] = noise_tile(wiener, 0, 0, edge, z)
    for one in passed:
        one.wait()


def flow_step(source, y, lane, keep):
    column = [source[y, z] for z in range(CZ)]
    above = [source[y + 1, z] for z in range(CZ)]
    below = [source[y - 1, z] for z in range(CZ)]
    row = lax.broadcasted_iota(jnp.int32, (8, NX), 0)
    results = []
    for z in range(CZ):
        total, change = stencil(column, above, below, z, lane)
        centre = column[z]
        moved = (
            source[y, z, 1:2] * change[0] + source[y, z, 2:3] * change[1] + source[y, z, 3:4] * change[2]
        )
        new = centre + time_step * viscosity * (total - 6.0 * centre) - speed_half * moved
        if keep is not None:
            new = new * keep
        results.append(jnp.where(row < 5, new, centre))
    return results


def transport(get, y, noise, noise_y, speeds, speeds_y, lane, emit):
    slow = [[speed_half * speeds[speeds_y, z, 1 + d : 2 + d] for d in range(3)] for z in range(CZ)]
    for f in range(FIELDS):
        column = [get(y, f, z) for z in range(CZ)]
        above = [get(y + 1, f, z) for z in range(CZ)]
        below = [get(y - 1, f, z) for z in range(CZ)]
        for z in range(CZ):
            total, change = stencil(column, above, below, z, lane)
            value = (1.0 - 6.0 * spread) * column[z] + spread * total
            for d in range(3):
                weight = noise_half * noise[noise_y, z, 3 * f + d : 3 * f + d + 1] - slow[z][d]
                value = value + weight * change[d]
            emit(f, z, value)


def store_halves(total, mine, other):
    core = lax.rem(lax.axis_index("field"), 2)
    for i in range(CZ // 2):
        mine[i] = total[core * 2 + i]
        other[i] = total[(1 - core) * 2 + i]


def join_halves(mine, other, total):
    core = lax.rem(lax.axis_index("field"), 2)
    for i in range(CZ // 2):
        total[core * 2 + i] = mine[i]
        total[(1 - core) * 2 + i] = other[i]


def first_edge(
    own, flow, noise_first, inner_flow, inner_sum, low_halo, high_halo,
    carried, flow_one, mine, other,
    wide, wide_flow, wide_noise, total,
):
    tile = lax.axis_index("tile")
    last = lax.axis_size("tile") - 1
    lane, lane_flow = lanes((SPECIES, NX)), lanes((8, NX))
    wide[2:4] = own[0:2]
    wide[4:6] = own[CY - 2 : CY]
    wide_flow[2:4] = flow[0:2]
    wide_flow[4:6] = flow[CY - 2 : CY]
    wide_noise[1] = noise_first[0]
    wide_noise[2] = noise_first[CY - 1]
    for halo, at, edge in ((low_halo, 0, 0), (high_halo, 6, 3)):
        wide[at : at + 2] = halo[0:SPECIES_ROWS].reshape(2, FIELDS, CZ, SPECIES, NX)
        wide_flow[at : at + 2] = halo[SPECIES_ROWS : SPECIES_ROWS + FLOW_ROWS].reshape(2, CZ, 8, NX)
        wide_noise[edge] = halo[SPECIES_ROWS + FLOW_ROWS :].reshape(CZ, 16, NX)
    flow_one[2:CY] = inner_flow[...]
    for z in range(CZ):
        total[z, 0:INNER] = inner_sum[z]

    def layer(e, _):
        outside = ((e == 0) & (tile == 0)) | ((e == 3) & (tile == last))
        keep = jnp.where(outside, 0.0, 1.0).astype(f32)
        high = e // 2
        centre, y = e + 1 + 2 * high, e + INNER * high
        for z, new in enumerate(flow_step(wide_flow, centre, lane_flow, keep)):
            flow_one[y, z] = new
        sums = [None] * CZ

        def emit(f, z, value):
            value = value * keep
            carried[e, f, z] = value
            sums[z] = value if sums[z] is None else sums[z] + value

        transport(lambda at, f, z: wide[at, f, z], centre, wide_noise, e, flow_one, y, lane, emit)
        for z in range(CZ):
            total[z, INNER + e] = sums[z]
        return 0

    lax.fori_loop(0, EDGES, layer, 0)
    store_halves(total, mine, other)


def prepare(consts, weights):
    stoich = consts[240:256, 0:REACT]
    for j in range(SPECIES):
        product = consts[224 + j : 225 + j, 0:REACT] * stoich
        high = product.astype(bf16)
        low = (product - high.astype(f32)).astype(bf16)
        weights[SPECIES * j : SPECIES * (j + 1)] = jnp.concatenate([high, low, high], 1)


def form(consts, flow, layers, weights, rates, out):
    for m, (y, _) in enumerate(layers):
        for z in range(CZ):
            level = flow[y, z, 4:5] - 1.0
            length = time_step / jnp.maximum(flow[y, z, 6:7], 1.0)
            rate = consts[0:REACT] * jnp.exp(consts[REACT : 2 * REACT] * level) * length
            high = rate.astype(bf16)
            low = (rate - high.astype(f32)).astype(bf16)
            at = slice(NX * (CZ * m + z), NX * (CZ * m + z + 1))
            rates[0:REACT, at] = high
            rates[REACT : 2 * REACT, at] = high
            rates[2 * REACT : 3 * REACT, at] = low
    product = jnp.dot(weights[...], rates[...], preferred_element_type=f32)
    for m, (_, n) in enumerate(layers):
        out[n] = product[:, CZ * NX * m : CZ * NX * (m + 1)]


def react(matrices, y, z, flow, flow_y, values, held):
    count = jnp.broadcast_to(flow[flow_y, z, 6:7], (SPECIES, NX))
    blocks = [matrices[y, SPECIES * j : SPECIES * (j + 1), NX * z : NX * (z + 1)] for j in range(SPECIES)]
    for k in range(SUBS):
        for n, value in enumerate(values):
            held[z, n] = value
        changes = [None] * len(values)
        for j in range(SPECIES):
            for n in range(len(values)):
                part = blocks[j] * held[z, n, j : j + 1]
                changes[n] = part if changes[n] is None else changes[n] + part
        values = [value + jnp.where(count > float(k), change, 0.0) for value, change in zip(values, changes)]
    return values


def react_own(flow, flow_y, matrices, y, carried, held, reacted):
    for z in range(CZ):
        values = react(matrices, y, z, flow, flow_y, [carried[y, f, z] for f in range(FIELDS)], held)
        own_share = 1.0 - flow[flow_y, z, 5:6]
        for f in range(FIELDS):
            reacted[y, f, z] = own_share * values[f]


def inner(
    bundle, consts,
    own, flow, noise_first, noise_second, noise_sum, flow_one, total, reacted, matrices, weights,
    carried, rates, held,
):
    lane, lane_flow = lanes((SPECIES, NX)), lanes((8, NX))
    prepare(consts, weights)
    flow[...] = bundle[2816:BUNDLE_ROWS].reshape(CY, CZ, 8, NX)

    def gather(y, _):
        for z in range(CZ):
            for f in range(FIELDS):
                own[y, f, z] = bundle[pl.ds(f * 512 + z * 8 + y, SPECIES, stride=32), :]
            noise_first[y, z] = noise_tile(bundle, 2048, 0, y, z)
            noise_second[y, z] = noise_tile(bundle, 2048, 1, y, z)
        return 0

    lax.fori_loop(0, CY, gather, 0)
    for z in range(CZ):
        for d in range(3):
            rows = [2048 + 384 + (f * 3 + d) * 32 + z * 8 for f in range(FIELDS)]
            noise_sum[z, 8 * d : 8 * d + 8] = (
                (bundle[rows[0] : rows[0] + 8] + bundle[rows[1] : rows[1] + 8])
                + (bundle[rows[2] : rows[2] + 8] + bundle[rows[3] : rows[3] + 8])
            )

    def layer(y, _):
        for z, new in enumerate(flow_step(flow, y + 1, lane_flow, None)):
            flow_one[y, z] = new
        sums = [None] * CZ

        def emit(f, z, value):
            carried[y, f, z] = value
            sums[z] = value if sums[z] is None else sums[z] + value

        transport(lambda at, f, z: own[at, f, z], y + 1, noise_first, y + 1, flow_one, y, lane, emit)
        for z in range(CZ):
            total[z, y] = sums[z]
        return 0

    lax.fori_loop(0, INNER, layer, 0)

    def form_group(g, _):
        form(consts, flow_one, [(3 * g + m, 3 * g + m) for m in range(3)], weights, rates, matrices)
        return 0

    lax.fori_loop(0, INNER // 3, form_group, 0)

    def react_layer(y, _):
        react_own(flow_one, y, matrices, y, carried, held, reacted)
        return 0

    lax.fori_loop(0, INNER, react_layer, 0)


def react_edge(
    carried, flow_one, inner_reacted, noise_second, noise_sum, weights, consts,
    matrices, partial, total,
    rates, held, edge_reacted, reacted, flow_two,
):
    lane, lane_flow = lanes((SPECIES, NX)), lanes((8, NX))

    def react_layer(e, _):
        react_own(flow_one, e + INNER * (e // 2), matrices, e, carried, held, edge_reacted)
        return 0

    form(consts, flow_one, [(0, 0), (1, 1), (CY, 2), (CY + 1, 3)], weights, rates, matrices)

    lax.fori_loop(0, EDGES, react_layer, 0)
    reacted[2:CY] = inner_reacted[...]
    reacted[0:2] = edge_reacted[0:2]
    reacted[CY : CY + 2] = edge_reacted[2:4]

    def layer(y, _):
        for z, new in enumerate(flow_step(flow_one, y + 1, lane_flow, None)):
            flow_two[y, z] = new
        sums = [None] * CZ

        def emit(f, z, value):
            partial[y, f, z] = value
            sums[z] = value if sums[z] is None else sums[z] + value

        transport(lambda at, f, z: reacted[at, f, z], y + 1, noise_second, y, flow_two, y, lane, emit)
        for z in range(CZ):
            total[z, pl.ds(y * SPECIES, SPECIES)] = sums[z]
        return 0

    lax.fori_loop(0, CY, layer, 0)
    for z in range(CZ):
        total[z, 128:152] = noise_sum[z]


def add_sources(flow_tile, total, after, heat, molar):
    density = jnp.sum(molar * after, 0, keepdims=True) / ALL_FIELDS
    released = jnp.sum(heat * (after - total), 0, keepdims=True) / ALL_FIELDS
    row = lax.broadcasted_iota(jnp.int32, (8, NX), 0)
    with_density = flow_tile + time_step * relaxation * (density - flow_tile)
    return jnp.where(row == 0, with_density, jnp.where(row == 4, flow_tile + released, flow_tile))


def second_step(
    sum_mine, sum_other, flow_one, inner_matrices, edge_matrices, partial, noise_second, weights, consts,
    matrices_two, own_part, shared, flow_two,
    total, flow_mid, rates, held,
):
    join_halves(sum_mine, sum_other, total)
    lane, lane_flow = lanes((SPECIES, NX)), lanes((8, NX))

    def mean_layer(matrices, n, at, y):
        for z in range(CZ):
            before = total[z, at]
            (after,) = react(matrices, n, z, flow_one, y, [before], held)
            shared[y, z] = (flow_one[y, z, 5:6] / ALL_FIELDS) * after
            flow_mid[y, z] = add_sources(
                flow_one[y, z], before, after, consts[192:208], consts[208:224]
            )

    def inner_layer(n, _):
        mean_layer(inner_matrices, n, n, n + 2)
        return 0

    def edge_layer(e, _):
        mean_layer(edge_matrices, e, INNER + e, e + INNER * (e // 2))
        return 0

    lax.fori_loop(0, INNER, inner_layer, 0)
    lax.fori_loop(0, EDGES, edge_layer, 0)

    def form_group(g, _):
        for m in range(4):
            for z, new in enumerate(flow_step(flow_mid, 4 * g + m + 1, lane_flow, None)):
                flow_two[4 * g + m, z] = new
        form(consts, flow_two, [(4 * g + m, 4 * g + m) for m in range(4)], weights, rates, matrices_two)
        return 0

    lax.fori_loop(0, CY // 4, form_group, 0)

    def layer(y, _):
        column = [shared[y + 1, z] for z in range(CZ)]
        above = [shared[y + 2, z] for z in range(CZ)]
        below = [shared[y, z] for z in range(CZ)]
        for z in range(CZ):
            neighbour_sum, change = stencil(column, above, below, z, lane)
            base = (1.0 - 6.0 * spread) * column[z] + spread * neighbour_sum
            slow = [speed_half * flow_two[y, z, 1 + d : 2 + d] for d in range(3)]
            values = []
            for f in range(FIELDS):
                value = partial[y, f, z] + base
                for d in range(3):
                    weight = noise_half * noise_second[y, z, 3 * f + d : 3 * f + d + 1] - slow[d]
                    value = value + weight * change[d]
                values.append(value)
            values = react(matrices_two, y, z, flow_two, y, values, held)
            own_share = 1.0 - flow_two[y, z, 5:6]
            for f in range(FIELDS):
                own_part[y, f, z] = own_share * values[f]
        return 0

    lax.fori_loop(0, CY, layer, 0)


def finish(
    sum_here, sum_there, shared, flow_two, matrices_two, own_part, consts,
    flow_out, species_out,
    total, held,
):
    total[...] = sum_here[...] + sum_there[...]
    lane = lanes((SPECIES, NX))

    def layer(y, _):
        column = [shared[y + 1, z] for z in range(CZ)]
        above = [shared[y + 2, z] for z in range(CZ)]
        below = [shared[y, z] for z in range(CZ)]
        for z in range(CZ):
            neighbour_sum, change = stencil(column, above, below, z, lane)
            before = total[z, pl.ds(y * SPECIES, SPECIES)] + ALL_FIELDS * (
                (1.0 - 6.0 * spread) * column[z] + spread * neighbour_sum
            )
            for d in range(3):
                weight = (
                    noise_half * total[z, pl.ds(128 + 8 * d + y, 1)]
                    - ALL_FIELDS * speed_half * flow_two[y, z, 1 + d : 2 + d]
                )
                before = before + weight * change[d]
            (after,) = react(matrices_two, y, z, flow_two, y, [before], held)
            tile = add_sources(flow_two[y, z], before, after, consts[192:208], consts[208:224])
            for v in range(5):
                flow_out[v, z, pl.ds(y, 1)] = tile[v : v + 1]
            mean = (flow_two[y, z, 5:6] / ALL_FIELDS) * after
            for f in range(FIELDS):
                species_out[pl.ds(f * 512 + z * 8 + y, SPECIES, stride=32), :] = own_part[y, f, z] + mean
        return 0

    lax.fori_loop(0, CY, layer, 0)


def call(kernel, name, outs, scratch, micros, *operands, far=0, far_outs=0, semaphores=0, weights_out=False, room=24):
    shapes = [jax.ShapeDtypeStruct(shape, f32) for shape in outs]
    if weights_out:
        shapes.append(jax.ShapeDtypeStruct(WEIGHTS, bf16))
    moved = sum(4 * math.prod(shape) for shape in outs) + sum(x.size * 4 for x in operands)
    places = [pl.BlockSpec(memory_space=pltpu.HBM if n < far else pltpu.VMEM) for n in range(len(operands))]
    out_places = [pl.BlockSpec(memory_space=pltpu.VMEM)] * (len(shapes) - far_outs)
    out_places += [pl.BlockSpec(memory_space=pltpu.HBM)] * far_outs
    semaphores = [pltpu.SemaphoreType.DMA((semaphores,))] if semaphores else []
    return pl.pallas_call(
        kernel,
        out_shape=tuple(shapes),
        in_specs=places,
        out_specs=tuple(out_places),
        scratch_shapes=[pltpu.VMEM(*entry) for entry in scratch] + semaphores,
        cost_estimate=pl.CostEstimate(flops=micros * 10**9, bytes_accessed=moved, transcendentals=0),
        compiler_params=pltpu.CompilerParams(vmem_limit_bytes=room << 20),
        name=name,
    )(*operands)


CORE_PAIRS = [(i, i ^ 1) for i in range(4)]
CHIP_PAIRS = [(i, i ^ 2) for i in range(4)]


def on_device(
    density, velocity, energy, species, wiener, substeps, mix_rate,
    reactants, stoich, kinetic_constants, excitation_sensitivity, heat, molar,
):
    tiles = lax.axis_size("tile")
    wide = CY + 2
    columns = jnp.concatenate([kinetic_constants, excitation_sensitivity, heat, molar])
    tables = jnp.concatenate([reactants.T, stoich], 0)
    consts = jnp.concatenate(
        [jnp.broadcast_to(columns[:, None], (2 * REACT + 32, NX)), jnp.pad(tables, ((0, 0), (0, NX - REACT)))], 0
    )
    grid = (FIELDS, CZ, SPECIES, NX)
    flow_grid, noise_grid = (CZ, 8, NX), (CZ, 16, NX)
    block = (1, CZ, CY, NX)
    fields = (species.reshape(-1, NX), density, velocity, energy, wiener.reshape(-1, NX), mix_rate, substeps)

    copies = [((2048, NX), f32), (block, f32), ((3,) + block, f32), (block, f32), ((768, NX), f32),
              (block, f32), (block, jnp.int32)]

    rates = ((3 * REACT, 4 * CZ * NX), bf16)
    held = ((CZ, FIELDS, SPECIES, NX), f32)
    low, high, bundle = call(
        pack, "pack", [(MESSAGE_ROWS, NX)] * 2 + [(BUNDLE_ROWS, NX)], copies + [((256, NX), f32)],
        2, *fields, far=7, far_outs=1, semaphores=10, room=64,
    )
    low_halo = lax.ppermute(high, "tile", [(i, i + 1) for i in range(tiles - 1)])
    high_halo = lax.ppermute(low, "tile", [(i + 1, i) for i in range(tiles - 1)])
    own, flow, noise_first, noise_second, noise_sum, inner_flow, inner_total, inner_reacted, inner_matrices, weights = call(
        inner, "inner",
        [(CY,) + grid, (CY,) + flow_grid, (CY,) + noise_grid, (CY,) + noise_grid, (CZ, 24, NX),
         (INNER,) + flow_grid, (CZ, INNER, SPECIES, NX), (INNER,) + grid, (INNER, 256, CZ * NX)],
        [((INNER,) + grid, f32), ((3 * REACT, 3 * CZ * NX), bf16), held],
        8, bundle, consts, weights_out=True,
    )
    carried, flow_one, mine, other = call(
        first_edge, "first_edge",
        [(EDGES,) + grid, (wide,) + flow_grid] + [(2, wide, SPECIES, NX)] * 2,
        [((8,) + grid, f32), ((8,) + flow_grid, f32), ((EDGES,) + noise_grid, f32), ((CZ, wide, SPECIES, NX), f32)],
        2, own, flow, noise_first, inner_flow, inner_total, low_halo, high_halo,
    )
    mine = mine + lax.ppermute(other, "field", CORE_PAIRS)
    mine, carried = lax.optimization_barrier((mine, carried))
    sum_mine = mine + lax.ppermute(mine, "field", CHIP_PAIRS)
    sum_other = lax.ppermute(sum_mine, "field", CORE_PAIRS)
    edge_matrices, partial, second = call(
        react_edge, "react_edge",
        [(EDGES, 256, CZ * NX), (CY,) + grid, (CZ, 152, NX)],
        [rates, held, ((EDGES,) + grid, f32), ((wide,) + grid, f32), ((CY,) + flow_grid, f32)],
        6, carried, flow_one, inner_reacted, noise_second, noise_sum, weights, consts,
    )
    second = second + lax.ppermute(second, "field", CORE_PAIRS)
    second_far = lax.ppermute(second, "field", CHIP_PAIRS)
    matrices_two, own_part, shared, flow_two = call(
        second_step, "second_step",
        [(CY, 256, CZ * NX), (CY,) + grid, (wide, CZ, SPECIES, NX), (CY,) + flow_grid],
        [((CZ, wide, SPECIES, NX), f32), ((wide,) + flow_grid, f32), rates, held],
        10, sum_mine, sum_other, flow_one, inner_matrices, edge_matrices, partial, noise_second, weights, consts,
    )
    flow_out, species_out = call(
        finish, "finish",
        [(5, CZ, CY, NX), (FIELDS * SPECIES * CZ * CY, NX)],
        [((CZ, 152, NX), f32), held],
        4, second, second_far, shared, flow_two, matrices_two, own_part, consts,
    )
    return flow_out[:, None], species_out.reshape(species.shape)


def solution(mesh):
    placed = (
        P("tile", None, None, None),
        P(None, "tile", None, None, None),
        P("tile", None, None, None),
        P("field", None, "tile", None, None, None),
        P(None, "field", None, "tile", None, None, None),
        P("tile", None, None, None),
        P("tile", None, None, None),
        P(),
        P(),
        P(),
        P(),
        P(),
        P(),
    )
    return jax.shard_map(
        on_device,
        mesh=mesh,
        in_specs=placed,
        out_specs=(P(None, "tile", None, None, None), P("field", None, "tile", None, None, None)),
        check_vma=False,
    )
```

time: 71.4 us -> 55 us (0.77)
  waiting for transfers between devices: 10.4 us -> 1.87 us
  local copies, waits for them, and re-layouts: 8.35 us -> 1.41 us
  starting transfers between devices: 20.7 us -> 17.6 us
  Pallas kernels: 29.4 us -> 31.4 us
  other arithmetic: 0.86 us -> 1.67 us
    ppermute x8 -> x7, waiting for transfers between devices: 10.4 us -> 1.87 us  [the longest x1 1.03 us: on_device(): mine = mine + lax.ppermute(other, 'field', CORE_PAIRS)]
    unnamed x20 -> x2, local copies, waits for them, and re-layouts: 8.27 us -> 1.41 us
    ppermute x8 -> x7, starting transfers between devices: 20.7 us -> 17.6 us  [the longest x1 7.94 us: on_device(): lax.ppermute(low, 'tile', [(i + 1, i) for i in range(tiles - 1)])]
    pallas_call x5 -> x6, Pallas kernels: 29.4 us -> 31.4 us  [call(): pl.pallas_call(kernel, out_shape=tuple(shapes), in_specs=places, out_spec...]
    concatenate x0 -> x2, other arithmetic: none -> 0.81 us  [the longest x1 0.72 us: on_device(): tables = jnp.concatenate([reactants.T, stoich], 0)]
  transfers between devices with their start and end apart: 8 -> 7, of which waited for: 4 -> 2; matrix products, arithmetic and copies ran while one was open for 1% -> 3% of each run, Pallas kernels for 30% -> 41%
where the time goes in v3:
time: 55 us; the launch traced here: 54.7 us
  Pallas kernels  31.4 us (57%)
  starting transfers between devices  17.6 us (32%)
  waiting for transfers between devices  1.87 us (3%)
  other arithmetic  1.67 us (3%)
  local copies, waits for them, and re-layouts  1.41 us (3%)
  between operations  0.74 us (1%)
    pallas_call x6, Pallas kernels, call(): pl.pallas_call(kernel, out_shape=tuple(shapes), in_specs=places, out_spec...  31.4 us
    ppermute x1, starting transfers between devices, on_device(): lax.ppermute(low, 'tile', [(i + 1, i) for i in range(tiles - 1)])  7.94 us
    ppermute x1, starting transfers between devices, on_device(): lax.ppermute(high, 'tile', [(i, i + 1) for i in range(tiles - 1)])  3.55 us
    ppermute x1, starting transfers between devices, on_device(): sum_mine = mine + lax.ppermute(mine, 'field', CHIP_PAIRS)  2.4 us
    ppermute x1, starting transfers between devices, on_device(): second_far = lax.ppermute(second, 'field', CHIP_PAIRS)  1.57 us
    unnamed x2, local copies, waits for them, and re-layouts  1.41 us
  transfers between devices with their start and end apart: 7, of which 2 were waited for; matrix products, arithmetic and copies ran while one was open for 3% of the time, Pallas kernels for 41%

profile of v3, /device:TPU:9, one launch (start us, length us, event | category | flops | bytes accessed | tf_op | source)
XLA Modules:
  0.0 54.7 jit_solution(4072347732883536636)
XLA Ops:
  0.6 3.4 %pack.1 = (f32[640,128]{1,0:T(8,128)}, f32[640,128]{1,0:T(8,128)}, f32[3072,128]{1,0:T(8,128)}) custom-call(f32[2048,128]{1,0:T(8,128)} %bitcast.10, f32[1,4,8,128]{3,2,1,0:T(8,128)} %density_far.1, f32[3,1,4,8,128]{4,3,2,1,0:T(8,128)} %velocity_far.1, f32[1,4,8,128]{3,2,1,0:T(8,128)} %energy_far.1, f32[768,128]{1,0:T(8,128)} %bitcast.11, ...), custom_call_target="tpu_custom_call" | custom-call | flops 2000000000 | bytes 3784704 | tf_op jit(solution)/shard_map/pack/pallas_call | solution.py:451
  4.1 3.5 %collective-permute-start = (f32[640,128]{1,0:T(8,128)}, f32[640,128]{1,0:T(8,128)S(1)}, u32[]{:S(2)}, u32[]{:S(2)}) collective-permute-start(f32[640,128]{1,0:T(8,128)} %get-tuple-element.36), channel_id=1, source_target_pairs={{0,1},{1,2},{2,3},{3,4},{4,5},{5,6},{6,7},{7,8},{8,9},{9,10},{10,1... | collective-permute-start | bytes 983048 | tf_op jit(solution)/shard_map/ppermute | solution.py:492
  7.6 7.9 %collective-permute-start.1 = (f32[640,128]{1,0:T(8,128)}, f32[640,128]{1,0:T(8,128)S(1)}, u32[]{:S(2)}, u32[]{:S(2)}) collective-permute-start(f32[640,128]{1,0:T(8,128)} %get-tuple-element.37), channel_id=1, source_target_pairs={{1,0},{2,1},{3,2},{4,3},{5,4},{6,5},{7,6},{8,7},{9,8},{10,9},{11,1... | collective-permute-start | bytes 983048 | tf_op jit(solution)/shard_map/ppermute | solution.py:493
  15.6 0.7 %select_maximum_fusion = f32[32,128]{1,0:T(8,128)S(1)} fusion(f32[16,96]{1,0:T(8,128)} %param.21, f32[16,96]{1,0:T(8,128)} %bitcast.9), kind=kLoop, calls=%fused_computation.1 | loop fusion | flops 16384 | bytes 28672 | tf_op jit(solution)/shard_map/concatenate | solution.py:474
  16.3 0.8 %pad_maximum_fusion.1 = f32[256]{0:T(256)S(1)} fusion(f32[16]{0:T(128)} %param.25, f32[16]{0:T(128)} %param.24, f32[96]{0:T(128)} %param.23, f32[96]{0:T(128)} %param.22), kind=kLoop, calls=%fused_computation.3 | loop fusion | flops 768 | bytes 1920 | tf_op jit(solution)/shard_map/concatenate | solution.py:473
  17.1 0.1 pad_maximum_fusion.consts
  17.2 1.4 %copy-done = f32[3072,128]{1,0:T(8,128)S(1)} copy-done((f32[3072,128]{1,0:T(8,128)S(1)}, f32[3072,128]{1,0:T(8,128)}, u32[]{:S(2)}) %copy-start) | copy-done | bytes 1572888
  18.6 7.3 %inner.1 = (f32[8,4,4,16,128]{4,3,2,1,0:T(8,128)S(1)}, f32[8,4,8,128]{3,2,1,0:T(8,128)S(1)}, f32[8,4,16,128]{3,2,1,0:T(8,128)S(1)}, f32[8,4,16,128]{3,2,1,0:T(8,...) custom-call(f32[3072,128]{1,0:T(8,128)S(1)} %copy-done, ...), custom_call_target="tpu_custom_call" | custom-call | flops 8000000000 | bytes 7684096 | tf_op jit(solution)/shard_map/inner/pallas_call | solution.py:451
  25.9 0.0 collective-permute-done.low_halo
  26.0 0.0 collective-permute-done.1.high_halo
  26.0 0.9 %first_edge.1 = (f32[4,4,4,16,128]{4,3,2,1,0:T(8,128)S(1)}, f32[10,4,8,128]{3,2,1,0:T(8,128)S(1)}, f32[2,10,16,128]{3,2,1,0:T(8,128)S(1)}, f32[2,10,16,128]{3,2,1,0:T(8,128)S(1)}) custom-call(f32[8,4,4,16,128]{4,3,2,1,0:T(8,128)S(1)} %get-tuple-element.31.own, f32[8,4,8,128]{3,2,1,0:T(8,128)S(1)} %get-tuple-element.32.flow, ...), custom_call_target="tpu_custom_call" | custom-call | flops 2000000000 | bytes 3407872 | tf_op jit(solution)/shard_map/first_edge/pallas_call | solution.py:451
  26.9 1.0 %collective-permute-start.2 = (f32[2,10,16,128]{3,2,1,0:T(8,128)S(1)}, f32[2,10,16,128]{3,2,1,0:T(8,128)S(1)}, u32[]{:S(2)}, u32[]{:S(2)}) collective-permute-start(f32[2,10,16,128]{3,2,1,0:T(8,128)S(1)} %get-tuple-element.39), channel_id=1, source_target_pairs={{0,64},{64,0},{128,192},{192,128},{1,65},{65,1},{129,193},{193,129... | collective-permute-start | bytes 491528 | tf_op jit(solution)/shard_map/ppermute | solution.py:507
  27.9 1.0 %collective-permute-done.2 = f32[2,10,16,128]{3,2,1,0:T(8,128)S(1)} collective-permute-done((f32[2,10,16,128]{3,2,1,0:T(8,128)S(1)}, f32[2,10,16,128]{3,2,1,0:T(8,128)S(1)}, u32[]{:S(2)}, u32[]{:S(2)}) %collective-permute-start.2) | collective-permute-done | bytes 163872 | tf_op jit(solution)/shard_map/ppermute | solution.py:507
  28.9 2.4 %collective-permute-start.5 = (f32[2,10,16,128]{3,2,1,0:T(8,128)S(1)}, f32[2,10,16,128]{3,2,1,0:T(8,128)S(1)}, u32[]{:S(2)}, u32[]{:S(2)}) collective-permute-start(f32[2,10,16,128]{3,2,1,0:T(8,128)S(1)} %add.11), channel_id=1, source_target_pairs={{0,128},{64,192},{128,0},{192,64},{1,129},{65,193},{129,1},{193,65... | collective-permute-start | bytes 491528 | tf_op jit(solution)/shard_map/ppermute | solution.py:509
  31.3 4.8 %react_edge.1 = (f32[4,256,512]{2,1,0:T(8,128)S(1)}, f32[8,4,4,16,128]{4,3,2,1,0:T(8,128)S(1)}, f32[4,152,128]{2,1,0:T(8,128)S(1)}) custom-call(f32[4,4,4,16,128]{4,3,2,1,0:T(8,128)S(1)} %get-tuple-element.41.carried, f32[10,4,8,128]{3,2,1,0:T(8,128)S(1)} %get-tuple-element.42.flow_one, f32[6,4,4,16,128]{4,3,2,1,0:T(8,128)S(1)} %get-tuple-element.43.inner_reacted, ...), custom_call_target="tpu_custom_call" | custom-call | flops 6000000000 | bytes 5668864 | tf_op jit(solution)/shard_map/react_edge/pallas_call | solution.py:451
  36.1 0.7 %collective-permute-start.3 = (f32[4,152,128]{2,1,0:T(8,128)S(1)}, f32[4,152,128]{2,1,0:T(8,128)S(1)}, u32[]{:S(2)}, u32[]{:S(2)}) collective-permute-start(f32[4,152,128]{2,1,0:T(8,128)S(1)} %get-tuple-element.47), channel_id=1, source_target_pairs={{0,64},{64,0},{128,192},{192,128},{1,65},{65,1},{129,193},{193,129... | collective-permute-start | bytes 933896 | tf_op jit(solution)/shard_map/ppermute | solution.py:517
  36.9 0.0 collective-permute-done.5
  36.9 0.4 collective-permute-start.6
  37.3 0.8 %collective-permute-done.3 = f32[4,152,128]{2,1,0:T(8,128)S(1)} collective-permute-done((f32[4,152,128]{2,1,0:T(8,128)S(1)}, f32[4,152,128]{2,1,0:T(8,128)S(1)}, u32[]{:S(2)}, u32[]{:S(2)}) %collective-permute-start.3) | collective-permute-done | bytes 311328 | tf_op jit(solution)/shard_map/ppermute | solution.py:517
  38.1 1.6 %collective-permute-start.4 = (f32[4,152,128]{2,1,0:T(8,128)S(1)}, f32[4,152,128]{2,1,0:T(8,128)S(1)}, u32[]{:S(2)}, u32[]{:S(2)}) collective-permute-start(f32[4,152,128]{2,1,0:T(8,128)S(1)} %add.12.sum_here), channel_id=1, source_target_pairs={{0,128},{64,192},{128,0},{192,64},{1,129},{65,193},{129,1},{193,65... | collective-permute-start | bytes 933896 | tf_op jit(solution)/shard_map/ppermute | solution.py:518
  39.7 0.0 collective-permute-done.6.sum_other
  39.7 10.3 %second_step.1 = (f32[8,256,512]{2,1,0:T(8,128)S(1)}, f32[8,4,4,16,128]{4,3,2,1,0:T(8,128)S(1)}, f32[10,4,16,128]{3,2,1,0:T(8,128)S(1)}, f32[8,4,8,128]{3,2,1,0:T(8,128)S(1)}) custom-call(f32[2,10,16,128]{3,2,1,0:T(8,128)S(1)} %add.13.sum_mine, f32[2,10,16,128]{3,2,1,0:T(8,128)S(1)} %collective-permute-done.6.sum_other, ...), custom_call_target="tpu_custom_call" | custom-call | flops 10000000000 | bytes 13172736 | tf_op jit(solution)/shard_map/second_step/pallas_call | solution.py:451
  50.0 0.0 collective-permute-done.4.sum_there
  50.1 4.6 %finish.1 = (f32[5,4,8,128]{3,2,1,0:T(8,128)}, f32[2048,128]{1,0:T(8,128)}) custom-call(f32[4,152,128]{2,1,0:T(8,128)S(1)} %add.12.sum_here, f32[4,152,128]{2,1,0:T(8,128)S(1)} %collective-permute-done.4.sum_there, f32[10,4,16,128]{3,2,1,0:T(8,128)S(1)} %get-tuple-element.52.shared, f32[8,4,8,128]{3,2,1,0:T(8,128)S(1)} %get-tuple-element.53.flow_two, ...), custom_call_target="tpu_custom_call" | custom-call | flops 4000000000 | bytes 7585792 | tf_op jit(solution)/shard_map/finish/pallas_call | solution.py:451
  (4 shorter events, 0.1 us)
Async XLA Ops:
  4.1 21.9 %collective-permute-start = (f32[640,128]{1,0:T(8,128)}, f32[640,128]{1,0:T(8,128)S(1)}, u32[]{:S(2)}, u32[]{:S(2)}) collective-permute-start(f32[640,128]{1,0:T(8,128)} %get-tuple-element.36), channel_id=1, source_target_pairs={{0,1},{1,2},{2,3},{3,4},{4,5},{5,6},{6,7},{7,8},{8,9},{9,10},{10,1... | collective-permute-start | bytes 983048 | tf_op jit(solution)/shard_map/ppermute | solution.py:492
  7.6 18.3 %collective-permute-start.1 = (f32[640,128]{1,0:T(8,128)}, f32[640,128]{1,0:T(8,128)S(1)}, u32[]{:S(2)}, u32[]{:S(2)}) collective-permute-start(f32[640,128]{1,0:T(8,128)} %get-tuple-element.37), channel_id=1, source_target_pairs={{1,0},{2,1},{3,2},{4,3},{5,4},{6,5},{7,6},{8,7},{9,8},{10,9},{11,1... | collective-permute-start | bytes 983048 | tf_op jit(solution)/shard_map/ppermute | solution.py:493
  17.2 1.4 %copy-start = (f32[3072,128]{1,0:T(8,128)S(1)}, f32[3072,128]{1,0:T(8,128)}, u32[]{:S(2)}) copy-start(f32[3072,128]{1,0:T(8,128)} %get-tuple-element.30.bundle) | copy-start | bytes 4718596
  26.9 2.1 %collective-permute-start.2 = (f32[2,10,16,128]{3,2,1,0:T(8,128)S(1)}, f32[2,10,16,128]{3,2,1,0:T(8,128)S(1)}, u32[]{:S(2)}, u32[]{:S(2)}) collective-permute-start(f32[2,10,16,128]{3,2,1,0:T(8,128)S(1)} %get-tuple-element.39), channel_id=1, source_target_pairs={{0,64},{64,0},{128,192},{192,128},{1,65},{65,1},{129,193},{193,129... | collective-permute-start | bytes 491528 | tf_op jit(solution)/shard_map/ppermute | solution.py:507
  28.9 7.9 %collective-permute-start.5 = (f32[2,10,16,128]{3,2,1,0:T(8,128)S(1)}, f32[2,10,16,128]{3,2,1,0:T(8,128)S(1)}, u32[]{:S(2)}, u32[]{:S(2)}) collective-permute-start(f32[2,10,16,128]{3,2,1,0:T(8,128)S(1)} %add.11), channel_id=1, source_target_pairs={{0,128},{64,192},{128,0},{192,64},{1,129},{65,193},{129,1},{193,65... | collective-permute-start | bytes 491528 | tf_op jit(solution)/shard_map/ppermute | solution.py:509
  36.1 2.0 %collective-permute-start.3 = (f32[4,152,128]{2,1,0:T(8,128)S(1)}, f32[4,152,128]{2,1,0:T(8,128)S(1)}, u32[]{:S(2)}, u32[]{:S(2)}) collective-permute-start(f32[4,152,128]{2,1,0:T(8,128)S(1)} %get-tuple-element.47), channel_id=1, source_target_pairs={{0,64},{64,0},{128,192},{192,128},{1,65},{65,1},{129,193},{193,129... | collective-permute-start | bytes 933896 | tf_op jit(solution)/shard_map/ppermute | solution.py:517
  36.9 2.8 %collective-permute-start.6 = (f32[2,10,16,128]{3,2,1,0:T(8,128)S(1)}, f32[2,10,16,128]{3,2,1,0:T(8,128)S(1)}, u32[]{:S(2)}, u32[]{:S(2)}) collective-permute-start(f32[2,10,16,128]{3,2,1,0:T(8,128)S(1)} %add.13.sum_mine), channel_id=1, source_target_pairs={{0,64},{64,0},{128,192},{192,128},{1,65},{65,1},{129,193},{193,129... | collective-permute-start | bytes 491528 | tf_op jit(solution)/shard_map/ppermute | solution.py:510
  38.1 11.9 %collective-permute-start.4 = (f32[4,152,128]{2,1,0:T(8,128)S(1)}, f32[4,152,128]{2,1,0:T(8,128)S(1)}, u32[]{:S(2)}, u32[]{:S(2)}) collective-permute-start(f32[4,152,128]{2,1,0:T(8,128)S(1)} %add.12.sum_here), channel_id=1, source_target_pairs={{0,128},{64,192},{128,0},{192,64},{1,129},{65,193},{129,1},{193,65... | collective-permute-start | bytes 933896 | tf_op jit(solution)/shard_map/ppermute | solution.py:518

commit v4 on v3

--- a/solution.py
+++ b/solution.py
@@ -25,7 +25,7 @@
 bf16 = jnp.bfloat16
 
 INNER, EDGES = CY - 2, 4
-BUNDLE_ROWS = 2048 + 768 + 256
+BUNDLE_ROWS = 2048 + 768 + 256 + 40
 WEIGHTS = (256, 3 * REACT)
 SPECIES_ROWS = 2 * FIELDS * CZ * SPECIES
 FLOW_ROWS = 2 * CZ * 8
@@ -73,17 +73,28 @@
 
 def pack(
     species_far, density_far, velocity_far, energy_far, wiener_far, mix_far, substeps_far,
+    reactants_far, stoich_far, rate_far, excitation_far, heat_far, molar_far,
     low, high, bundle,
-    species, density, velocity, energy, wiener, mix, substeps, flow, sems,
+    species, density, velocity, energy, wiener, mix, substeps,
+    reactants, stoich, rate, excitation, heat, molar, flow, table, sems,
 ):
     inputs = start([(species_far, species), (density_far, density), (velocity_far, velocity), (energy_far, energy),
-                    (wiener_far, wiener), (mix_far, mix), (substeps_far, substeps)], sems, 0)
+                    (wiener_far, wiener), (mix_far, mix), (substeps_far, substeps),
+                    (reactants_far, reactants), (stoich_far, stoich), (rate_far, rate), (excitation_far, excitation),
+                    (heat_far, heat), (molar_far, molar)], sems, 0)
     for one in inputs:
         one.wait()
-    passed = start([(species, bundle.at[0:2048]), (wiener, bundle.at[2048:2816])], sems, 7)
+    passed = start([(species, bundle.at[0:2048]), (wiener, bundle.at[2048:2816])], sems, 13)
+    table[...] = jnp.zeros_like(table)
+    table[0:16, 0:REACT] = reactants[...]
+    table[16:32, 0:REACT] = stoich[...]
+    for n, vector in enumerate((rate, excitation)):
+        table[32 + n : 33 + n, 0:REACT] = vector[...]
+    for n, vector in enumerate((heat, molar)):
+        table[34 + n : 35 + n, 0:SPECIES] = vector[...]
     parts = [density[0], velocity[0, 0], velocity[1, 0], velocity[2, 0], energy[0], mix[0], substeps[0].astype(f32)]
     flow_tiles(parts, flow)
-    passed += start([(flow, bundle.at[2816:BUNDLE_ROWS])], sems, 9)
+    passed += start([(flow, bundle.at[2816:3072]), (table, bundle.at[3072:BUNDLE_ROWS])], sems, 15)
     for out, first, edge in ((low, 0, 0), (high, CY - 2, CY - 1)):
         for n in range(2):
             y = first + n
@@ -194,10 +205,13 @@
     store_halves(total, mine, other)
 
 
-def prepare(consts, weights):
-    stoich = consts[240:256, 0:REACT]
+def prepare(bundle, consts, weights):
+    for n, (at, size) in enumerate(((0, REACT), (REACT, REACT), (2 * REACT, SPECIES), (2 * REACT + 16, SPECIES))):
+        square = jnp.broadcast_to(bundle[3104 + n : 3105 + n], (NX, NX)).T
+        consts[at : at + size] = square[0:size]
+    stoich = bundle[3088:3104, 0:REACT]
     for j in range(SPECIES):
-        product = consts[224 + j : 225 + j, 0:REACT] * stoich
+        product = bundle[3072 + j : 3073 + j, 0:REACT] * stoich
         high = product.astype(bf16)
         low = (product - high.astype(f32)).astype(bf16)
         weights[SPECIES * j : SPECIES * (j + 1)] = jnp.concatenate([high, low, high], 1)
@@ -220,17 +234,20 @@
         out[n] = product[:, CZ * NX * m : CZ * NX * (m + 1)]
 
 
-def react(matrices, y, z, flow, flow_y, values, held):
+def react(matrices, y, z, flow, flow_y, values, held, place=None):
+    place = z if place is None else place
     count = jnp.broadcast_to(flow[flow_y, z, 6:7], (SPECIES, NX))
     blocks = [matrices[y, SPECIES * j : SPECIES * (j + 1), NX * z : NX * (z + 1)] for j in range(SPECIES)]
     for k in range(SUBS):
         for n, value in enumerate(values):
-            held[z, n] = value
-        changes = [None] * len(values)
+            held[place, n] = value
+        parts = 2 if len(values) == 1 else 1
+        changes = [[None] * parts for _ in values]
         for j in range(SPECIES):
-            for n in range(len(values)):
-                part = blocks[j] * held[z, n, j : j + 1]
-                changes[n] = part if changes[n] is None else changes[n] + part
+            for n, sums in enumerate(changes):
+                part = blocks[j] * held[place, n, j : j + 1]
+                sums[j % parts] = part if sums[j % parts] is None else sums[j % parts] + part
+        changes = [sum(sums[1:], sums[0]) for sums in changes]
         values = [value + jnp.where(count > float(k), change, 0.0) for value, change in zip(values, changes)]
     return values
 
@@ -244,13 +261,13 @@
 
 
 def inner(
-    bundle, consts,
-    own, flow, noise_first, noise_second, noise_sum, flow_one, total, reacted, matrices, weights,
+    bundle,
+    own, flow, noise_first, noise_second, noise_sum, flow_one, total, reacted, matrices, consts, weights,
     carried, rates, held,
 ):
     lane, lane_flow = lanes((SPECIES, NX)), lanes((8, NX))
-    prepare(consts, weights)
-    flow[...] = bundle[2816:BUNDLE_ROWS].reshape(CY, CZ, 8, NX)
+    prepare(bundle, consts, weights)
+    flow[...] = bundle[2816:3072].reshape(CY, CZ, 8, NX)
 
     def gather(y, _):
         for z in range(CZ):
@@ -407,36 +424,41 @@
 def finish(
     sum_here, sum_there, shared, flow_two, matrices_two, own_part, consts,
     flow_out, species_out,
-    total, held,
+    total, held, ready, sems,
 ):
     total[...] = sum_here[...] + sum_there[...]
     lane = lanes((SPECIES, NX))
-
-    def layer(y, _):
-        column = [shared[y + 1, z] for z in range(CZ)]
-        above = [shared[y + 2, z] for z in range(CZ)]
-        below = [shared[y, z] for z in range(CZ)]
-        for z in range(CZ):
-            neighbour_sum, change = stencil(column, above, below, z, lane)
-            before = total[z, pl.ds(y * SPECIES, SPECIES)] + ALL_FIELDS * (
-                (1.0 - 6.0 * spread) * column[z] + spread * neighbour_sum
-            )
-            for d in range(3):
-                weight = (
-                    noise_half * total[z, pl.ds(128 + 8 * d + y, 1)]
-                    - ALL_FIELDS * speed_half * flow_two[y, z, 1 + d : 2 + d]
+    rows = ready.reshape(CZ * FIELDS * SPECIES * CY, NX)
+    sent = []
+    for z in range(CZ):
+
+        def layers(g, _, z=z):
+            for m in range(4):
+                y = 4 * g + m
+                column = {at: shared[y + 1, at] for at in range(max(z - 1, 0), min(z + 2, CZ))}
+                neighbour_sum, change = stencil(column, {z: shared[y + 2, z]}, {z: shared[y, z]}, z, lane)
+                before = total[z, pl.ds(y * SPECIES, SPECIES)] + ALL_FIELDS * (
+                    (1.0 - 6.0 * spread) * column[z] + spread * neighbour_sum
                 )
-                before = before + weight * change[d]
-            (after,) = react(matrices_two, y, z, flow_two, y, [before], held)
-            tile = add_sources(flow_two[y, z], before, after, consts[192:208], consts[208:224])
-            for v in range(5):
-                flow_out[v, z, pl.ds(y, 1)] = tile[v : v + 1]
-            mean = (flow_two[y, z, 5:6] / ALL_FIELDS) * after
-            for f in range(FIELDS):
-                species_out[pl.ds(f * 512 + z * 8 + y, SPECIES, stride=32), :] = own_part[y, f, z] + mean
-        return 0
-
-    lax.fori_loop(0, CY, layer, 0)
+                for d in range(3):
+                    weight = (
+                        noise_half * total[z, pl.ds(128 + 8 * d + y, 1)]
+                        - ALL_FIELDS * speed_half * flow_two[y, z, 1 + d : 2 + d]
+                    )
+                    before = before + weight * change[d]
+                (after,) = react(matrices_two, y, z, flow_two, y, [before], held, m)
+                tile = add_sources(flow_two[y, z], before, after, consts[192:208], consts[208:224])
+                for v in range(5):
+                    flow_out[v, z, pl.ds(y, 1)] = tile[v : v + 1]
+                mean = (flow_two[y, z, 5:6] / ALL_FIELDS) * after
+                for f in range(FIELDS):
+                    rows[pl.ds((z * FIELDS + f) * SPECIES * CY + y, SPECIES, stride=CY), :] = own_part[y, f, z] + mean
+            return 0
+
+        lax.fori_loop(0, CY // 4, layers, 0)
+        sent += start([(ready.at[z], species_out.at[:, z])], sems, z)
+    for one in sent:
+        one.wait()
 
 
 def call(kernel, name, outs, scratch, micros, *operands, far=0, far_outs=0, semaphores=0, weights_out=False, room=24):
@@ -470,11 +492,8 @@
 ):
     tiles = lax.axis_size("tile")
     wide = CY + 2
-    columns = jnp.concatenate([kinetic_constants, excitation_sensitivity, heat, molar])
-    tables = jnp.concatenate([reactants.T, stoich], 0)
-    consts = jnp.concatenate(
-        [jnp.broadcast_to(columns[:, None], (2 * REACT + 32, NX)), jnp.pad(tables, ((0, 0), (0, NX - REACT)))], 0
-    )
+    vectors = (kinetic_constants, excitation_sensitivity, heat, molar)
+    tables = (reactants.T, stoich) + tuple(vector[None] for vector in vectors)
     grid = (FIELDS, CZ, SPECIES, NX)
     flow_grid, noise_grid = (CZ, 8, NX), (CZ, 16, NX)
     block = (1, CZ, CY, NX)
@@ -482,21 +501,25 @@
 
     copies = [((2048, NX), f32), (block, f32), ((3,) + block, f32), (block, f32), ((768, NX), f32),
               (block, f32), (block, jnp.int32)]
+    copies += [(table.shape, f32) for table in tables]
 
     rates = ((3 * REACT, 4 * CZ * NX), bf16)
     held = ((CZ, FIELDS, SPECIES, NX), f32)
     low, high, bundle = call(
-        pack, "pack", [(MESSAGE_ROWS, NX)] * 2 + [(BUNDLE_ROWS, NX)], copies + [((256, NX), f32)],
-        2, *fields, far=7, far_outs=1, semaphores=10, room=64,
+        pack, "pack", [(MESSAGE_ROWS, NX)] * 2 + [(BUNDLE_ROWS, NX)], copies + [((256, NX), f32), ((40, NX), f32)],
+        2, *fields, *tables, far=13, far_outs=1, semaphores=17, room=64,
     )
     low_halo = lax.ppermute(high, "tile", [(i, i + 1) for i in range(tiles - 1)])
     high_halo = lax.ppermute(low, "tile", [(i + 1, i) for i in range(tiles - 1)])
-    own, flow, noise_first, noise_second, noise_sum, inner_flow, inner_total, inner_reacted, inner_matrices, weights = call(
+    (
+        own, flow, noise_first, noise_second, noise_sum, inner_flow, inner_total, inner_reacted, inner_matrices,
+        consts, weights,
+    ) = call(
         inner, "inner",
         [(CY,) + grid, (CY,) + flow_grid, (CY,) + noise_grid, (CY,) + noise_grid, (CZ, 24, NX),
-         (INNER,) + flow_grid, (CZ, INNER, SPECIES, NX), (INNER,) + grid, (INNER, 256, CZ * NX)],
+         (INNER,) + flow_grid, (CZ, INNER, SPECIES, NX), (INNER,) + grid, (INNER, 256, CZ * NX), (224, NX)],
         [((INNER,) + grid, f32), ((3 * REACT, 3 * CZ * NX), bf16), held],
-        8, bundle, consts, weights_out=True,
+        8, bundle, weights_out=True,
     )
     carried, flow_one, mine, other = call(
         first_edge, "first_edge",
@@ -524,9 +547,10 @@
     )
     flow_out, species_out = call(
         finish, "finish",
-        [(5, CZ, CY, NX), (FIELDS * SPECIES * CZ * CY, NX)],
-        [((CZ, 152, NX), f32), held],
+        [(5, CZ, CY, NX), (FIELDS * SPECIES, CZ, CY, NX)],
+        [((CZ, 152, NX), f32), held, ((CZ, FIELDS * SPECIES, CY, NX), f32)],
         4, second, second_far, shared, flow_two, matrices_two, own_part, consts,
+        far_outs=1, semaphores=CZ,
     )
     return flow_out[:, None], species_out.reshape(species.shape)
 

time: 55 us -> 53.2 us (0.967)
  other arithmetic: 1.67 us -> 0.07 us
    concatenate x3 -> x0, other arithmetic: 1.59 us -> none  [the longest x1 0.78 us: on_device(): jnp.concatenate([kinetic_constants, excitation_sensitivity, heat, molar])]
  transfers between devices with their start and end apart: 7 -> 7, of which waited for: 2 -> 2; matrix products, arithmetic and copies ran while one was open for 3% -> 0% of each run, Pallas kernels for 41% -> 43%
where the time goes in v4:
time: 53.2 us; the launch traced here: 53 us
  Pallas kernels  31.3 us (59%)
  starting transfers between devices  17.6 us (33%)
  waiting for transfers between devices  1.87 us (4%)
  local copies, waits for them, and re-layouts  1.41 us (3%)
  between operations  0.74 us (1%)
    pallas_call x6, Pallas kernels, call(): pl.pallas_call(kernel, out_shape=tuple(shapes), in_specs=places, out_spec...  31.3 us
    ppermute x1, starting transfers between devices, on_device(): lax.ppermute(low, 'tile', [(i + 1, i) for i in range(tiles - 1)])  7.94 us
    ppermute x1, starting transfers between devices, on_device(): lax.ppermute(high, 'tile', [(i, i + 1) for i in range(tiles - 1)])  3.55 us
    ppermute x1, starting transfers between devices, on_device(): sum_mine = mine + lax.ppermute(mine, 'field', CHIP_PAIRS)  2.39 us
    ppermute x1, starting transfers between devices, on_device(): second_far = lax.ppermute(second, 'field', CHIP_PAIRS)  1.57 us
    unnamed x2, local copies, waits for them, and re-layouts  1.41 us
  transfers between devices with their start and end apart: 7, of which 2 were waited for; matrix products, arithmetic and copies ran while one was open for 0% of the time, Pallas kernels for 43%

profile of v4, /device:TPU:9, one launch (start us, length us, event | category | flops | bytes accessed | tf_op | source)
XLA Modules:
  0.0 53.0 jit_solution(15436050514538980439)
XLA Ops:
  0.6 3.5 %pack.1 = (f32[640,128]{1,0:T(8,128)}, f32[640,128]{1,0:T(8,128)}, f32[3112,128]{1,0:T(8,128)}) custom-call(f32[2048,128]{1,0:T(8,128)} %bitcast.13, f32[1,4,8,128]{3,2,1,0:T(8,128)} %density_far.1, f32[3,1,4,8,128]{4,3,2,1,0:T(8,128)} %velocity_far.1, f32[1,4,8,128]{3,2,1,0:T(8,128)} %energy_far.1, f32[768,128]{1,0:T(8,128)} %bitcast.14, ...), custom_call_target="tpu_custom_call" | custom-call | flops 2000000000 | bytes 3818368 | tf_op jit(solution)/shard_map/pack/pallas_call | solution.py:473
  4.2 3.5 %collective-permute-start = (f32[640,128]{1,0:T(8,128)}, f32[640,128]{1,0:T(8,128)S(1)}, u32[]{:S(2)}, u32[]{:S(2)}) collective-permute-start(f32[640,128]{1,0:T(8,128)} %get-tuple-element.37), channel_id=1, source_target_pairs={{0,1},{1,2},{2,3},{3,4},{4,5},{5,6},{6,7},{7,8},{8,9},{9,10},{10,1... | collective-permute-start | bytes 983048 | tf_op jit(solution)/shard_map/ppermute | solution.py:512
  7.7 7.9 %collective-permute-start.1 = (f32[640,128]{1,0:T(8,128)}, f32[640,128]{1,0:T(8,128)S(1)}, u32[]{:S(2)}, u32[]{:S(2)}) collective-permute-start(f32[640,128]{1,0:T(8,128)} %get-tuple-element.38), channel_id=1, source_target_pairs={{1,0},{2,1},{3,2},{4,3},{5,4},{6,5},{7,6},{8,7},{9,8},{10,9},{11,1... | collective-permute-start | bytes 983048 | tf_op jit(solution)/shard_map/ppermute | solution.py:513
  15.7 0.0 copy-start
  15.7 1.4 %copy-done = f32[3112,128]{1,0:T(8,128)S(1)} copy-done((f32[3112,128]{1,0:T(8,128)S(1)}, f32[3112,128]{1,0:T(8,128)}, u32[]{:S(2)}) %copy-start) | copy-done | bytes 1593368
  17.1 7.5 %inner.1 = (f32[8,4,4,16,128]{4,3,2,1,0:T(8,128)S(1)}, f32[8,4,8,128]{3,2,1,0:T(8,128)S(1)}, f32[8,4,16,128]{3,2,1,0:T(8,128)S(1)}, f32[8,4,16,128]{3,2,1,0:T(8,...) custom-call(f32[3112,128]{1,0:T(8,128)S(1)} %copy-done), custom_call_target="tpu_custom_call" | custom-call | flops 8000000000 | bytes 7688192 | tf_op jit(solution)/shard_map/inner/pallas_call | solution.py:473
  24.6 0.0 collective-permute-done.low_halo
  24.6 0.0 collective-permute-done.1.high_halo
  24.6 0.9 %first_edge.1 = (f32[4,4,4,16,128]{4,3,2,1,0:T(8,128)S(1)}, f32[10,4,8,128]{3,2,1,0:T(8,128)S(1)}, f32[2,10,16,128]{3,2,1,0:T(8,128)S(1)}, f32[2,10,16,128]{3,2,1,0:T(8,128)S(1)}) custom-call(f32[8,4,4,16,128]{4,3,2,1,0:T(8,128)S(1)} %get-tuple-element.32.own, f32[8,4,8,128]{3,2,1,0:T(8,128)S(1)} %get-tuple-element.33.flow, ...), custom_call_target="tpu_custom_call" | custom-call | flops 2000000000 | bytes 3407872 | tf_op jit(solution)/shard_map/first_edge/pallas_call | solution.py:473
  25.5 1.0 %collective-permute-start.2 = (f32[2,10,16,128]{3,2,1,0:T(8,128)S(1)}, f32[2,10,16,128]{3,2,1,0:T(8,128)S(1)}, u32[]{:S(2)}, u32[]{:S(2)}) collective-permute-start(f32[2,10,16,128]{3,2,1,0:T(8,128)S(1)} %get-tuple-element.40), channel_id=1, source_target_pairs={{0,64},{64,0},{128,192},{192,128},{1,65},{65,1},{129,193},{193,129... | collective-permute-start | bytes 491528 | tf_op jit(solution)/shard_map/ppermute | solution.py:530
  26.5 1.0 %collective-permute-done.2 = f32[2,10,16,128]{3,2,1,0:T(8,128)S(1)} collective-permute-done((f32[2,10,16,128]{3,2,1,0:T(8,128)S(1)}, f32[2,10,16,128]{3,2,1,0:T(8,128)S(1)}, u32[]{:S(2)}, u32[]{:S(2)}) %collective-permute-start.2) | collective-permute-done | bytes 163872 | tf_op jit(solution)/shard_map/ppermute | solution.py:530
  27.6 2.4 %collective-permute-start.5 = (f32[2,10,16,128]{3,2,1,0:T(8,128)S(1)}, f32[2,10,16,128]{3,2,1,0:T(8,128)S(1)}, u32[]{:S(2)}, u32[]{:S(2)}) collective-permute-start(f32[2,10,16,128]{3,2,1,0:T(8,128)S(1)} %add.9), channel_id=1, source_target_pairs={{0,128},{64,192},{128,0},{192,64},{1,129},{65,193},{129,1},{193,65... | collective-permute-start | bytes 491528 | tf_op jit(solution)/shard_map/ppermute | solution.py:532
  30.0 4.8 %react_edge.1 = (f32[4,256,512]{2,1,0:T(8,128)S(1)}, f32[8,4,4,16,128]{4,3,2,1,0:T(8,128)S(1)}, f32[4,152,128]{2,1,0:T(8,128)S(1)}) custom-call(f32[4,4,4,16,128]{4,3,2,1,0:T(8,128)S(1)} %get-tuple-element.42.carried, f32[10,4,8,128]{3,2,1,0:T(8,128)S(1)} %get-tuple-element.43.flow_one, f32[6,4,4,16,128]{4,3,2,1,0:T(8,128)S(1)} %get-tuple-element.44.inner_reacted, ...), custom_call_target="tpu_custom_call" | custom-call | flops 6000000000 | bytes 5652480 | tf_op jit(solution)/shard_map/react_edge/pallas_call | solution.py:473
  34.8 0.7 %collective-permute-start.3 = (f32[4,152,128]{2,1,0:T(8,128)S(1)}, f32[4,152,128]{2,1,0:T(8,128)S(1)}, u32[]{:S(2)}, u32[]{:S(2)}) collective-permute-start(f32[4,152,128]{2,1,0:T(8,128)S(1)} %get-tuple-element.49), channel_id=1, source_target_pairs={{0,64},{64,0},{128,192},{192,128},{1,65},{65,1},{129,193},{193,129... | collective-permute-start | bytes 933896 | tf_op jit(solution)/shard_map/ppermute | solution.py:540
  35.5 0.0 collective-permute-done.5
  35.5 0.4 collective-permute-start.6
  35.9 0.8 %collective-permute-done.3 = f32[4,152,128]{2,1,0:T(8,128)S(1)} collective-permute-done((f32[4,152,128]{2,1,0:T(8,128)S(1)}, f32[4,152,128]{2,1,0:T(8,128)S(1)}, u32[]{:S(2)}, u32[]{:S(2)}) %collective-permute-start.3) | collective-permute-done | bytes 311328 | tf_op jit(solution)/shard_map/ppermute | solution.py:540
  36.8 1.6 %collective-permute-start.4 = (f32[4,152,128]{2,1,0:T(8,128)S(1)}, f32[4,152,128]{2,1,0:T(8,128)S(1)}, u32[]{:S(2)}, u32[]{:S(2)}) collective-permute-start(f32[4,152,128]{2,1,0:T(8,128)S(1)} %add.10.sum_here), channel_id=1, source_target_pairs={{0,128},{64,192},{128,0},{192,64},{1,129},{65,193},{129,1},{193,65... | collective-permute-start | bytes 933896 | tf_op jit(solution)/shard_map/ppermute | solution.py:541
  38.4 0.0 collective-permute-done.6.sum_other
  38.4 10.3 %second_step.1 = (f32[8,256,512]{2,1,0:T(8,128)S(1)}, f32[8,4,4,16,128]{4,3,2,1,0:T(8,128)S(1)}, f32[10,4,16,128]{3,2,1,0:T(8,128)S(1)}, f32[8,4,8,128]{3,2,1,0:T(8,128)S(1)}) custom-call(f32[2,10,16,128]{3,2,1,0:T(8,128)S(1)} %add.11.sum_mine, f32[2,10,16,128]{3,2,1,0:T(8,128)S(1)} %collective-permute-done.6.sum_other, ...), custom_call_target="tpu_custom_call" | custom-call | flops 10000000000 | bytes 13156352 | tf_op jit(solution)/shard_map/second_step/pallas_call | solution.py:473
  48.6 0.0 collective-permute-done.4.sum_there
  48.7 4.4 %finish.1 = (f32[5,4,8,128]{3,2,1,0:T(8,128)}, f32[64,4,8,128]{3,2,1,0:T(8,128)}) custom-call(f32[4,152,128]{2,1,0:T(8,128)S(1)} %add.10.sum_here, f32[4,152,128]{2,1,0:T(8,128)S(1)} %collective-permute-done.4.sum_there, f32[10,4,16,128]{3,2,1,0:T(8,128)S(1)} %get-tuple-element.54.shared, f32[8,4,8,128]{3,2,1,0:T(8,128)S(1)} %get-tuple-element.55.flow_two, ...), custom_call_target="tpu_custom_call" | custom-call | flops 4000000000 | bytes 7569408 | tf_op jit(solution)/shard_map/finish/pallas_call | solution.py:473
  (3 shorter events, 0.1 us)
Async XLA Ops:
  4.2 20.4 %collective-permute-start = (f32[640,128]{1,0:T(8,128)}, f32[640,128]{1,0:T(8,128)S(1)}, u32[]{:S(2)}, u32[]{:S(2)}) collective-permute-start(f32[640,128]{1,0:T(8,128)} %get-tuple-element.37), channel_id=1, source_target_pairs={{0,1},{1,2},{2,3},{3,4},{4,5},{5,6},{6,7},{7,8},{8,9},{9,10},{10,1... | collective-permute-start | bytes 983048 | tf_op jit(solution)/shard_map/ppermute | solution.py:512
  7.7 16.9 %collective-permute-start.1 = (f32[640,128]{1,0:T(8,128)}, f32[640,128]{1,0:T(8,128)S(1)}, u32[]{:S(2)}, u32[]{:S(2)}) collective-permute-start(f32[640,128]{1,0:T(8,128)} %get-tuple-element.38), channel_id=1, source_target_pairs={{1,0},{2,1},{3,2},{4,3},{5,4},{6,5},{7,6},{8,7},{9,8},{10,9},{11,1... | collective-permute-start | bytes 983048 | tf_op jit(solution)/shard_map/ppermute | solution.py:513
  15.7 1.4 %copy-start = (f32[3112,128]{1,0:T(8,128)S(1)}, f32[3112,128]{1,0:T(8,128)}, u32[]{:S(2)}) copy-start(f32[3112,128]{1,0:T(8,128)} %get-tuple-element.31.bundle) | copy-start | bytes 4780036
  25.5 2.1 %collective-permute-start.2 = (f32[2,10,16,128]{3,2,1,0:T(8,128)S(1)}, f32[2,10,16,128]{3,2,1,0:T(8,128)S(1)}, u32[]{:S(2)}, u32[]{:S(2)}) collective-permute-start(f32[2,10,16,128]{3,2,1,0:T(8,128)S(1)} %get-tuple-element.40), channel_id=1, source_target_pairs={{0,64},{64,0},{128,192},{192,128},{1,65},{65,1},{129,193},{193,129... | collective-permute-start | bytes 491528 | tf_op jit(solution)/shard_map/ppermute | solution.py:530
  27.6 7.9 %collective-permute-start.5 = (f32[2,10,16,128]{3,2,1,0:T(8,128)S(1)}, f32[2,10,16,128]{3,2,1,0:T(8,128)S(1)}, u32[]{:S(2)}, u32[]{:S(2)}) collective-permute-start(f32[2,10,16,128]{3,2,1,0:T(8,128)S(1)} %add.9), channel_id=1, source_target_pairs={{0,128},{64,192},{128,0},{192,64},{1,129},{65,193},{129,1},{193,65... | collective-permute-start | bytes 491528 | tf_op jit(solution)/shard_map/ppermute | solution.py:532
  34.8 2.0 %collective-permute-start.3 = (f32[4,152,128]{2,1,0:T(8,128)S(1)}, f32[4,152,128]{2,1,0:T(8,128)S(1)}, u32[]{:S(2)}, u32[]{:S(2)}) collective-permute-start(f32[4,152,128]{2,1,0:T(8,128)S(1)} %get-tuple-element.49), channel_id=1, source_target_pairs={{0,64},{64,0},{128,192},{192,128},{1,65},{65,1},{129,193},{193,129... | collective-permute-start | bytes 933896 | tf_op jit(solution)/shard_map/ppermute | solution.py:540
  35.5 2.8 %collective-permute-start.6 = (f32[2,10,16,128]{3,2,1,0:T(8,128)S(1)}, f32[2,10,16,128]{3,2,1,0:T(8,128)S(1)}, u32[]{:S(2)}, u32[]{:S(2)}) collective-permute-start(f32[2,10,16,128]{3,2,1,0:T(8,128)S(1)} %add.11.sum_mine), channel_id=1, source_target_pairs={{0,64},{64,0},{128,192},{192,128},{1,65},{65,1},{129,193},{193,129... | collective-permute-start | bytes 491528 | tf_op jit(solution)/shard_map/ppermute | solution.py:533
  36.8 11.9 %collective-permute-start.4 = (f32[4,152,128]{2,1,0:T(8,128)S(1)}, f32[4,152,128]{2,1,0:T(8,128)S(1)}, u32[]{:S(2)}, u32[]{:S(2)}) collective-permute-start(f32[4,152,128]{2,1,0:T(8,128)S(1)} %add.10.sum_here), channel_id=1, source_target_pairs={{0,128},{64,192},{128,0},{192,64},{1,129},{65,193},{129,1},{193,65... | collective-permute-start | bytes 933896 | tf_op jit(solution)/shard_map/ppermute | solution.py:541

commit v5 on v4

--- a/solution.py
+++ b/solution.py
@@ -76,7 +76,7 @@
     reactants_far, stoich_far, rate_far, excitation_far, heat_far, molar_far,
     low, high, bundle,
     species, density, velocity, energy, wiener, mix, substeps,
-    reactants, stoich, rate, excitation, heat, molar, flow, table, sems,
+    reactants, stoich, rate, excitation, heat, molar, flow, table, low_held, high_held, sems,
 ):
     inputs = start([(species_far, species), (density_far, density), (velocity_far, velocity), (energy_far, energy),
                     (wiener_far, wiener), (mix_far, mix), (substeps_far, substeps),
@@ -95,7 +95,7 @@
     parts = [density[0], velocity[0, 0], velocity[1, 0], velocity[2, 0], energy[0], mix[0], substeps[0].astype(f32)]
     flow_tiles(parts, flow)
     passed += start([(flow, bundle.at[2816:3072]), (table, bundle.at[3072:BUNDLE_ROWS])], sems, 15)
-    for out, first, edge in ((low, 0, 0), (high, CY - 2, CY - 1)):
+    for k, (out, sent, first, edge) in enumerate(((low_held, low, 0, 0), (high_held, high, CY - 2, CY - 1))):
         for n in range(2):
             y = first + n
             for f in range(FIELDS):
@@ -108,6 +108,7 @@
         for z in range(CZ):
             row = SPECIES_ROWS + FLOW_ROWS + z * 16
             out[row : row + 16] = noise_tile(wiener, 0, 0, edge, z)
+        passed += start([(out, sent)], sems, 17 + k)
     for one in passed:
         one.wait()
 
@@ -368,25 +369,29 @@
     join_halves(sum_mine, sum_other, total)
     lane, lane_flow = lanes((SPECIES, NX)), lanes((8, NX))
 
-    def mean_layer(matrices, n, at, y):
+    def mean_layer(matrices, n, at, y, slot):
         for z in range(CZ):
             before = total[z, at]
-            (after,) = react(matrices, n, z, flow_one, y, [before], held)
+            (after,) = react(matrices, n, z, flow_one, y, [before], held, slot * CZ + z)
             shared[y, z] = (flow_one[y, z, 5:6] / ALL_FIELDS) * after
             flow_mid[y, z] = add_sources(
                 flow_one[y, z], before, after, consts[192:208], consts[208:224]
             )
 
     def inner_layer(n, _):
-        mean_layer(inner_matrices, n, n, n + 2)
+        for m in range(2):
+            at = 2 * n + m
+            mean_layer(inner_matrices, at, at, at + 2, m)
         return 0
 
     def edge_layer(e, _):
-        mean_layer(edge_matrices, e, INNER + e, e + INNER * (e // 2))
-        return 0
-
-    lax.fori_loop(0, INNER, inner_layer, 0)
-    lax.fori_loop(0, EDGES, edge_layer, 0)
+        for m in range(2):
+            at = 2 * e + m
+            mean_layer(edge_matrices, at, INNER + at, at + INNER * e, m)
+        return 0
+
+    lax.fori_loop(0, INNER // 2, inner_layer, 0)
+    lax.fori_loop(0, EDGES // 2, edge_layer, 0)
 
     def form_group(g, _):
         for m in range(4):
@@ -504,10 +509,10 @@
     copies += [(table.shape, f32) for table in tables]
 
     rates = ((3 * REACT, 4 * CZ * NX), bf16)
-    held = ((CZ, FIELDS, SPECIES, NX), f32)
+    held = ((2 * CZ, FIELDS, SPECIES, NX), f32)
     low, high, bundle = call(
-        pack, "pack", [(MESSAGE_ROWS, NX)] * 2 + [(BUNDLE_ROWS, NX)], copies + [((256, NX), f32), ((40, NX), f32)],
-        2, *fields, *tables, far=13, far_outs=1, semaphores=17, room=64,
+        pack, "pack", [(MESSAGE_ROWS, NX)] * 2 + [(BUNDLE_ROWS, NX)], copies + [((256, NX), f32), ((40, NX), f32)] + [((MESSAGE_ROWS, NX), f32)] * 2,
+        2, *fields, *tables, far=13, far_outs=3, semaphores=19, room=64,
     )
     low_halo = lax.ppermute(high, "tile", [(i, i + 1) for i in range(tiles - 1)])
     high_halo = lax.ppermute(low, "tile", [(i + 1, i) for i in range(tiles - 1)])

time: 53.2 us -> 52.3 us (0.983)
  Pallas kernels: 31.3 us -> 30.4 us
    pallas_call x6, Pallas kernels: 31.3 us -> 30.4 us  [call(): pl.pallas_call(kernel, out_shape=tuple(shapes), in_specs=places, out_spec...]
where the time goes in v5:
time: 52.3 us; the launch traced here: 52.1 us
  Pallas kernels  30.4 us (58%)
  starting transfers between devices  17.6 us (34%)
  waiting for transfers between devices  1.87 us (4%)
  local copies, waits for them, and re-layouts  1.41 us (3%)
  between operations  0.74 us (1%)
    pallas_call x6, Pallas kernels, call(): pl.pallas_call(kernel, out_shape=tuple(shapes), in_specs=places, out_spec...  30.4 us
    ppermute x1, starting transfers between devices, on_device(): lax.ppermute(low, 'tile', [(i + 1, i) for i in range(tiles - 1)])  7.94 us
    ppermute x1, starting transfers between devices, on_device(): lax.ppermute(high, 'tile', [(i, i + 1) for i in range(tiles - 1)])  3.55 us
    ppermute x1, starting transfers between devices, on_device(): sum_mine = mine + lax.ppermute(mine, 'field', CHIP_PAIRS)  2.39 us
    ppermute x1, starting transfers between devices, on_device(): second_far = lax.ppermute(second, 'field', CHIP_PAIRS)  1.57 us
    unnamed x2, local copies, waits for them, and re-layouts  1.41 us
  transfers between devices with their start and end apart: 7, of which 2 were waited for; matrix products, arithmetic and copies ran while one was open for 0% of the time, Pallas kernels for 43%

profile of v5, /device:TPU:9, one launch (start us, length us, event | category | flops | bytes accessed | tf_op | source)
XLA Modules:
  0.0 52.1 jit_solution(13177824675180916232)
XLA Ops:
  0.6 2.9 %pack.1 = (f32[640,128]{1,0:T(8,128)}, f32[640,128]{1,0:T(8,128)}, f32[3112,128]{1,0:T(8,128)}) custom-call(f32[2048,128]{1,0:T(8,128)} %bitcast.13, f32[1,4,8,128]{3,2,1,0:T(8,128)} %density_far.1, f32[3,1,4,8,128]{4,3,2,1,0:T(8,128)} %velocity_far.1, f32[1,4,8,128]{3,2,1,0:T(8,128)} %energy_far.1, f32[768,128]{1,0:T(8,128)} %bitcast.14, ...), custom_call_target="tpu_custom_call" | custom-call | flops 2000000000 | bytes 3818368 | tf_op jit(solution)/shard_map/pack/pallas_call | solution.py:478
  3.5 3.5 %collective-permute-start = (f32[640,128]{1,0:T(8,128)}, f32[640,128]{1,0:T(8,128)S(1)}, u32[]{:S(2)}, u32[]{:S(2)}) collective-permute-start(f32[640,128]{1,0:T(8,128)} %get-tuple-element.37), channel_id=1, source_target_pairs={{0,1},{1,2},{2,3},{3,4},{4,5},{5,6},{6,7},{7,8},{8,9},{9,10},{10,1... | collective-permute-start | bytes 983048 | tf_op jit(solution)/shard_map/ppermute | solution.py:517
  7.1 7.9 %collective-permute-start.1 = (f32[640,128]{1,0:T(8,128)}, f32[640,128]{1,0:T(8,128)S(1)}, u32[]{:S(2)}, u32[]{:S(2)}) collective-permute-start(f32[640,128]{1,0:T(8,128)} %get-tuple-element.38), channel_id=1, source_target_pairs={{1,0},{2,1},{3,2},{4,3},{5,4},{6,5},{7,6},{8,7},{9,8},{10,9},{11,1... | collective-permute-start | bytes 983048 | tf_op jit(solution)/shard_map/ppermute | solution.py:518
  15.0 0.0 copy-start
  15.0 1.4 %copy-done = f32[3112,128]{1,0:T(8,128)S(1)} copy-done((f32[3112,128]{1,0:T(8,128)S(1)}, f32[3112,128]{1,0:T(8,128)}, u32[]{:S(2)}) %copy-start) | copy-done | bytes 1593368
  16.5 7.5 %inner.1 = (f32[8,4,4,16,128]{4,3,2,1,0:T(8,128)S(1)}, f32[8,4,8,128]{3,2,1,0:T(8,128)S(1)}, f32[8,4,16,128]{3,2,1,0:T(8,128)S(1)}, f32[8,4,16,128]{3,2,1,0:T(8,...) custom-call(f32[3112,128]{1,0:T(8,128)S(1)} %copy-done), custom_call_target="tpu_custom_call" | custom-call | flops 8000000000 | bytes 7688192 | tf_op jit(solution)/shard_map/inner/pallas_call | solution.py:478
  24.0 0.0 collective-permute-done.low_halo
  24.0 0.0 collective-permute-done.1.high_halo
  24.0 0.9 %first_edge.1 = (f32[4,4,4,16,128]{4,3,2,1,0:T(8,128)S(1)}, f32[10,4,8,128]{3,2,1,0:T(8,128)S(1)}, f32[2,10,16,128]{3,2,1,0:T(8,128)S(1)}, f32[2,10,16,128]{3,2,1,0:T(8,128)S(1)}) custom-call(f32[8,4,4,16,128]{4,3,2,1,0:T(8,128)S(1)} %get-tuple-element.32.own, f32[8,4,8,128]{3,2,1,0:T(8,128)S(1)} %get-tuple-element.33.flow, ...), custom_call_target="tpu_custom_call" | custom-call | flops 2000000000 | bytes 3407872 | tf_op jit(solution)/shard_map/first_edge/pallas_call | solution.py:478
  24.9 1.0 %collective-permute-start.2 = (f32[2,10,16,128]{3,2,1,0:T(8,128)S(1)}, f32[2,10,16,128]{3,2,1,0:T(8,128)S(1)}, u32[]{:S(2)}, u32[]{:S(2)}) collective-permute-start(f32[2,10,16,128]{3,2,1,0:T(8,128)S(1)} %get-tuple-element.40), channel_id=1, source_target_pairs={{0,64},{64,0},{128,192},{192,128},{1,65},{65,1},{129,193},{193,129... | collective-permute-start | bytes 491528 | tf_op jit(solution)/shard_map/ppermute | solution.py:535
  25.9 1.0 %collective-permute-done.2 = f32[2,10,16,128]{3,2,1,0:T(8,128)S(1)} collective-permute-done((f32[2,10,16,128]{3,2,1,0:T(8,128)S(1)}, f32[2,10,16,128]{3,2,1,0:T(8,128)S(1)}, u32[]{:S(2)}, u32[]{:S(2)}) %collective-permute-start.2) | collective-permute-done | bytes 163872 | tf_op jit(solution)/shard_map/ppermute | solution.py:535
  27.0 2.4 %collective-permute-start.5 = (f32[2,10,16,128]{3,2,1,0:T(8,128)S(1)}, f32[2,10,16,128]{3,2,1,0:T(8,128)S(1)}, u32[]{:S(2)}, u32[]{:S(2)}) collective-permute-start(f32[2,10,16,128]{3,2,1,0:T(8,128)S(1)} %add.9), channel_id=1, source_target_pairs={{0,128},{64,192},{128,0},{192,64},{1,129},{65,193},{129,1},{193,65... | collective-permute-start | bytes 491528 | tf_op jit(solution)/shard_map/ppermute | solution.py:537
  29.4 4.8 %react_edge.1 = (f32[4,256,512]{2,1,0:T(8,128)S(1)}, f32[8,4,4,16,128]{4,3,2,1,0:T(8,128)S(1)}, f32[4,152,128]{2,1,0:T(8,128)S(1)}) custom-call(f32[4,4,4,16,128]{4,3,2,1,0:T(8,128)S(1)} %get-tuple-element.42.carried, f32[10,4,8,128]{3,2,1,0:T(8,128)S(1)} %get-tuple-element.43.flow_one, f32[6,4,4,16,128]{4,3,2,1,0:T(8,128)S(1)} %get-tuple-element.44.inner_reacted, ...), custom_call_target="tpu_custom_call" | custom-call | flops 6000000000 | bytes 5652480 | tf_op jit(solution)/shard_map/react_edge/pallas_call | solution.py:478
  34.1 0.7 %collective-permute-start.3 = (f32[4,152,128]{2,1,0:T(8,128)S(1)}, f32[4,152,128]{2,1,0:T(8,128)S(1)}, u32[]{:S(2)}, u32[]{:S(2)}) collective-permute-start(f32[4,152,128]{2,1,0:T(8,128)S(1)} %get-tuple-element.49), channel_id=1, source_target_pairs={{0,64},{64,0},{128,192},{192,128},{1,65},{65,1},{129,193},{193,129... | collective-permute-start | bytes 933896 | tf_op jit(solution)/shard_map/ppermute | solution.py:545
  34.9 0.0 collective-permute-done.5
  34.9 0.4 collective-permute-start.6
  35.3 0.8 %collective-permute-done.3 = f32[4,152,128]{2,1,0:T(8,128)S(1)} collective-permute-done((f32[4,152,128]{2,1,0:T(8,128)S(1)}, f32[4,152,128]{2,1,0:T(8,128)S(1)}, u32[]{:S(2)}, u32[]{:S(2)}) %collective-permute-start.3) | collective-permute-done | bytes 311328 | tf_op jit(solution)/shard_map/ppermute | solution.py:545
  36.1 1.6 %collective-permute-start.4 = (f32[4,152,128]{2,1,0:T(8,128)S(1)}, f32[4,152,128]{2,1,0:T(8,128)S(1)}, u32[]{:S(2)}, u32[]{:S(2)}) collective-permute-start(f32[4,152,128]{2,1,0:T(8,128)S(1)} %add.10.sum_here), channel_id=1, source_target_pairs={{0,128},{64,192},{128,0},{192,64},{1,129},{65,193},{129,1},{193,65... | collective-permute-start | bytes 933896 | tf_op jit(solution)/shard_map/ppermute | solution.py:546
  37.7 0.0 collective-permute-done.6.sum_other
  37.7 10.0 %second_step.1 = (f32[8,256,512]{2,1,0:T(8,128)S(1)}, f32[8,4,4,16,128]{4,3,2,1,0:T(8,128)S(1)}, f32[10,4,16,128]{3,2,1,0:T(8,128)S(1)}, f32[8,4,8,128]{3,2,1,0:T(8,128)S(1)}) custom-call(f32[2,10,16,128]{3,2,1,0:T(8,128)S(1)} %add.11.sum_mine, f32[2,10,16,128]{3,2,1,0:T(8,128)S(1)} %collective-permute-done.6.sum_other, ...), custom_call_target="tpu_custom_call" | custom-call | flops 10000000000 | bytes 13156352 | tf_op jit(solution)/shard_map/second_step/pallas_call | solution.py:478
  47.8 0.0 collective-permute-done.4.sum_there
  47.8 4.4 %finish.1 = (f32[5,4,8,128]{3,2,1,0:T(8,128)}, f32[64,4,8,128]{3,2,1,0:T(8,128)}) custom-call(f32[4,152,128]{2,1,0:T(8,128)S(1)} %add.10.sum_here, f32[4,152,128]{2,1,0:T(8,128)S(1)} %collective-permute-done.4.sum_there, f32[10,4,16,128]{3,2,1,0:T(8,128)S(1)} %get-tuple-element.54.shared, f32[8,4,8,128]{3,2,1,0:T(8,128)S(1)} %get-tuple-element.55.flow_two, ...), custom_call_target="tpu_custom_call" | custom-call | flops 4000000000 | bytes 7569408 | tf_op jit(solution)/shard_map/finish/pallas_call | solution.py:478
  (3 shorter events, 0.1 us)
Async XLA Ops:
  3.5 20.4 %collective-permute-start = (f32[640,128]{1,0:T(8,128)}, f32[640,128]{1,0:T(8,128)S(1)}, u32[]{:S(2)}, u32[]{:S(2)}) collective-permute-start(f32[640,128]{1,0:T(8,128)} %get-tuple-element.37), channel_id=1, source_target_pairs={{0,1},{1,2},{2,3},{3,4},{4,5},{5,6},{6,7},{7,8},{8,9},{9,10},{10,1... | collective-permute-start | bytes 983048 | tf_op jit(solution)/shard_map/ppermute | solution.py:517
  7.1 16.9 %collective-permute-start.1 = (f32[640,128]{1,0:T(8,128)}, f32[640,128]{1,0:T(8,128)S(1)}, u32[]{:S(2)}, u32[]{:S(2)}) collective-permute-start(f32[640,128]{1,0:T(8,128)} %get-tuple-element.38), channel_id=1, source_target_pairs={{1,0},{2,1},{3,2},{4,3},{5,4},{6,5},{7,6},{8,7},{9,8},{10,9},{11,1... | collective-permute-start | bytes 983048 | tf_op jit(solution)/shard_map/ppermute | solution.py:518
  15.0 1.4 %copy-start = (f32[3112,128]{1,0:T(8,128)S(1)}, f32[3112,128]{1,0:T(8,128)}, u32[]{:S(2)}) copy-start(f32[3112,128]{1,0:T(8,128)} %get-tuple-element.31.bundle) | copy-start | bytes 4780036
  24.9 2.1 %collective-permute-start.2 = (f32[2,10,16,128]{3,2,1,0:T(8,128)S(1)}, f32[2,10,16,128]{3,2,1,0:T(8,128)S(1)}, u32[]{:S(2)}, u32[]{:S(2)}) collective-permute-start(f32[2,10,16,128]{3,2,1,0:T(8,128)S(1)} %get-tuple-element.40), channel_id=1, source_target_pairs={{0,64},{64,0},{128,192},{192,128},{1,65},{65,1},{129,193},{193,129... | collective-permute-start | bytes 491528 | tf_op jit(solution)/shard_map/ppermute | solution.py:535
  27.0 7.9 %collective-permute-start.5 = (f32[2,10,16,128]{3,2,1,0:T(8,128)S(1)}, f32[2,10,16,128]{3,2,1,0:T(8,128)S(1)}, u32[]{:S(2)}, u32[]{:S(2)}) collective-permute-start(f32[2,10,16,128]{3,2,1,0:T(8,128)S(1)} %add.9), channel_id=1, source_target_pairs={{0,128},{64,192},{128,0},{192,64},{1,129},{65,193},{129,1},{193,65... | collective-permute-start | bytes 491528 | tf_op jit(solution)/shard_map/ppermute | solution.py:537
  34.1 2.0 %collective-permute-start.3 = (f32[4,152,128]{2,1,0:T(8,128)S(1)}, f32[4,152,128]{2,1,0:T(8,128)S(1)}, u32[]{:S(2)}, u32[]{:S(2)}) collective-permute-start(f32[4,152,128]{2,1,0:T(8,128)S(1)} %get-tuple-element.49), channel_id=1, source_target_pairs={{0,64},{64,0},{128,192},{192,128},{1,65},{65,1},{129,193},{193,129... | collective-permute-start | bytes 933896 | tf_op jit(solution)/shard_map/ppermute | solution.py:545
  34.9 2.8 %collective-permute-start.6 = (f32[2,10,16,128]{3,2,1,0:T(8,128)S(1)}, f32[2,10,16,128]{3,2,1,0:T(8,128)S(1)}, u32[]{:S(2)}, u32[]{:S(2)}) collective-permute-start(f32[2,10,16,128]{3,2,1,0:T(8,128)S(1)} %add.11.sum_mine), channel_id=1, source_target_pairs={{0,64},{64,0},{128,192},{192,128},{1,65},{65,1},{129,193},{193,129... | collective-permute-start | bytes 491528 | tf_op jit(solution)/shard_map/ppermute | solution.py:538
  36.1 11.6 %collective-permute-start.4 = (f32[4,152,128]{2,1,0:T(8,128)S(1)}, f32[4,152,128]{2,1,0:T(8,128)S(1)}, u32[]{:S(2)}, u32[]{:S(2)}) collective-permute-start(f32[4,152,128]{2,1,0:T(8,128)S(1)} %add.10.sum_here), channel_id=1, source_target_pairs={{0,128},{64,192},{128,0},{192,64},{1,129},{65,193},{129,1},{193,65... | collective-permute-start | bytes 933896 | tf_op jit(solution)/shard_map/ppermute | solution.py:546

commit v6 on v5

--- a/solution.py
+++ b/solution.py
@@ -436,31 +436,25 @@
     rows = ready.reshape(CZ * FIELDS * SPECIES * CY, NX)
     sent = []
     for z in range(CZ):
-
-        def layers(g, _, z=z):
-            for m in range(4):
-                y = 4 * g + m
-                column = {at: shared[y + 1, at] for at in range(max(z - 1, 0), min(z + 2, CZ))}
-                neighbour_sum, change = stencil(column, {z: shared[y + 2, z]}, {z: shared[y, z]}, z, lane)
-                before = total[z, pl.ds(y * SPECIES, SPECIES)] + ALL_FIELDS * (
-                    (1.0 - 6.0 * spread) * column[z] + spread * neighbour_sum
+        for y in range(CY):
+            column = {at: shared[y + 1, at] for at in range(max(z - 1, 0), min(z + 2, CZ))}
+            neighbour_sum, change = stencil(column, {z: shared[y + 2, z]}, {z: shared[y, z]}, z, lane)
+            before = total[z, pl.ds(y * SPECIES, SPECIES)] + ALL_FIELDS * (
+                (1.0 - 6.0 * spread) * column[z] + spread * neighbour_sum
+            )
+            for d in range(3):
+                weight = (
+                    noise_half * total[z, pl.ds(128 + 8 * d + y, 1)]
+                    - ALL_FIELDS * speed_half * flow_two[y, z, 1 + d : 2 + d]
                 )
-                for d in range(3):
-                    weight = (
-                        noise_half * total[z, pl.ds(128 + 8 * d + y, 1)]
-                        - ALL_FIELDS * speed_half * flow_two[y, z, 1 + d : 2 + d]
-                    )
-                    before = before + weight * change[d]
-                (after,) = react(matrices_two, y, z, flow_two, y, [before], held, m)
-                tile = add_sources(flow_two[y, z], before, after, consts[192:208], consts[208:224])
-                for v in range(5):
-                    flow_out[v, z, pl.ds(y, 1)] = tile[v : v + 1]
-                mean = (flow_two[y, z, 5:6] / ALL_FIELDS) * after
-                for f in range(FIELDS):
-                    rows[pl.ds((z * FIELDS + f) * SPECIES * CY + y, SPECIES, stride=CY), :] = own_part[y, f, z] + mean
-            return 0
-
-        lax.fori_loop(0, CY // 4, layers, 0)
+                before = before + weight * change[d]
+            (after,) = react(matrices_two, y, z, flow_two, y, [before], held, y)
+            tile = add_sources(flow_two[y, z], before, after, consts[192:208], consts[208:224])
+            for v in range(5):
+                flow_out[v, z, pl.ds(y, 1)] = tile[v : v + 1]
+            mean = (flow_two[y, z, 5:6] / ALL_FIELDS) * after
+            for f in range(FIELDS):
+                rows[pl.ds((z * FIELDS + f) * SPECIES * CY + y, SPECIES, stride=CY), :] = own_part[y, f, z] + mean
         sent += start([(ready.at[z], species_out.at[:, z])], sems, z)
     for one in sent:
         one.wait()

time: 52.3 us -> 51.7 us (0.989)
    pallas_call x6, Pallas kernels: 30.4 us -> 29.9 us  [call(): pl.pallas_call(kernel, out_shape=tuple(shapes), in_specs=places, out_spec...]
where the time goes in v6:
time: 51.7 us; the launch traced here: 51.6 us
  Pallas kernels  29.9 us (58%)
  starting transfers between devices  17.6 us (34%)
  waiting for transfers between devices  1.87 us (4%)
  local copies, waits for them, and re-layouts  1.41 us (3%)
  between operations  0.74 us (1%)
    pallas_call x6, Pallas kernels, call(): pl.pallas_call(kernel, out_shape=tuple(shapes), in_specs=places, out_spec...  29.9 us
    ppermute x1, starting transfers between devices, on_device(): lax.ppermute(low, 'tile', [(i + 1, i) for i in range(tiles - 1)])  7.94 us
    ppermute x1, starting transfers between devices, on_device(): lax.ppermute(high, 'tile', [(i, i + 1) for i in range(tiles - 1)])  3.55 us
    ppermute x1, starting transfers between devices, on_device(): sum_mine = mine + lax.ppermute(mine, 'field', CHIP_PAIRS)  2.39 us
    ppermute x1, starting transfers between devices, on_device(): second_far = lax.ppermute(second, 'field', CHIP_PAIRS)  1.57 us
    unnamed x2, local copies, waits for them, and re-layouts  1.41 us
    ppermute x1, starting transfers between devices, on_device(): mine = mine + lax.ppermute(other, 'field', CORE_PAIRS)  1.04 us
  transfers between devices with their start and end apart: 7, of which 2 were waited for; matrix products, arithmetic and copies ran while one was open for 0% of the time, Pallas kernels for 43%

profile of v6, /device:TPU:9, one launch (start us, length us, event | category | flops | bytes accessed | tf_op | source)
XLA Modules:
  0.0 51.6 jit_solution(12471985783895006380)
XLA Ops:
  0.6 2.9 %pack.1 = (f32[640,128]{1,0:T(8,128)}, f32[640,128]{1,0:T(8,128)}, f32[3112,128]{1,0:T(8,128)}) custom-call(f32[2048,128]{1,0:T(8,128)} %bitcast.13, f32[1,4,8,128]{3,2,1,0:T(8,128)} %density_far.1, f32[3,1,4,8,128]{4,3,2,1,0:T(8,128)} %velocity_far.1, f32[1,4,8,128]{3,2,1,0:T(8,128)} %energy_far.1, f32[768,128]{1,0:T(8,128)} %bitcast.14, ...), custom_call_target="tpu_custom_call" | custom-call | flops 2000000000 | bytes 3818368 | tf_op jit(solution)/shard_map/pack/pallas_call | solution.py:472
  3.5 3.5 %collective-permute-start = (f32[640,128]{1,0:T(8,128)}, f32[640,128]{1,0:T(8,128)S(1)}, u32[]{:S(2)}, u32[]{:S(2)}) collective-permute-start(f32[640,128]{1,0:T(8,128)} %get-tuple-element.37), channel_id=1, source_target_pairs={{0,1},{1,2},{2,3},{3,4},{4,5},{5,6},{6,7},{7,8},{8,9},{9,10},{10,1... | collective-permute-start | bytes 983048 | tf_op jit(solution)/shard_map/ppermute | solution.py:511
  7.1 7.9 %collective-permute-start.1 = (f32[640,128]{1,0:T(8,128)}, f32[640,128]{1,0:T(8,128)S(1)}, u32[]{:S(2)}, u32[]{:S(2)}) collective-permute-start(f32[640,128]{1,0:T(8,128)} %get-tuple-element.38), channel_id=1, source_target_pairs={{1,0},{2,1},{3,2},{4,3},{5,4},{6,5},{7,6},{8,7},{9,8},{10,9},{11,1... | collective-permute-start | bytes 983048 | tf_op jit(solution)/shard_map/ppermute | solution.py:512
  15.0 0.0 copy-start
  15.0 1.4 %copy-done = f32[3112,128]{1,0:T(8,128)S(1)} copy-done((f32[3112,128]{1,0:T(8,128)S(1)}, f32[3112,128]{1,0:T(8,128)}, u32[]{:S(2)}) %copy-start) | copy-done | bytes 1593368
  16.5 7.5 %inner.1 = (f32[8,4,4,16,128]{4,3,2,1,0:T(8,128)S(1)}, f32[8,4,8,128]{3,2,1,0:T(8,128)S(1)}, f32[8,4,16,128]{3,2,1,0:T(8,128)S(1)}, f32[8,4,16,128]{3,2,1,0:T(8,...) custom-call(f32[3112,128]{1,0:T(8,128)S(1)} %copy-done), custom_call_target="tpu_custom_call" | custom-call | flops 8000000000 | bytes 7688192 | tf_op jit(solution)/shard_map/inner/pallas_call | solution.py:472
  24.0 0.0 collective-permute-done.low_halo
  24.0 0.0 collective-permute-done.1.high_halo
  24.0 0.9 %first_edge.1 = (f32[4,4,4,16,128]{4,3,2,1,0:T(8,128)S(1)}, f32[10,4,8,128]{3,2,1,0:T(8,128)S(1)}, f32[2,10,16,128]{3,2,1,0:T(8,128)S(1)}, f32[2,10,16,128]{3,2,1,0:T(8,128)S(1)}) custom-call(f32[8,4,4,16,128]{4,3,2,1,0:T(8,128)S(1)} %get-tuple-element.32.own, f32[8,4,8,128]{3,2,1,0:T(8,128)S(1)} %get-tuple-element.33.flow, ...), custom_call_target="tpu_custom_call" | custom-call | flops 2000000000 | bytes 3407872 | tf_op jit(solution)/shard_map/first_edge/pallas_call | solution.py:472
  24.9 1.0 %collective-permute-start.2 = (f32[2,10,16,128]{3,2,1,0:T(8,128)S(1)}, f32[2,10,16,128]{3,2,1,0:T(8,128)S(1)}, u32[]{:S(2)}, u32[]{:S(2)}) collective-permute-start(f32[2,10,16,128]{3,2,1,0:T(8,128)S(1)} %get-tuple-element.40), channel_id=1, source_target_pairs={{0,64},{64,0},{128,192},{192,128},{1,65},{65,1},{129,193},{193,129... | collective-permute-start | bytes 491528 | tf_op jit(solution)/shard_map/ppermute | solution.py:529
  25.9 1.0 %collective-permute-done.2 = f32[2,10,16,128]{3,2,1,0:T(8,128)S(1)} collective-permute-done((f32[2,10,16,128]{3,2,1,0:T(8,128)S(1)}, f32[2,10,16,128]{3,2,1,0:T(8,128)S(1)}, u32[]{:S(2)}, u32[]{:S(2)}) %collective-permute-start.2) | collective-permute-done | bytes 163872 | tf_op jit(solution)/shard_map/ppermute | solution.py:529
  27.0 2.4 %collective-permute-start.5 = (f32[2,10,16,128]{3,2,1,0:T(8,128)S(1)}, f32[2,10,16,128]{3,2,1,0:T(8,128)S(1)}, u32[]{:S(2)}, u32[]{:S(2)}) collective-permute-start(f32[2,10,16,128]{3,2,1,0:T(8,128)S(1)} %add.9), channel_id=1, source_target_pairs={{0,128},{64,192},{128,0},{192,64},{1,129},{65,193},{129,1},{193,65... | collective-permute-start | bytes 491528 | tf_op jit(solution)/shard_map/ppermute | solution.py:531
  29.4 4.8 %react_edge.1 = (f32[4,256,512]{2,1,0:T(8,128)S(1)}, f32[8,4,4,16,128]{4,3,2,1,0:T(8,128)S(1)}, f32[4,152,128]{2,1,0:T(8,128)S(1)}) custom-call(f32[4,4,4,16,128]{4,3,2,1,0:T(8,128)S(1)} %get-tuple-element.42.carried, f32[10,4,8,128]{3,2,1,0:T(8,128)S(1)} %get-tuple-element.43.flow_one, f32[6,4,4,16,128]{4,3,2,1,0:T(8,128)S(1)} %get-tuple-element.44.inner_reacted, ...), custom_call_target="tpu_custom_call" | custom-call | flops 6000000000 | bytes 5652480 | tf_op jit(solution)/shard_map/react_edge/pallas_call | solution.py:472
  34.1 0.7 %collective-permute-start.3 = (f32[4,152,128]{2,1,0:T(8,128)S(1)}, f32[4,152,128]{2,1,0:T(8,128)S(1)}, u32[]{:S(2)}, u32[]{:S(2)}) collective-permute-start(f32[4,152,128]{2,1,0:T(8,128)S(1)} %get-tuple-element.49), channel_id=1, source_target_pairs={{0,64},{64,0},{128,192},{192,128},{1,65},{65,1},{129,193},{193,129... | collective-permute-start | bytes 933896 | tf_op jit(solution)/shard_map/ppermute | solution.py:539
  34.9 0.0 collective-permute-done.5
  34.9 0.4 collective-permute-start.6
  35.3 0.8 %collective-permute-done.3 = f32[4,152,128]{2,1,0:T(8,128)S(1)} collective-permute-done((f32[4,152,128]{2,1,0:T(8,128)S(1)}, f32[4,152,128]{2,1,0:T(8,128)S(1)}, u32[]{:S(2)}, u32[]{:S(2)}) %collective-permute-start.3) | collective-permute-done | bytes 311328 | tf_op jit(solution)/shard_map/ppermute | solution.py:539
  36.1 1.6 %collective-permute-start.4 = (f32[4,152,128]{2,1,0:T(8,128)S(1)}, f32[4,152,128]{2,1,0:T(8,128)S(1)}, u32[]{:S(2)}, u32[]{:S(2)}) collective-permute-start(f32[4,152,128]{2,1,0:T(8,128)S(1)} %add.10.sum_here), channel_id=1, source_target_pairs={{0,128},{64,192},{128,0},{192,64},{1,129},{65,193},{129,1},{193,65... | collective-permute-start | bytes 933896 | tf_op jit(solution)/shard_map/ppermute | solution.py:540
  37.7 0.0 collective-permute-done.6.sum_other
  37.7 10.0 %second_step.1 = (f32[8,256,512]{2,1,0:T(8,128)S(1)}, f32[8,4,4,16,128]{4,3,2,1,0:T(8,128)S(1)}, f32[10,4,16,128]{3,2,1,0:T(8,128)S(1)}, f32[8,4,8,128]{3,2,1,0:T(8,128)S(1)}) custom-call(f32[2,10,16,128]{3,2,1,0:T(8,128)S(1)} %add.11.sum_mine, f32[2,10,16,128]{3,2,1,0:T(8,128)S(1)} %collective-permute-done.6.sum_other, ...), custom_call_target="tpu_custom_call" | custom-call | flops 10000000000 | bytes 13156352 | tf_op jit(solution)/shard_map/second_step/pallas_call | solution.py:472
  47.8 0.0 collective-permute-done.4.sum_there
  47.8 3.8 %finish.1 = (f32[5,4,8,128]{3,2,1,0:T(8,128)}, f32[64,4,8,128]{3,2,1,0:T(8,128)}) custom-call(f32[4,152,128]{2,1,0:T(8,128)S(1)} %add.10.sum_here, f32[4,152,128]{2,1,0:T(8,128)S(1)} %collective-permute-done.4.sum_there, f32[10,4,16,128]{3,2,1,0:T(8,128)S(1)} %get-tuple-element.54.shared, f32[8,4,8,128]{3,2,1,0:T(8,128)S(1)} %get-tuple-element.55.flow_two, ...), custom_call_target="tpu_custom_call" | custom-call | flops 4000000000 | bytes 7569408 | tf_op jit(solution)/shard_map/finish/pallas_call | solution.py:472
  (3 shorter events, 0.1 us)
Async XLA Ops:
  3.5 20.4 %collective-permute-start = (f32[640,128]{1,0:T(8,128)}, f32[640,128]{1,0:T(8,128)S(1)}, u32[]{:S(2)}, u32[]{:S(2)}) collective-permute-start(f32[640,128]{1,0:T(8,128)} %get-tuple-element.37), channel_id=1, source_target_pairs={{0,1},{1,2},{2,3},{3,4},{4,5},{5,6},{6,7},{7,8},{8,9},{9,10},{10,1... | collective-permute-start | bytes 983048 | tf_op jit(solution)/shard_map/ppermute | solution.py:511
  7.1 16.9 %collective-permute-start.1 = (f32[640,128]{1,0:T(8,128)}, f32[640,128]{1,0:T(8,128)S(1)}, u32[]{:S(2)}, u32[]{:S(2)}) collective-permute-start(f32[640,128]{1,0:T(8,128)} %get-tuple-element.38), channel_id=1, source_target_pairs={{1,0},{2,1},{3,2},{4,3},{5,4},{6,5},{7,6},{8,7},{9,8},{10,9},{11,1... | collective-permute-start | bytes 983048 | tf_op jit(solution)/shard_map/ppermute | solution.py:512
  15.0 1.4 %copy-start = (f32[3112,128]{1,0:T(8,128)S(1)}, f32[3112,128]{1,0:T(8,128)}, u32[]{:S(2)}) copy-start(f32[3112,128]{1,0:T(8,128)} %get-tuple-element.31.bundle) | copy-start | bytes 4780036
  24.9 2.1 %collective-permute-start.2 = (f32[2,10,16,128]{3,2,1,0:T(8,128)S(1)}, f32[2,10,16,128]{3,2,1,0:T(8,128)S(1)}, u32[]{:S(2)}, u32[]{:S(2)}) collective-permute-start(f32[2,10,16,128]{3,2,1,0:T(8,128)S(1)} %get-tuple-element.40), channel_id=1, source_target_pairs={{0,64},{64,0},{128,192},{192,128},{1,65},{65,1},{129,193},{193,129... | collective-permute-start | bytes 491528 | tf_op jit(solution)/shard_map/ppermute | solution.py:529
  27.0 7.9 %collective-permute-start.5 = (f32[2,10,16,128]{3,2,1,0:T(8,128)S(1)}, f32[2,10,16,128]{3,2,1,0:T(8,128)S(1)}, u32[]{:S(2)}, u32[]{:S(2)}) collective-permute-start(f32[2,10,16,128]{3,2,1,0:T(8,128)S(1)} %add.9), channel_id=1, source_target_pairs={{0,128},{64,192},{128,0},{192,64},{1,129},{65,193},{129,1},{193,65... | collective-permute-start | bytes 491528 | tf_op jit(solution)/shard_map/ppermute | solution.py:531
  34.1 2.0 %collective-permute-start.3 = (f32[4,152,128]{2,1,0:T(8,128)S(1)}, f32[4,152,128]{2,1,0:T(8,128)S(1)}, u32[]{:S(2)}, u32[]{:S(2)}) collective-permute-start(f32[4,152,128]{2,1,0:T(8,128)S(1)} %get-tuple-element.49), channel_id=1, source_target_pairs={{0,64},{64,0},{128,192},{192,128},{1,65},{65,1},{129,193},{193,129... | collective-permute-start | bytes 933896 | tf_op jit(solution)/shard_map/ppermute | solution.py:539
  34.9 2.8 %collective-permute-start.6 = (f32[2,10,16,128]{3,2,1,0:T(8,128)S(1)}, f32[2,10,16,128]{3,2,1,0:T(8,128)S(1)}, u32[]{:S(2)}, u32[]{:S(2)}) collective-permute-start(f32[2,10,16,128]{3,2,1,0:T(8,128)S(1)} %add.11.sum_mine), channel_id=1, source_target_pairs={{0,64},{64,0},{128,192},{192,128},{1,65},{65,1},{129,193},{193,129... | collective-permute-start | bytes 491528 | tf_op jit(solution)/shard_map/ppermute | solution.py:532
  36.1 11.6 %collective-permute-start.4 = (f32[4,152,128]{2,1,0:T(8,128)S(1)}, f32[4,152,128]{2,1,0:T(8,128)S(1)}, u32[]{:S(2)}, u32[]{:S(2)}) collective-permute-start(f32[4,152,128]{2,1,0:T(8,128)S(1)} %add.10.sum_here), channel_id=1, source_target_pairs={{0,128},{64,192},{128,0},{192,64},{1,129},{65,193},{129,1},{193,65... | collective-permute-start | bytes 933896 | tf_op jit(solution)/shard_map/ppermute | solution.py:540

commit v7 on v6

--- a/solution.py
+++ b/solution.py
@@ -379,8 +379,8 @@
             )
 
     def inner_layer(n, _):
-        for m in range(2):
-            at = 2 * n + m
+        for m in range(3):
+            at = 3 * n + m
             mean_layer(inner_matrices, at, at, at + 2, m)
         return 0
 
@@ -390,7 +390,7 @@
             mean_layer(edge_matrices, at, INNER + at, at + INNER * e, m)
         return 0
 
-    lax.fori_loop(0, INNER // 2, inner_layer, 0)
+    lax.fori_loop(0, INNER // 3, inner_layer, 0)
     lax.fori_loop(0, EDGES // 2, edge_layer, 0)
 
     def form_group(g, _):
@@ -503,7 +503,7 @@
     copies += [(table.shape, f32) for table in tables]
 
     rates = ((3 * REACT, 4 * CZ * NX), bf16)
-    held = ((2 * CZ, FIELDS, SPECIES, NX), f32)
+    held = ((3 * CZ, FIELDS, SPECIES, NX), f32)
     low, high, bundle = call(
         pack, "pack", [(MESSAGE_ROWS, NX)] * 2 + [(BUNDLE_ROWS, NX)], copies + [((256, NX), f32), ((40, NX), f32)] + [((MESSAGE_ROWS, NX), f32)] * 2,
         2, *fields, *tables, far=13, far_outs=3, semaphores=19, room=64,

time: 51.7 us -> 51.7 us (level)
  no operation moved by 1% of the time
where the time goes in v7:
time: 51.7 us; the launch traced here: 51.5 us
  Pallas kernels  29.8 us (58%)
  starting transfers between devices  17.6 us (34%)
  waiting for transfers between devices  1.87 us (4%)
  local copies, waits for them, and re-layouts  1.41 us (3%)
  between operations  0.74 us (1%)
    pallas_call x6, Pallas kernels, call(): pl.pallas_call(kernel, out_shape=tuple(shapes), in_specs=places, out_spec...  29.8 us
    ppermute x1, starting transfers between devices, on_device(): lax.ppermute(low, 'tile', [(i + 1, i) for i in range(tiles - 1)])  7.94 us
    ppermute x1, starting transfers between devices, on_device(): lax.ppermute(high, 'tile', [(i, i + 1) for i in range(tiles - 1)])  3.55 us
    ppermute x1, starting transfers between devices, on_device(): sum_mine = mine + lax.ppermute(mine, 'field', CHIP_PAIRS)  2.39 us
    ppermute x1, starting transfers between devices, on_device(): second_far = lax.ppermute(second, 'field', CHIP_PAIRS)  1.57 us
    unnamed x2, local copies, waits for them, and re-layouts  1.41 us
    ppermute x1, starting transfers between devices, on_device(): mine = mine + lax.ppermute(other, 'field', CORE_PAIRS)  1.04 us
  transfers between devices with their start and end apart: 7, of which 2 were waited for; matrix products, arithmetic and copies ran while one was open for 0% of the time, Pallas kernels for 43%

profile of v7, /device:TPU:9, one launch (start us, length us, event | category | flops | bytes accessed | tf_op | source)
XLA Modules:
  0.0 51.5 jit_solution(6746276086701157964)
XLA Ops:
  0.6 2.9 %pack.1 = (f32[640,128]{1,0:T(8,128)}, f32[640,128]{1,0:T(8,128)}, f32[3112,128]{1,0:T(8,128)}) custom-call(f32[2048,128]{1,0:T(8,128)} %bitcast.13, f32[1,4,8,128]{3,2,1,0:T(8,128)} %density_far.1, f32[3,1,4,8,128]{4,3,2,1,0:T(8,128)} %velocity_far.1, f32[1,4,8,128]{3,2,1,0:T(8,128)} %energy_far.1, f32[768,128]{1,0:T(8,128)} %bitcast.14, ...), custom_call_target="tpu_custom_call" | custom-call | flops 2000000000 | bytes 3818368 | tf_op jit(solution)/shard_map/pack/pallas_call | solution.py:472
  3.5 3.5 %collective-permute-start = (f32[640,128]{1,0:T(8,128)}, f32[640,128]{1,0:T(8,128)S(1)}, u32[]{:S(2)}, u32[]{:S(2)}) collective-permute-start(f32[640,128]{1,0:T(8,128)} %get-tuple-element.37), channel_id=1, source_target_pairs={{0,1},{1,2},{2,3},{3,4},{4,5},{5,6},{6,7},{7,8},{8,9},{9,10},{10,1... | collective-permute-start | bytes 983048 | tf_op jit(solution)/shard_map/ppermute | solution.py:511
  7.1 7.9 %collective-permute-start.1 = (f32[640,128]{1,0:T(8,128)}, f32[640,128]{1,0:T(8,128)S(1)}, u32[]{:S(2)}, u32[]{:S(2)}) collective-permute-start(f32[640,128]{1,0:T(8,128)} %get-tuple-element.38), channel_id=1, source_target_pairs={{1,0},{2,1},{3,2},{4,3},{5,4},{6,5},{7,6},{8,7},{9,8},{10,9},{11,1... | collective-permute-start | bytes 983048 | tf_op jit(solution)/shard_map/ppermute | solution.py:512
  15.0 0.0 copy-start
  15.0 1.4 %copy-done = f32[3112,128]{1,0:T(8,128)S(1)} copy-done((f32[3112,128]{1,0:T(8,128)S(1)}, f32[3112,128]{1,0:T(8,128)}, u32[]{:S(2)}) %copy-start) | copy-done | bytes 1593368
  16.5 7.5 %inner.1 = (f32[8,4,4,16,128]{4,3,2,1,0:T(8,128)S(1)}, f32[8,4,8,128]{3,2,1,0:T(8,128)S(1)}, f32[8,4,16,128]{3,2,1,0:T(8,128)S(1)}, f32[8,4,16,128]{3,2,1,0:T(8,...) custom-call(f32[3112,128]{1,0:T(8,128)S(1)} %copy-done), custom_call_target="tpu_custom_call" | custom-call | flops 8000000000 | bytes 7688192 | tf_op jit(solution)/shard_map/inner/pallas_call | solution.py:472
  24.0 0.0 collective-permute-done.low_halo
  24.0 0.0 collective-permute-done.1.high_halo
  24.0 0.9 %first_edge.1 = (f32[4,4,4,16,128]{4,3,2,1,0:T(8,128)S(1)}, f32[10,4,8,128]{3,2,1,0:T(8,128)S(1)}, f32[2,10,16,128]{3,2,1,0:T(8,128)S(1)}, f32[2,10,16,128]{3,2,1,0:T(8,128)S(1)}) custom-call(f32[8,4,4,16,128]{4,3,2,1,0:T(8,128)S(1)} %get-tuple-element.32.own, f32[8,4,8,128]{3,2,1,0:T(8,128)S(1)} %get-tuple-element.33.flow, ...), custom_call_target="tpu_custom_call" | custom-call | flops 2000000000 | bytes 3407872 | tf_op jit(solution)/shard_map/first_edge/pallas_call | solution.py:472
  24.9 1.0 %collective-permute-start.2 = (f32[2,10,16,128]{3,2,1,0:T(8,128)S(1)}, f32[2,10,16,128]{3,2,1,0:T(8,128)S(1)}, u32[]{:S(2)}, u32[]{:S(2)}) collective-permute-start(f32[2,10,16,128]{3,2,1,0:T(8,128)S(1)} %get-tuple-element.40), channel_id=1, source_target_pairs={{0,64},{64,0},{128,192},{192,128},{1,65},{65,1},{129,193},{193,129... | collective-permute-start | bytes 491528 | tf_op jit(solution)/shard_map/ppermute | solution.py:529
  25.9 1.0 %collective-permute-done.2 = f32[2,10,16,128]{3,2,1,0:T(8,128)S(1)} collective-permute-done((f32[2,10,16,128]{3,2,1,0:T(8,128)S(1)}, f32[2,10,16,128]{3,2,1,0:T(8,128)S(1)}, u32[]{:S(2)}, u32[]{:S(2)}) %collective-permute-start.2) | collective-permute-done | bytes 163872 | tf_op jit(solution)/shard_map/ppermute | solution.py:529
  27.0 2.4 %collective-permute-start.5 = (f32[2,10,16,128]{3,2,1,0:T(8,128)S(1)}, f32[2,10,16,128]{3,2,1,0:T(8,128)S(1)}, u32[]{:S(2)}, u32[]{:S(2)}) collective-permute-start(f32[2,10,16,128]{3,2,1,0:T(8,128)S(1)} %add.9), channel_id=1, source_target_pairs={{0,128},{64,192},{128,0},{192,64},{1,129},{65,193},{129,1},{193,65... | collective-permute-start | bytes 491528 | tf_op jit(solution)/shard_map/ppermute | solution.py:531
  29.4 4.8 %react_edge.1 = (f32[4,256,512]{2,1,0:T(8,128)S(1)}, f32[8,4,4,16,128]{4,3,2,1,0:T(8,128)S(1)}, f32[4,152,128]{2,1,0:T(8,128)S(1)}) custom-call(f32[4,4,4,16,128]{4,3,2,1,0:T(8,128)S(1)} %get-tuple-element.42.carried, f32[10,4,8,128]{3,2,1,0:T(8,128)S(1)} %get-tuple-element.43.flow_one, f32[6,4,4,16,128]{4,3,2,1,0:T(8,128)S(1)} %get-tuple-element.44.inner_reacted, ...), custom_call_target="tpu_custom_call" | custom-call | flops 6000000000 | bytes 5652480 | tf_op jit(solution)/shard_map/react_edge/pallas_call | solution.py:472
  34.1 0.7 %collective-permute-start.3 = (f32[4,152,128]{2,1,0:T(8,128)S(1)}, f32[4,152,128]{2,1,0:T(8,128)S(1)}, u32[]{:S(2)}, u32[]{:S(2)}) collective-permute-start(f32[4,152,128]{2,1,0:T(8,128)S(1)} %get-tuple-element.49), channel_id=1, source_target_pairs={{0,64},{64,0},{128,192},{192,128},{1,65},{65,1},{129,193},{193,129... | collective-permute-start | bytes 933896 | tf_op jit(solution)/shard_map/ppermute | solution.py:539
  34.9 0.0 collective-permute-done.5
  34.9 0.4 collective-permute-start.6
  35.3 0.8 %collective-permute-done.3 = f32[4,152,128]{2,1,0:T(8,128)S(1)} collective-permute-done((f32[4,152,128]{2,1,0:T(8,128)S(1)}, f32[4,152,128]{2,1,0:T(8,128)S(1)}, u32[]{:S(2)}, u32[]{:S(2)}) %collective-permute-start.3) | collective-permute-done | bytes 311328 | tf_op jit(solution)/shard_map/ppermute | solution.py:539
  36.1 1.6 %collective-permute-start.4 = (f32[4,152,128]{2,1,0:T(8,128)S(1)}, f32[4,152,128]{2,1,0:T(8,128)S(1)}, u32[]{:S(2)}, u32[]{:S(2)}) collective-permute-start(f32[4,152,128]{2,1,0:T(8,128)S(1)} %add.10.sum_here), channel_id=1, source_target_pairs={{0,128},{64,192},{128,0},{192,64},{1,129},{65,193},{129,1},{193,65... | collective-permute-start | bytes 933896 | tf_op jit(solution)/shard_map/ppermute | solution.py:540
  37.7 0.0 collective-permute-done.6.sum_other
  37.7 10.0 %second_step.1 = (f32[8,256,512]{2,1,0:T(8,128)S(1)}, f32[8,4,4,16,128]{4,3,2,1,0:T(8,128)S(1)}, f32[10,4,16,128]{3,2,1,0:T(8,128)S(1)}, f32[8,4,8,128]{3,2,1,0:T(8,128)S(1)}) custom-call(f32[2,10,16,128]{3,2,1,0:T(8,128)S(1)} %add.11.sum_mine, f32[2,10,16,128]{3,2,1,0:T(8,128)S(1)} %collective-permute-done.6.sum_other, ...), custom_call_target="tpu_custom_call" | custom-call | flops 10000000000 | bytes 13156352 | tf_op jit(solution)/shard_map/second_step/pallas_call | solution.py:472
  47.7 0.0 collective-permute-done.4.sum_there
  47.7 3.8 %finish.1 = (f32[5,4,8,128]{3,2,1,0:T(8,128)}, f32[64,4,8,128]{3,2,1,0:T(8,128)}) custom-call(f32[4,152,128]{2,1,0:T(8,128)S(1)} %add.10.sum_here, f32[4,152,128]{2,1,0:T(8,128)S(1)} %collective-permute-done.4.sum_there, f32[10,4,16,128]{3,2,1,0:T(8,128)S(1)} %get-tuple-element.54.shared, f32[8,4,8,128]{3,2,1,0:T(8,128)S(1)} %get-tuple-element.55.flow_two, ...), custom_call_target="tpu_custom_call" | custom-call | flops 4000000000 | bytes 7569408 | tf_op jit(solution)/shard_map/finish/pallas_call | solution.py:472
  (3 shorter events, 0.1 us)
Async XLA Ops:
  3.5 20.4 %collective-permute-start = (f32[640,128]{1,0:T(8,128)}, f32[640,128]{1,0:T(8,128)S(1)}, u32[]{:S(2)}, u32[]{:S(2)}) collective-permute-start(f32[640,128]{1,0:T(8,128)} %get-tuple-element.37), channel_id=1, source_target_pairs={{0,1},{1,2},{2,3},{3,4},{4,5},{5,6},{6,7},{7,8},{8,9},{9,10},{10,1... | collective-permute-start | bytes 983048 | tf_op jit(solution)/shard_map/ppermute | solution.py:511
  7.1 16.9 %collective-permute-start.1 = (f32[640,128]{1,0:T(8,128)}, f32[640,128]{1,0:T(8,128)S(1)}, u32[]{:S(2)}, u32[]{:S(2)}) collective-permute-start(f32[640,128]{1,0:T(8,128)} %get-tuple-element.38), channel_id=1, source_target_pairs={{1,0},{2,1},{3,2},{4,3},{5,4},{6,5},{7,6},{8,7},{9,8},{10,9},{11,1... | collective-permute-start | bytes 983048 | tf_op jit(solution)/shard_map/ppermute | solution.py:512
  15.0 1.4 %copy-start = (f32[3112,128]{1,0:T(8,128)S(1)}, f32[3112,128]{1,0:T(8,128)}, u32[]{:S(2)}) copy-start(f32[3112,128]{1,0:T(8,128)} %get-tuple-element.31.bundle) | copy-start | bytes 4780036
  24.9 2.1 %collective-permute-start.2 = (f32[2,10,16,128]{3,2,1,0:T(8,128)S(1)}, f32[2,10,16,128]{3,2,1,0:T(8,128)S(1)}, u32[]{:S(2)}, u32[]{:S(2)}) collective-permute-start(f32[2,10,16,128]{3,2,1,0:T(8,128)S(1)} %get-tuple-element.40), channel_id=1, source_target_pairs={{0,64},{64,0},{128,192},{192,128},{1,65},{65,1},{129,193},{193,129... | collective-permute-start | bytes 491528 | tf_op jit(solution)/shard_map/ppermute | solution.py:529
  27.0 7.9 %collective-permute-start.5 = (f32[2,10,16,128]{3,2,1,0:T(8,128)S(1)}, f32[2,10,16,128]{3,2,1,0:T(8,128)S(1)}, u32[]{:S(2)}, u32[]{:S(2)}) collective-permute-start(f32[2,10,16,128]{3,2,1,0:T(8,128)S(1)} %add.9), channel_id=1, source_target_pairs={{0,128},{64,192},{128,0},{192,64},{1,129},{65,193},{129,1},{193,65... | collective-permute-start | bytes 491528 | tf_op jit(solution)/shard_map/ppermute | solution.py:531
  34.1 2.0 %collective-permute-start.3 = (f32[4,152,128]{2,1,0:T(8,128)S(1)}, f32[4,152,128]{2,1,0:T(8,128)S(1)}, u32[]{:S(2)}, u32[]{:S(2)}) collective-permute-start(f32[4,152,128]{2,1,0:T(8,128)S(1)} %get-tuple-element.49), channel_id=1, source_target_pairs={{0,64},{64,0},{128,192},{192,128},{1,65},{65,1},{129,193},{193,129... | collective-permute-start | bytes 933896 | tf_op jit(solution)/shard_map/ppermute | solution.py:539
  34.9 2.8 %collective-permute-start.6 = (f32[2,10,16,128]{3,2,1,0:T(8,128)S(1)}, f32[2,10,16,128]{3,2,1,0:T(8,128)S(1)}, u32[]{:S(2)}, u32[]{:S(2)}) collective-permute-start(f32[2,10,16,128]{3,2,1,0:T(8,128)S(1)} %add.11.sum_mine), channel_id=1, source_target_pairs={{0,64},{64,0},{128,192},{192,128},{1,65},{65,1},{129,193},{193,129... | collective-permute-start | bytes 491528 | tf_op jit(solution)/shard_map/ppermute | solution.py:532
  36.1 11.6 %collective-permute-start.4 = (f32[4,152,128]{2,1,0:T(8,128)S(1)}, f32[4,152,128]{2,1,0:T(8,128)S(1)}, u32[]{:S(2)}, u32[]{:S(2)}) collective-permute-start(f32[4,152,128]{2,1,0:T(8,128)S(1)} %add.10.sum_here), channel_id=1, source_target_pairs={{0,128},{64,192},{128,0},{192,64},{1,129},{65,193},{129,1},{193,65... | collective-permute-start | bytes 933896 | tf_op jit(solution)/shard_map/ppermute | solution.py:540
